TPU v7x, 32 devices: a whole 2x2x4 slice. The times are simulated.
32 devices in a mesh: row: 4 (over x, core), col: 8 (over z, y).
Axes of the slice: x: 2, y: 2, z: 4, core: 2. Of those that a mesh axis runs over, the one named last changes fastest.
Arguments:
- inputs: bfloat16 [8, 1024, 512], P('col', 'row'), may hold values from -6 to 6
- seg_start: int32 [8, 1024], P('col', 'row'), may hold values from 0 to 1023, as said below
- cotangent: bfloat16 [8, 1024, 512], P('col', 'row'), may hold values from -6 to 6
- project_weight: bfloat16 [512, 1536], P('row', 'col'), may hold values from -0.25 to 0.25
- project_bias: bfloat16 [1536], P(('row', 'col')), may hold values from -1.5 to 1.5
- output_weight: bfloat16 [512, 512], P('col', 'row'), may hold values from -0.75 to 0.75
- output_bias: bfloat16 [512], P(('row', 'col')), may hold values from -1.5 to 1.5
- up_weight: bfloat16 [512, 2048], P('row', 'col'), may hold values from -0.25 to 0.25
- up_bias: bfloat16 [2048], P(('row', 'col')), may hold values from -1.5 to 1.5
- down_weight: bfloat16 [2048, 512], P('col', 'row'), may hold values from -0.125 to 0.125
- down_bias: bfloat16 [512], P(('row', 'col')), may hold values from -1.5 to 1.5
- first_gain: bfloat16 [512], P(('row', 'col')), may hold values from 0.25 to 1.75
- first_bias: bfloat16 [512], P(('row', 'col')), may hold values from -1.5 to 1.5
- second_gain: bfloat16 [512], P(('row', 'col')), may hold values from 0.25 to 1.75
- second_bias: bfloat16 [512], P(('row', 'col')), may hold values from -1.5 to 1.5
Outputs:
- output: bfloat16 [8, 1024, 512], P('col', 'row')
- input_grad: float32 [8, 1024, 512], P('col', 'row')
- project_weight_grad: float32 [512, 1536], P('row', 'col')
- project_bias_grad: float32 [1536], P(('row', 'col'))
- output_weight_grad: float32 [512, 512], P('col', 'row')
- output_bias_grad: float32 [512], P(('row', 'col'))
- up_weight_grad: float32 [512, 2048], P('row', 'col')
- up_bias_grad: float32 [2048], P(('row', 'col'))
- down_weight_grad: float32 [2048, 512], P('col', 'row')
- down_bias_grad: float32 [512], P(('row', 'col'))
- first_gain_grad: float32 [512], P(('row', 'col'))
- first_bias_grad: float32 [512], P(('row', 'col'))
- second_gain_grad: float32 [512], P(('row', 'col'))
- second_bias_grad: float32 [512], P(('row', 'col'))
Inputs may be any that keep to these rules, and one draw needn't show every extreme that they name: `seg_start`: for each token, the place within its sequence of its document's first token; documents are runs of consecutive tokens, and in every sequence one document starts before place 1024 / 4 and reaches place 3 * 256 or later.
All inputs are finite; a program needn't handle non-finite values.
Results may differ from a plain program's by a relative error of at most 0.012.
Values may be sent and summed in bfloat16 or wider, within the bound.
No kernel may reach another device: no remote copies, remote signals or barrier semaphores. Data moves between devices by JAX's collectives and lax.ppermute only.
A program may use at most 128 MiB of HBM per device.

v0:
```python
import math

import jax
import jax.numpy as jnp
from jax import lax
from jax.sharding import PartitionSpec as P

HD = 64
ROT = 16


EPS = 1e-05
MASKED = -1e30


def layer_norm(rows_in, gain, shift):
    average = jnp.mean(rows_in, axis=-1, keepdims=True)
    centred = rows_in - average
    spread = jnp.mean(centred * centred, axis=-1, keepdims=True)
    return centred * lax.rsqrt(spread + EPS) * gain + shift


def rotate(tensor, positions):
    half_rot = ROT // 2
    exponent = jnp.arange(half_rot, dtype=jnp.float32) * (2.0 / ROT)
    frequency = jnp.exp(exponent * -math.log(10000.0))
    angles = positions[..., None].astype(jnp.float32) * frequency
    cosine = jnp.cos(angles)[..., None, :]
    sine_part = jnp.sin(angles)[..., None, :]
    leading = tensor[..., :half_rot]
    trailing = tensor[..., half_rot:ROT]
    return jnp.concatenate(
        [
            leading * cosine - trailing * sine_part,
            trailing * cosine + leading * sine_part,
            tensor[..., ROT:],
        ],
        axis=-1,
    )


def gather_params(
    project_weight,
    project_bias,
    output_weight,
    output_bias,
    up_weight,
    up_bias,
    down_weight,
    down_bias,
    first_gain,
    first_bias,
    second_gain,
    second_bias,
):
    parted = (
        lax.all_gather(project_weight, "row", axis=0, tiled=True),
        lax.all_gather(project_bias, "row", axis=0, tiled=True),
        lax.all_gather(output_weight, "row", axis=1, tiled=True),
        lax.all_gather(output_bias, "row", axis=0, tiled=True),
        lax.all_gather(up_weight, "row", axis=0, tiled=True),
        lax.all_gather(up_bias, "row", axis=0, tiled=True),
        lax.all_gather(down_weight, "row", axis=1, tiled=True),
        lax.all_gather(down_bias, "row", axis=0, tiled=True),
        lax.all_gather(first_gain, "row", axis=0, tiled=True),
        lax.all_gather(first_bias, "row", axis=0, tiled=True),
        lax.all_gather(second_gain, "row", axis=0, tiled=True),
        lax.all_gather(second_bias, "row", axis=0, tiled=True),
    )
    return (
        lax.all_gather(parted[0], "col", axis=1, tiled=True),
        lax.all_gather(parted[1], "col", axis=1, tiled=True),
        lax.all_gather(parted[2], "col", axis=0, tiled=True),
        lax.all_gather(parted[3], "col", axis=1, tiled=True),
        lax.all_gather(parted[4], "col", axis=1, tiled=True),
        lax.all_gather(parted[5], "col", axis=1, tiled=True),
        lax.all_gather(parted[6], "col", axis=0, tiled=True),
        lax.all_gather(parted[7], "col", axis=1, tiled=True),
        lax.all_gather(parted[8], "col", axis=1, tiled=True),
        lax.all_gather(parted[9], "col", axis=1, tiled=True),
        lax.all_gather(parted[10], "col", axis=1, tiled=True),
        lax.all_gather(parted[11], "col", axis=1, tiled=True),
    )


def scatter_grads(
    project_grad,
    project_shift,
    output_grad,
    output_shift,
    up_grad,
    up_shift,
    down_grad,
    gain_one,
    shift_one,
    gain_two,
    shift_two,
):
    parted = (
        lax.psum_scatter(project_grad, "col", scatter_dimension=1, tiled=True),
        lax.psum_scatter(project_shift, "col", scatter_dimension=1, tiled=True),
        lax.psum_scatter(output_grad, "col", scatter_dimension=0, tiled=True),
        lax.psum_scatter(output_shift, "col", scatter_dimension=1, tiled=True),
        lax.psum_scatter(up_grad, "col", scatter_dimension=1, tiled=True),
        lax.psum_scatter(up_shift, "col", scatter_dimension=1, tiled=True),
        lax.psum_scatter(down_grad, "col", scatter_dimension=0, tiled=True),
        lax.psum_scatter(gain_one, "col", scatter_dimension=1, tiled=True),
        lax.psum_scatter(shift_one, "col", scatter_dimension=1, tiled=True),
        lax.psum_scatter(gain_two, "col", scatter_dimension=1, tiled=True),
        lax.psum_scatter(shift_two, "col", scatter_dimension=1, tiled=True),
    )
    return (
        lax.psum_scatter(
            parted[0].astype(jnp.bfloat16), "row", scatter_dimension=0, tiled=True
        ).astype(jnp.float32),
        lax.psum_scatter(
            parted[1].astype(jnp.bfloat16), "row", scatter_dimension=0, tiled=True
        ).astype(jnp.float32),
        lax.psum_scatter(
            parted[2].astype(jnp.bfloat16), "row", scatter_dimension=1, tiled=True
        ).astype(jnp.float32),
        lax.psum_scatter(
            parted[3].astype(jnp.bfloat16), "row", scatter_dimension=0, tiled=True
        ).astype(jnp.float32),
        lax.psum_scatter(
            parted[4].astype(jnp.bfloat16), "row", scatter_dimension=0, tiled=True
        ).astype(jnp.float32),
        lax.psum_scatter(
            parted[5].astype(jnp.bfloat16), "row", scatter_dimension=0, tiled=True
        ).astype(jnp.float32),
        lax.psum_scatter(
            parted[6].astype(jnp.bfloat16), "row", scatter_dimension=1, tiled=True
        ).astype(jnp.float32),
        lax.psum_scatter(
            parted[7].astype(jnp.bfloat16), "row", scatter_dimension=0, tiled=True
        ).astype(jnp.float32),
        lax.psum_scatter(
            parted[8].astype(jnp.bfloat16), "row", scatter_dimension=0, tiled=True
        ).astype(jnp.float32),
        lax.psum_scatter(
            parted[9].astype(jnp.bfloat16), "row", scatter_dimension=0, tiled=True
        ).astype(jnp.float32),
        lax.psum_scatter(
            parted[10].astype(jnp.bfloat16), "row", scatter_dimension=0, tiled=True
        ).astype(jnp.float32),
    )


def on_device(
    inputs,
    seg_start,
    cotangent,
    project_weight,
    project_bias,
    output_weight,
    output_bias,
    up_weight,
    up_bias,
    down_weight,
    down_bias,
    first_gain,
    first_bias,
    second_gain,
    second_bias,
):
    row_count = lax.axis_size("row")
    full = gather_params(
        project_weight,
        project_bias[None, :],
        output_weight,
        output_bias[None, :],
        up_weight,
        up_bias[None, :],
        down_weight,
        down_bias[None, :],
        first_gain[None, :],
        first_bias[None, :],
        second_gain[None, :],
        second_bias[None, :],
    )
    project_full = full[0]
    project_shift = full[1].reshape(-1).astype(jnp.float32)
    output_full = full[2]
    output_shift = full[3].reshape(-1).astype(jnp.float32)
    up_full = full[4]
    up_shift = full[5].reshape(-1).astype(jnp.float32)
    down_full = full[6]
    down_shift = full[7].reshape(-1).astype(jnp.float32)
    gain_one = full[8].reshape(-1).astype(jnp.float32)
    shift_one = full[9].reshape(-1).astype(jnp.float32)
    gain_two = full[10].reshape(-1).astype(jnp.float32)
    shift_two = full[11].reshape(-1).astype(jnp.float32)
    count_here = inputs.shape[1]
    model_width = inputs.shape[2]
    head_count = model_width // HD
    scaling = HD ** (-0.5)
    flattened = inputs.reshape(-1, model_width).astype(jnp.float32)
    own_starts = seg_start.reshape(-1)
    all_starts = lax.all_gather(seg_start, "row", axis=1, tiled=True).reshape(-1)
    row_index = lax.axis_index("row")
    own_index = row_index * count_here + jnp.arange(count_here, dtype=jnp.int32)
    key_index = jnp.arange(all_starts.shape[0], dtype=jnp.int32)
    positions = own_index - own_starts
    allowed = (own_starts[:, None] == all_starts[None, :]) & (
        own_index[:, None] >= key_index[None, :]
    )
    normed_one = layer_norm(flattened, gain_one, shift_one).astype(jnp.bfloat16)
    projected = (
        jnp.dot(normed_one, project_full, preferred_element_type=jnp.float32) + project_shift
    )
    projected = projected.reshape(count_here, head_count, 3 * HD)
    queries = rotate(projected[..., :HD], positions).astype(jnp.bfloat16)
    key_rows = rotate(projected[..., HD : 2 * HD], positions).astype(jnp.bfloat16)
    values = projected[..., 2 * HD :].astype(jnp.bfloat16)
    all_keys, all_values = (
        lax.all_gather(key_rows, "row", axis=0, tiled=True),
        lax.all_gather(values, "row", axis=0, tiled=True),
    )
    scores = (
        jnp.einsum("qhe,khe->hqk", queries, all_keys, preferred_element_type=jnp.float32) * scaling
    )
    scores = jnp.where(allowed[None], scores, MASKED)
    maximum = jnp.max(scores, axis=-1, keepdims=True)
    exponent = jnp.exp(scores - maximum)
    probability = exponent / jnp.sum(exponent, axis=-1, keepdims=True)
    prob_low = probability.astype(jnp.bfloat16)
    context = jnp.einsum("hqk,khe->qhe", prob_low, all_values, preferred_element_type=jnp.float32)
    context = context.reshape(count_here, model_width).astype(jnp.bfloat16)
    attn_out = jnp.dot(context, output_full, preferred_element_type=jnp.float32) + output_shift
    normed_two = layer_norm(flattened, gain_two, shift_two).astype(jnp.bfloat16)
    hidden = jnp.dot(normed_two, up_full, preferred_element_type=jnp.float32) + up_shift
    active = jax.nn.gelu(hidden, approximate=False).astype(jnp.bfloat16)
    mlp_out = jnp.dot(active, down_full, preferred_element_type=jnp.float32) + down_shift
    output = (flattened + attn_out + mlp_out).astype(jnp.bfloat16).reshape(inputs.shape)
    cot_low = cotangent.reshape(-1, model_width)
    grad_out = cot_low.astype(jnp.float32)
    d_active = jnp.einsum("td,fd->tf", cot_low, down_full, preferred_element_type=jnp.float32)
    unused, gelu_back = jax.vjp(lambda pre_act: jax.nn.gelu(pre_act, approximate=False), hidden)
    d_hidden = gelu_back(d_active)[0].astype(jnp.bfloat16)
    down_grad = jnp.einsum("tf,td->fd", active, cot_low, preferred_element_type=jnp.float32)
    shift_grad = jnp.sum(grad_out, axis=0)
    up_grad = jnp.einsum("td,tf->df", normed_two, d_hidden, preferred_element_type=jnp.float32)
    up_shift_grad = jnp.sum(d_hidden.astype(jnp.float32), axis=0)
    d_second = jnp.einsum("tf,df->td", d_hidden, up_full, preferred_element_type=jnp.float32)
    output_grad = jnp.einsum("te,td->ed", context, cot_low, preferred_element_type=jnp.float32)
    d_context = jnp.einsum("td,ed->te", cot_low, output_full, preferred_element_type=jnp.float32)
    d_context = d_context.astype(jnp.bfloat16).reshape(count_here, head_count, HD)
    d_prob = jnp.einsum("qhe,khe->hqk", d_context, all_values, preferred_element_type=jnp.float32)
    d_scores = probability * (d_prob - jnp.sum(d_prob * probability, axis=-1, keepdims=True))
    d_scores = d_scores.astype(jnp.bfloat16)
    d_queries = (
        jnp.einsum("hqk,khe->qhe", d_scores, all_keys, preferred_element_type=jnp.float32) * scaling
    )
    key_part = (
        jnp.einsum("hqk,qhe->khe", d_scores, queries, preferred_element_type=jnp.float32) * scaling
    )
    value_part = jnp.einsum("hqk,qhe->khe", prob_low, d_context, preferred_element_type=jnp.float32)
    d_keys, d_values = (
        lax.psum_scatter(
            key_part.astype(jnp.bfloat16), "row", scatter_dimension=0, tiled=True
        ).astype(jnp.float32),
        lax.psum_scatter(
            value_part.astype(jnp.bfloat16), "row", scatter_dimension=0, tiled=True
        ).astype(jnp.float32),
    )
    d_projected = jnp.concatenate(
        [rotate(d_queries, -positions), rotate(d_keys, -positions), d_values], axis=-1
    )
    d_projected = d_projected.reshape(count_here, 3 * model_width).astype(jnp.bfloat16)
    project_grad = jnp.einsum(
        "td,tf->df", normed_one, d_projected, preferred_element_type=jnp.float32
    )
    project_shift_grad = jnp.sum(d_projected.astype(jnp.float32), axis=0)
    d_first = jnp.einsum("tf,df->td", d_projected, project_full, preferred_element_type=jnp.float32)
    unused, norm_back_one = jax.vjp(layer_norm, flattened, gain_one, shift_one)
    input_one, gain_one_grad, shift_one_grad = norm_back_one(d_first)
    unused, norm_back_two = jax.vjp(layer_norm, flattened, gain_two, shift_two)
    input_two, gain_two_grad, shift_two_grad = norm_back_two(d_second)
    input_grad = (grad_out + input_one + input_two).reshape(inputs.shape)
    pieces = scatter_grads(
        project_grad,
        project_shift_grad.reshape(row_count, -1),
        output_grad,
        shift_grad.reshape(row_count, -1),
        up_grad,
        up_shift_grad.reshape(row_count, -1),
        down_grad,
        gain_one_grad.reshape(row_count, -1),
        shift_one_grad.reshape(row_count, -1),
        gain_two_grad.reshape(row_count, -1),
        shift_two_grad.reshape(row_count, -1),
    )
    bias_piece = pieces[3].reshape(-1)
    return (
        output,
        input_grad,
        pieces[0],
        pieces[1].reshape(-1),
        pieces[2],
        bias_piece,
        pieces[4],
        pieces[5].reshape(-1),
        pieces[6],
        bias_piece,
        pieces[7].reshape(-1),
        pieces[8].reshape(-1),
        pieces[9].reshape(-1),
        pieces[10].reshape(-1),
    )


def solution(mesh):
    return jax.shard_map(
        on_device,
        mesh=mesh,
        in_specs=(
            P("col", "row", None),
            P("col", "row"),
            P("col", "row", None),
            P("row", "col"),
            P(("row", "col")),
            P("col", "row"),
            P(("row", "col")),
            P("row", "col"),
            P(("row", "col")),
            P("col", "row"),
            P(("row", "col")),
            P(("row", "col")),
            P(("row", "col")),
            P(("row", "col")),
            P(("row", "col")),
        ),
        out_specs=(
            P("col", "row", None),
            P("col", "row", None),
            P("row", "col"),
            P(("row", "col")),
            P("col", "row"),
            P(("row", "col")),
            P("row", "col"),
            P(("row", "col")),
            P("col", "row"),
            P(("row", "col")),
            P(("row", "col")),
            P(("row", "col")),
            P(("row", "col")),
            P(("row", "col")),
        ),
        check_vma=False,
    )
```

profile of v0, /device:TPU:0, one launch (start us, length us, event | category | flops | bytes accessed | tf_op | source)
XLA Modules:
  0.0 1158.8 jit_solution(14924906517098602735)
XLA Ops:
  7.2 8.6 all_gather.87
  24.3 6.6 all-reduce.16
  31.0 20.8 %all-gather.10 = bf16[8,48,4]{1,2,0:T(4,128)(2,1)S(1)} all-gather(bf16[1,48,4]{1,2,0:T(4,128)(2,1)S(1)} %bitcast.307), channel_id=1, replica_groups=mesh['row'=4,'col'=8] {'col'}, dimensions={0}, use_global_device_ids=true | all-gather | bytes 3456 | tf_op jit(solution)/shard_map/all_gather | solution.py:72
  52.0 16.3 %all-gather.9 = bf16[8,16,4]{1,2,0:T(4,128)(2,1)S(1)} all-gather(bf16[1,16,4]{1,2,0:T(4,128)(2,1)S(1)} %bitcast.308), channel_id=1, replica_groups=mesh['row'=4,'col'=8] {'col'}, dimensions={0}, use_global_device_ids=true | all-gather | bytes 1152 | tf_op jit(solution)/shard_map/all_gather | solution.py:80
  68.5 18.2 %all-gather.8 = bf16[8,16,4]{1,2,0:T(4,128)(2,1)S(1)} all-gather(bf16[1,16,4]{1,2,0:T(4,128)(2,1)S(1)} %bitcast.309), channel_id=1, replica_groups=mesh['row'=4,'col'=8] {'col'}, dimensions={0}, use_global_device_ids=true | all-gather | bytes 1152 | tf_op jit(solution)/shard_map/all_gather | solution.py:79
  94.4 6.2 all_gather.103
  100.7 8.0 all_gather.107
  114.1 31.7 %all_gather.96 = bf16[512,512]{1,0:T(8,128)(2,1)S(1)} all-gather(bf16[64,512]{1,0:T(8,128)(2,1)S(1)} %all_gather.95), channel_id=1, replica_groups=mesh['row'=4,'col'=8] {'col'}, dimensions={0}, use_global_device_ids=true | all-gather | bytes 589824 | tf_op jit(solution)/shard_map/all_gather | solution.py:73
  151.8 7.5 fusion.107
  171.2 16.6 %all-gather.13 = bf16[8,16,4]{1,2,0:T(4,128)(2,1)S(1)} all-gather(bf16[1,16,4]{1,2,0:T(4,128)(2,1)S(1)} %bitcast.303), channel_id=1, replica_groups=mesh['row'=4,'col'=8] {'col'}, dimensions={0}, use_global_device_ids=true | all-gather | bytes 1152 | tf_op jit(solution)/shard_map/all_gather | solution.py:82
  187.8 18.1 %all-gather.12 = bf16[8,16,4]{1,2,0:T(4,128)(2,1)S(1)} all-gather(bf16[1,16,4]{1,2,0:T(4,128)(2,1)S(1)} %bitcast.304), channel_id=1, replica_groups=mesh['row'=4,'col'=8] {'col'}, dimensions={0}, use_global_device_ids=true | all-gather | bytes 1152 | tf_op jit(solution)/shard_map/all_gather | solution.py:81
  205.9 16.7 %all-gather.14 = bf16[8,64,4]{1,2,0:T(4,128)(2,1)S(1)} all-gather(bf16[1,64,4]{1,2,0:T(4,128)(2,1)S(1)} %bitcast.302), channel_id=1, replica_groups=mesh['row'=4,'col'=8] {'col'}, dimensions={0}, use_global_device_ids=true | all-gather | bytes 4608 | tf_op jit(solution)/shard_map/all_gather | solution.py:76
  228.8 8.2 multiply_convert_fusion.2
  261.6 23.2 %reduce-scatter.40.cloned.1.call-done = bf16[256,8,64]{0,2,1:T(8,128)(2,1)} async-done(((bf16[1024,8,64]{0,2,1:T(8,128)(2,1)}), bf16[256,8,64]{0,2,1:T(8,128)(2,1)}) %reduce-scatter.40.cloned.1.call-update) | async-done | bytes 262160 | tf_op jit(solution)/shard_map/reduce_scatter | solution.py:262
  305.5 43.9 %reduce-scatter.60.cloned.1.call-done = f32[64,4]{1,0:T(8,128)} async-done(((f32[512,4]{1,0:T(8,128)}), f32[64,4]{1,0:T(8,128)}) %reduce-scatter.60.cloned.1.call-update) | async-done | bytes 1040
  350.2 64.9 %reduce-scatter.44.cloned.1.call-done = f32[64,512]{1,0:T(8,128)} async-done(((f32[512,512]{1,0:T(8,128)}), f32[64,512]{1,0:T(8,128)}) %reduce-scatter.44.cloned.1.call-update) | async-done | bytes 131088 | tf_op jit(solution)/shard_map/reduce_scatter | solution.py:102
  416.9 62.7 %reduce-scatter.58.cloned.1.call-done = f32[16,4]{1,0:T(8,128)} async-done(((f32[128,4]{1,0:T(8,128)}), f32[16,4]{1,0:T(8,128)}) %reduce-scatter.58.cloned.1.call-update) | async-done | bytes 272
  480.4 63.8 %reduce-scatter.64.cloned.1.call-done = f32[16,4]{1,0:T(8,128)} async-done(((f32[128,4]{1,0:T(8,128)}), f32[16,4]{1,0:T(8,128)}) %reduce-scatter.64.cloned.1.call-update) | async-done | bytes 272
  545.0 63.1 %reduce-scatter.66.cloned.1.call-done = f32[16,4]{1,0:T(8,128)} async-done(((f32[128,4]{1,0:T(8,128)}), f32[16,4]{1,0:T(8,128)}) %reduce-scatter.66.cloned.1.call-update) | async-done | bytes 272
  608.9 63.2 %reduce-scatter.68.cloned.1.call-done = f32[16,4]{1,0:T(8,128)} async-done(((f32[128,4]{1,0:T(8,128)}), f32[16,4]{1,0:T(8,128)}) %reduce-scatter.68.cloned.1.call-update) | async-done | bytes 272
  673.0 63.1 %reduce-scatter.70.cloned.1.call-done = f32[16,4]{1,0:T(8,128)} async-done(((f32[128,4]{1,0:T(8,128)}), f32[16,4]{1,0:T(8,128)}) %reduce-scatter.70.cloned.1.call-update) | async-done | bytes 272
  736.9 62.9 %reduce-scatter.54.cloned.1.call-done = f32[48,4]{1,0:T(8,128)} async-done(((f32[384,4]{1,0:T(8,128)}), f32[48,4]{1,0:T(8,128)}) %reduce-scatter.54.cloned.1.call-update) | async-done | bytes 784
  800.6 5.7 all-reduce.15
  807.7 19.1 %all-gather.11 = bf16[8,16,4]{1,2,0:T(4,128)(2,1)S(1)} all-gather(bf16[1,16,4]{1,2,0:T(4,128)(2,1)S(1)} %bitcast.305), channel_id=1, replica_groups=mesh['row'=4,'col'=8] {'col'}, dimensions={0}, use_global_device_ids=true | all-gather | bytes 1152 | tf_op jit(solution)/shard_map/all_gather | solution.py:74
  826.8 16.7 %all-gather.15 = bf16[8,16,4]{1,2,0:T(4,128)(2,1)S(1)} all-gather(bf16[1,16,4]{1,2,0:T(4,128)(2,1)S(1)} %bitcast.306), channel_id=1, replica_groups=mesh['row'=4,'col'=8] {'col'}, dimensions={0}, use_global_device_ids=true | all-gather | bytes 1152 | tf_op jit(solution)/shard_map/all_gather | solution.py:78
  844.2 46.7 %reduce-scatter.50.cloned.1.call-done = f32[256,512]{1,0:T(8,128)} async-done(((f32[2048,512]{1,0:T(8,128)}), f32[256,512]{1,0:T(8,128)}) %reduce-scatter.50.cloned.1.call-update) | async-done | bytes 524304 | tf_op jit(solution)/shard_map/reduce_scatter | solution.py:106
  894.0 88.4 %reduce-scatter.46.cloned.1.call-done = f32[512,256]{1,0:T(8,128)} async-done(((f32[512,2048]{1,0:T(8,128)}), f32[512,256]{1,0:T(8,128)}) %reduce-scatter.46.cloned.1.call-update) | async-done | bytes 524304 | tf_op jit(solution)/shard_map/reduce_scatter | solution.py:104
  988.2 72.1 %reduce-scatter.42.cloned.1.call-done = f32[512,192]{0,1:T(8,128)} async-done(((f32[512,1536]{0,1:T(8,128)}), f32[512,192]{0,1:T(8,128)}) %reduce-scatter.42.cloned.1.call-update) | async-done | bytes 393232 | tf_op jit(solution)/shard_map/reduce_scatter | solution.py:100
  1066.4 15.8 %reduce-scatter.56.cloned.1.call-done = bf16[128,64]{1,0:T(8,128)(2,1)} async-done(((bf16[512,64]{1,0:T(8,128)(2,1)}), bf16[128,64]{1,0:T(8,128)(2,1)}) %reduce-scatter.56.cloned.1.call-update) | async-done | bytes 16400
  1083.7 20.9 %reduce-scatter.62.cloned.1.call-done = bf16[128,256]{1,0:T(8,128)(2,1)} async-done(((bf16[512,256]{1,0:T(8,128)(2,1)}), bf16[128,256]{1,0:T(8,128)(2,1)}) %reduce-scatter.62.cloned.1.call-update) | async-done | bytes 65552
  1106.2 21.1 %reduce-scatter.48.cloned.1.call-done = bf16[128,256]{1,0:T(8,128)(2,1)} async-done(((bf16[512,256]{1,0:T(8,128)(2,1)}), bf16[128,256]{1,0:T(8,128)(2,1)}) %reduce-scatter.48.cloned.1.call-update) | async-done | bytes 65552 | tf_op jit(solution)/shard_map/reduce_scatter | solution.py:125
  1128.8 21.0 %reduce-scatter.52.cloned.1.call-done = bf16[128,192]{1,0:T(8,128)(2,1)} async-done(((bf16[512,192]{1,0:T(8,128)(2,1)}), bf16[128,192]{1,0:T(8,128)(2,1)}) %reduce-scatter.52.cloned.1.call-update) | async-done | bytes 49168
  (211 shorter events, 119.7 us)
Async XLA Ops:
  7.2 82.8 %all-gather.22.cloned.1.call-start = ((), (), s32[]{:S(2)}) async-start(), calls=%async_computation.17 | async-start | bytes 1769472 | tf_op jit(solution)/shard_map/all_gather | solution.py:71
  15.9 135.9 %all-gather.26.cloned.1.call-start = ((), (), s32[]{:S(2)}) async-start(), calls=%async_computation.19 | async-start | bytes 1310720 | tf_op jit(solution)/shard_map/all_gather | solution.py:216
  92.7 8.0 copy-start.6
  92.7 16.1 %copy-start.7 = (bf16[64,128]{1,0:T(8,128)(2,1)S(1)}, bf16[64,128]{1,0:T(8,128)(2,1)}, u32[]{:S(2)}) copy-start(bf16[64,128]{1,0:T(8,128)(2,1)} %param.20) | copy-start | bytes 49156
  92.7 53.1 %copy-start.2 = (bf16[1,256,512]{2,1,0:T(8,128)(2,1)S(1)}, bf16[1,256,512]{2,1,0:T(8,128)(2,1)}, u32[]{:S(2)}) copy-start(bf16[1,256,512]{2,1,0:T(8,128)(2,1)} %param.17) | copy-start | bytes 786436
  93.5 52.8 %copy-start.8 = (s32[1,256]{1,0:T(1,128)S(1)}, s32[1,256]{1,0:T(1,128)}, u32[]{:S(2)}) copy-start(s32[1,256]{1,0:T(1,128)} %param.16) | copy-start | bytes 3076
  93.5 65.7 %all-gather.24.cloned.1.call-start = ((), (), s32[]{:S(2)}) async-start(), calls=%async_computation.18 | async-start | bytes 1310720 | tf_op jit(solution)/shard_map/all_gather | solution.py:217
  94.3 134.4 %all-gather.28.cloned.1.call-start = ((), (), s32[]{:S(2)}) async-start(), calls=%async_computation.20 | async-start | bytes 2359296 | tf_op jit(solution)/shard_map/all_gather | solution.py:75
  100.7 136.3 %all-gather.30.cloned.1.call-start = ((), (), s32[]{:S(2)}) async-start(), calls=%async_computation.21 | async-start | bytes 2359296 | tf_op jit(solution)/shard_map/all_gather | solution.py:77
  108.7 151.8 %reduce-scatter.38.cloned.1.call-start = ((), (), s32[]{:S(2)}) async-start(), calls=%async_computation.22 | async-start | bytes 1310720 | tf_op jit(solution)/shard_map/reduce_scatter | solution.py:259
  159.3 5.1 slice-start
  159.3 6.3 slice-start.1
  170.9 113.9 %reduce-scatter.40.cloned.1.call-start = ((), (), s32[]{:S(2)}) async-start(), calls=%async_computation.23 | async-start | bytes 1310720 | tf_op jit(solution)/shard_map/reduce_scatter | solution.py:262
  222.7 6.1 copy-start.1
  228.3 121.1 %reduce-scatter.60.cloned.1.call-start = ((), (), s32[]{:S(2)}) async-start(), calls=%async_computation.33 | async-start | bytes 294912
  243.2 172.0 %reduce-scatter.44.cloned.1.call-start = ((), (), s32[]{:S(2)}) async-start(), calls=%async_computation.25 | async-start | bytes 1179648 | tf_op jit(solution)/shard_map/reduce_scatter | solution.py:102
  245.9 6.6 copy-start.9
  260.5 219.1 %reduce-scatter.58.cloned.1.call-start = ((), (), s32[]{:S(2)}) async-start(), calls=%async_computation.32 | async-start | bytes 73728
  290.4 253.8 %reduce-scatter.64.cloned.1.call-start = ((), (), s32[]{:S(2)}) async-start(), calls=%async_computation.35 | async-start | bytes 73728
  291.2 316.9 %reduce-scatter.66.cloned.1.call-start = ((), (), s32[]{:S(2)}) async-start(), calls=%async_computation.36 | async-start | bytes 73728
  292.0 380.1 %reduce-scatter.68.cloned.1.call-start = ((), (), s32[]{:S(2)}) async-start(), calls=%async_computation.37 | async-start | bytes 73728
  292.8 443.3 %reduce-scatter.70.cloned.1.call-start = ((), (), s32[]{:S(2)}) async-start(), calls=%async_computation.38 | async-start | bytes 73728
  293.6 506.1 %reduce-scatter.54.cloned.1.call-start = ((), (), s32[]{:S(2)}) async-start(), calls=%async_computation.30 | async-start | bytes 221184
  295.0 595.9 %reduce-scatter.50.cloned.1.call-start = ((), (), s32[]{:S(2)}) async-start(), calls=%async_computation.28 | async-start | bytes 4718592 | tf_op jit(solution)/shard_map/reduce_scatter | solution.py:106
  297.8 684.6 %reduce-scatter.46.cloned.1.call-start = ((), (), s32[]{:S(2)}) async-start(), calls=%async_computation.26 | async-start | bytes 4718592 | tf_op jit(solution)/shard_map/reduce_scatter | solution.py:104
  301.9 758.5 %reduce-scatter.42.cloned.1.call-start = ((), (), s32[]{:S(2)}) async-start(), calls=%async_computation.24 | async-start | bytes 3538944 | tf_op jit(solution)/shard_map/reduce_scatter | solution.py:100
  304.4 683.5 %copy-start.4 = (bf16[8,64,256]{2,1,0:T(8,128)(2,1)S(1)}, bf16[8,64,256]{2,1,0:T(8,128)(2,1)}, u32[]{:S(2)}) copy-start(bf16[8,64,256]{2,1,0:T(8,128)(2,1)} %copy-done.3) | copy-start | bytes 786436
  304.4 777.8 %reduce-scatter.56.cloned.1.call-start = ((), (), s32[]{:S(2)}) async-start(), calls=%async_computation.31 | async-start | bytes 163840
  416.8 687.8 %reduce-scatter.62.cloned.1.call-start = ((), (), s32[]{:S(2)}) async-start(), calls=%async_computation.34 | async-start | bytes 327680
  844.1 307.3 %copy-start.12 = (f32[16]{0:T(128)}, f32[16]{0:T(128)S(1)}, u32[]{:S(2)}) copy-start(f32[16]{0:T(128)S(1)} %fusion.84) | copy-start | bytes 196
  892.8 234.5 %reduce-scatter.48.cloned.1.call-start = ((), (), s32[]{:S(2)}) async-start(), calls=%async_computation.27 | async-start | bytes 327680 | tf_op jit(solution)/shard_map/reduce_scatter | solution.py:125
  984.2 165.6 %reduce-scatter.52.cloned.1.call-start = ((), (), s32[]{:S(2)}) async-start(), calls=%async_computation.29 | async-start | bytes 327680
  (5 other events, 6.0 us)
Sparse Core Ops, SparseCore 0:
  16.0 44.4 all-gather.21
  93.7 15.5 all-gather.25
  111.3 16.8 all-gather.23
  130.1 51.5 all-gather.27
  183.6 47.7 all-gather.29
  233.8 23.3 reduce-scatter.37
  259.9 24.8 reduce-scatter.39
  288.1 61.1 reduce-scatter.59
  352.8 62.3 reduce-scatter.43
  419.3 60.2 reduce-scatter.57
  484.0 60.2 reduce-scatter.63
  547.9 60.2 reduce-scatter.65
  611.9 60.2 reduce-scatter.67
  675.8 60.2 reduce-scatter.69
  739.6 60.1 reduce-scatter.53
  803.7 87.1 reduce-scatter.49
  894.3 88.0 reduce-scatter.45
  986.2 74.0 reduce-scatter.41
  1063.5 18.6 reduce-scatter.55
  1084.5 20.0 reduce-scatter.61
  1107.2 20.0 reduce-scatter.47
  1129.7 20.0 reduce-scatter.51
where the time goes:
time: 1160 us
  waiting for transfers between devices  797 us (69%)
  blocking collectives  220 us (19%)
  matrix products  64.2 us (6%)
  local copies, waits for them, and re-layouts  31.7 us (3%)
  other arithmetic  27.4 us (2%)
  between operations  16.8 us (1%)
    unnamed x32, waiting for transfers between devices  481 us
    reduce_scatter x1, waiting for transfers between devices, scatter_grads(): lax.psum_scatter(up_grad, 'col', scatter_dimension=1, tiled=True)  88.4 us
    reduce_scatter x1, waiting for transfers between devices, scatter_grads(): lax.psum_scatter(project_grad, 'col', scatter_dimension=1, tiled=True)  72.1 us
    reduce_scatter x1, waiting for transfers between devices, scatter_grads(): lax.psum_scatter(output_grad, 'col', scatter_dimension=0, tiled=True)  64.9 us
    reduce_scatter x1, waiting for transfers between devices, scatter_grads(): lax.psum_scatter(down_grad, 'col', scatter_dimension=0, tiled=True)  46.7 us
    all_gather x1, blocking collectives, gather_params(): lax.all_gather(parted[2], 'col', axis=0, tiled=True)  31.7 us
    unnamed x71, local copies, waits for them, and re-layouts  28.9 us
  transfers between devices with their start and end apart: 22, of which 16 were waited for; matrix products, arithmetic and copies ran while one was open for 10% of the time, Pallas kernels for 0%

commit v1 on v0

v1 whole, which is shorter than its diff:
```python
import math

import jax
import jax.numpy as jnp
import numpy as np
from jax import lax
from jax.sharding import PartitionSpec as P

HD = 64
ROT = 16
EPS = 1e-05
MASKED = -1e30
BF = jnp.bfloat16
F32 = jnp.float32


def normalize(rows_in):
    average = jnp.mean(rows_in, axis=-1, keepdims=True)
    centred = rows_in - average
    spread = jnp.mean(centred * centred, axis=-1, keepdims=True)
    root = lax.rsqrt(spread + EPS)
    return centred * root, root


def dot(a, b, dims=((1,), (0,))):
    return lax.dot_general(a, b, (dims, ((), ())), preferred_element_type=F32)


def pack_project(b):
    half = b.shape[0] // 2
    return jnp.concatenate(
        [b[:, :128], jnp.concatenate([b[:half, 128:], b[half:, 128:]], axis=1)], axis=0
    )


def unpack_project(p):
    rest = p[128:192]
    return jnp.concatenate(
        [p[:128], jnp.concatenate([rest[:, :64], rest[:, 64:]], axis=0)], axis=1
    )


def pack_up(b):
    return jnp.concatenate([b[:, :128], b[:, 128:]], axis=0)


def unpack_up(p):
    return jnp.concatenate([p[:128], p[128:256]], axis=1)


def xor_order(stacked, key):
    return [
        lax.dynamic_index_in_dim(stacked, g ^ key, keepdims=False) for g in range(stacked.shape[0])
    ]


def rotary_tables(positions):
    lane = np.arange(2 * HD) % HD
    frequency = np.where(lane < ROT, 10000.0 ** (-(lane % (ROT // 2)) * 2.0 / ROT), 0.0)
    angles = positions[:, None].astype(F32) * jnp.asarray(frequency, F32)[None, :]
    return jnp.cos(angles), jnp.sin(angles)


def rotate(tensor, cosine, sine):
    half = ROT // 2
    swapped = jnp.concatenate(
        [-tensor[:, half:ROT], tensor[:, :half], tensor[:, ROT:]], axis=1
    )
    return tensor * cosine + swapped * sine


def mlp_half(normed, cot, slots, key, up_shift):
    blocks = xor_order(slots, key)
    up = jnp.concatenate([unpack_up(b[:256]) for b in blocks], axis=0)
    down = jnp.concatenate([b[256:] for b in blocks], axis=1)
    hidden = dot(normed, up) + up_shift[None, :]
    cdf = 0.5 * (1.0 + lax.erf(hidden * math.sqrt(0.5)))
    active = (hidden * cdf).astype(BF)
    slope = cdf + hidden * jnp.exp(-0.5 * hidden * hidden) * (1.0 / math.sqrt(2 * math.pi))
    out = dot(active, down)
    d_hidden = (dot(cot, down, ((1,), (1,))) * slope).astype(BF)
    down_grad = dot(active, cot, ((0,), (0,)))
    up_grad = dot(normed, d_hidden, ((0,), (0,)))
    up_shift_grad = jnp.sum(d_hidden.astype(F32), axis=0)
    d_second = dot(d_hidden, up, ((1,), (1,)))
    grads = jnp.stack(
        [
            jnp.concatenate(
                [pack_up(up_grad[128 * g : 128 * g + 128]), down_grad[:, 128 * g : 128 * g + 128]],
                axis=0,
            )
            for g in range(4)
        ]
    )
    return out, d_second, jnp.stack(xor_order(grads, key)), up_shift_grad


def att_head(normed, cot, slots, key, shift, cosine, sine, starts):
    blocks = xor_order(slots, key)
    project = jnp.concatenate([unpack_project(b[:192]) for b in blocks], axis=0)
    mix = jnp.concatenate([b[192:] for b in blocks], axis=1)
    cosine, sine = cosine[:, :HD], sine[:, :HD]
    projected = dot(normed, project) + shift[None, :]
    q = rotate(projected[:, :HD], cosine, sine).astype(BF)
    k = rotate(projected[:, HD : 2 * HD], cosine, sine).astype(BF)
    v = projected[:, 2 * HD :].astype(BF)
    scaling = HD**-0.5
    count = q.shape[0]
    place = jnp.arange(count, dtype=jnp.int32)
    allowed = (place[None, :] >= starts[:, None]) & (place[:, None] >= place[None, :])
    scores = jnp.where(allowed, dot(q, k, ((1,), (1,))) * scaling, MASKED)
    exponent = jnp.exp(scores - jnp.max(scores, axis=-1, keepdims=True))
    probability = exponent / jnp.sum(exponent, axis=-1, keepdims=True)
    prob_low = probability.astype(BF)
    context = dot(prob_low, v).astype(BF)
    out = dot(context, mix)
    mix_grad = dot(context, cot, ((0,), (0,)))
    d_context = dot(cot, mix, ((1,), (1,))).astype(BF)
    d_prob = dot(d_context, v, ((1,), (1,)))
    d_scores = probability * (d_prob - jnp.sum(d_prob * probability, axis=-1, keepdims=True))
    d_scores = d_scores.astype(BF)
    d_q = dot(d_scores, k) * scaling
    d_k = dot(d_scores, q, ((0,), (0,))) * scaling
    d_v = dot(prob_low, d_context, ((0,), (0,)))
    d_projected = jnp.concatenate(
        [rotate(d_q, cosine, -sine), rotate(d_k, cosine, -sine), d_v], axis=1
    ).astype(BF)
    project_grad = dot(normed, d_projected, ((0,), (0,)))
    shift_grad = jnp.sum(d_projected.astype(F32), axis=0)
    d_first = dot(d_projected, project, ((1,), (1,)))
    grads = jnp.stack(
        [
            jnp.concatenate(
                [
                    pack_project(project_grad[128 * g : 128 * g + 128]),
                    mix_grad[:, 128 * g : 128 * g + 128],
                ],
                axis=0,
            )
            for g in range(4)
        ]
    )
    return out, d_first, jnp.stack(xor_order(grads, key)), shift_grad


def on_device(
    inputs,
    seg_start,
    cotangent,
    project_weight,
    project_bias,
    output_weight,
    output_bias,
    up_weight,
    up_bias,
    down_weight,
    down_bias,
    first_gain,
    first_bias,
    second_gain,
    second_bias,
):
    rows, cols = lax.axis_size("row"), lax.axis_size("col")
    per = cols // rows
    r, c = lax.axis_index("row"), lax.axis_index("col")
    both = ("row", "col")
    count, width = inputs.shape[1], inputs.shape[2]
    paired = per == 2

    def flip(value, bit):
        return lax.ppermute(value, "row", [(i, i ^ bit) for i in range(rows)])

    def home(i, k):
        rr, cc = divmod(i, cols)
        z, y = divmod(cc, per)
        return z * cols + (rr ^ k) * per + y

    everyone = range(rows * cols)

    def spread(block):
        parts = [
            lax.ppermute(block, both, [(i, home(i, k)) for i in everyone]) for k in range(rows)
        ]
        own = jnp.stack(parts)
        return own, lax.ppermute(own, "col", [(i, i ^ 1) for i in range(cols)])

    def bring_other(grads):
        return lax.ppermute(grads, "col", [(i, i ^ 1) for i in range(cols)])

    def collect(grads):
        parts = [
            lax.ppermute(grads[k], both, [(home(i, k), i) for i in everyone]) for k in range(rows)
        ]
        return sum(p.astype(F32) for p in parts)

    def slot_of(i):
        rr, cc = divmod(i, cols)
        return (cc // per) * cols + (cc % per) * rows + rr

    def fetch(block):
        moved = lax.ppermute(block, both, [(i, slot_of(i)) for i in everyone])
        whole = lax.all_gather(moved, "col", axis=0)
        return whole.reshape((per, rows) + block.shape)

    def fetch_columns(block):
        whole = fetch(block).transpose(1, 2, 0, 3).reshape(rows, block.shape[0], 2, -1)
        return whole.transpose(2, 0, 1, 3)

    def fetch_rows(block):
        whole = fetch(block).transpose(1, 0, 2, 3).reshape(rows, 2, -1, block.shape[1])
        return whole.transpose(1, 0, 2, 3)

    def deliver(blocks):
        flat = blocks.reshape((cols,) + blocks.shape[2:]).astype(BF)
        mine = lax.psum_scatter(flat, "col", scatter_dimension=0, tiled=False)
        return lax.ppermute(mine, both, [(slot_of(i), i) for i in everyone]).astype(F32)

    def deliver_columns(halves):
        deep = halves.shape[2]
        whole = halves.transpose(1, 2, 0, 3).reshape(rows, deep, per, -1)
        return deliver(whole.transpose(2, 0, 1, 3))

    def deliver_rows(halves):
        wide = halves.shape[3]
        whole = halves.transpose(1, 0, 2, 3).reshape(rows, per, -1, wide)
        return deliver(whole.transpose(1, 0, 2, 3))

    act = jnp.stack([inputs[0], cotangent[0]])
    act_two = jnp.stack([act, flip(act, 2)])
    act_far = flip(act_two, 1)
    act_all = jnp.stack([act_two[0], act_far[0], act_two[1], act_far[1]])
    act_all = jnp.stack(xor_order(act_all, r), axis=1)
    x_all = act_all[0].reshape(-1, width)
    cot_all = act_all[1].reshape(-1, width)

    if paired:
        key, y = c // per, c % per
        mlp_slots = spread(jnp.concatenate([pack_up(up_weight), down_weight], axis=0))
        att_slots = spread(jnp.concatenate([pack_project(project_weight), output_weight], axis=0))
    else:
        key, y = jnp.int32(0), jnp.int32(0)
        ups, downs = fetch_columns(up_weight), fetch_rows(down_weight)
        projects, mixes = fetch_columns(project_weight), fetch_rows(output_weight)
        mlp_slots = [
            jnp.stack(
                [jnp.concatenate([pack_up(ups[h, g]), downs[h, g]], axis=0) for g in range(rows)]
            )
            for h in range(2)
        ]
        att_slots = [
            jnp.stack(
                [
                    jnp.concatenate([pack_project(projects[h, g]), mixes[h, g]], axis=0)
                    for g in range(rows)
                ]
            )
            for h in range(2)
        ]

    seg_own = seg_start[0]
    small = jnp.concatenate(
        [
            first_gain,
            first_bias,
            second_gain,
            second_bias,
            output_bias,
            down_bias,
            project_bias,
            up_bias,
            (seg_own // 32).astype(BF),
            (seg_own % 32).astype(BF),
        ]
    )
    every = lax.all_to_all(
        jnp.broadcast_to(small[None], (rows * cols, small.shape[0])), both, 0, 0, tiled=True
    )
    part = first_gain.shape[0]
    norms = every[:, : 6 * part].reshape(-1, 6, part).transpose(1, 0, 2).reshape(6, -1).astype(F32)
    lengths = (project_bias.shape[0], up_bias.shape[0])
    begin = 6 * part
    mine = lax.dynamic_slice_in_dim(every, r * cols, cols, axis=0)
    project_shift = mine[:, begin : begin + lengths[0]].reshape(2, -1).astype(F32)
    begin += lengths[0]
    up_shift = mine[:, begin : begin + lengths[1]].reshape(2, -1).astype(F32)
    begin += lengths[1]
    project_shift = jnp.where(y == 0, project_shift, project_shift[::-1])
    up_shift = jnp.where(y == 0, up_shift, up_shift[::-1])
    segs = every.reshape(rows, cols, -1)[:, :, begin:]
    segs = lax.dynamic_index_in_dim(segs, c, axis=1, keepdims=False).astype(jnp.int32)
    starts = (segs[:, :count] * 32 + segs[:, count:]).reshape(-1)
    cosine, sine = rotary_tables(jnp.arange(rows * count, dtype=jnp.int32) - starts)

    xhat, root = normalize(x_all.astype(F32))
    normed_one = (xhat * norms[0] + norms[1]).astype(BF)
    normed_two = (xhat * norms[2] + norms[3]).astype(BF)

    out_oth, d2_oth, mlp_send, ub_oth = mlp_half(normed_two, cot_all, mlp_slots[1], key, up_shift[1])
    out_own, d2_own, mlp_keep, ub_own = mlp_half(normed_two, cot_all, mlp_slots[0], key, up_shift[0])
    out_a, d1_oth, att_send, pb_oth = att_head(
        normed_one, cot_all, att_slots[1], key, project_shift[1], cosine, sine, starts
    )
    out_b, d1_own, att_keep, pb_own = att_head(
        normed_one, cot_all, att_slots[0], key, project_shift[0], cosine, sine, starts
    )
    d_first, d_second = d1_oth + d1_own, d2_oth + d2_own
    out_part = out_oth + out_own + out_a + out_b
    e_part = d_first * norms[0] + d_second * norms[2]

    if paired:
        mlp_done = collect((mlp_keep + bring_other(mlp_send.astype(BF)).astype(F32)).astype(BF))
        att_done = collect((att_keep + bring_other(att_send.astype(BF)).astype(F32)).astype(BF))
        project_done, mix_done = unpack_project(att_done[:192]), att_done[192:]
        up_done, down_done = unpack_up(mlp_done[:256]), mlp_done[256:]
    else:
        att_grads, mlp_grads = jnp.stack([att_keep, att_send]), jnp.stack([mlp_keep, mlp_send])
        every_pair = [(h, g) for h in range(2) for g in range(rows)]

        def regroup(parts):
            return jnp.stack(parts).reshape((2, rows) + parts[0].shape)

        project_done = deliver_columns(
            regroup([unpack_project(att_grads[h, g][:192]) for h, g in every_pair])
        )
        mix_done = deliver_rows(regroup([att_grads[h, g][192:] for h, g in every_pair]))
        up_done = deliver_columns(
            regroup([unpack_up(mlp_grads[h, g][:256]) for h, g in every_pair])
        )
        down_done = deliver_rows(regroup([mlp_grads[h, g][256:] for h, g in every_pair]))

    oe = jnp.stack([out_part, e_part]).reshape(2, rows, count, width)
    chunk = [lax.dynamic_index_in_dim(oe, r ^ j, axis=1, keepdims=False) for j in range(4)]
    near = flip(jnp.stack([chunk[1], chunk[3]]).astype(BF), 1).astype(F32)
    mine_sum, far_sum = chunk[0] + near[0], chunk[2] + near[1]
    total = mine_sum + flip(far_sum.astype(BF), 2).astype(F32)
    x_own = inputs[0].astype(F32)
    cot_own = cotangent[0].astype(F32)
    output = (x_own + total[0] + norms[4] + norms[5]).astype(BF)[None]
    e_all = total[1]
    xhat_own, root_own = normalize(x_own)
    input_grad = cot_own + root_own * (
        e_all
        - jnp.mean(e_all, axis=-1, keepdims=True)
        - xhat_own * jnp.mean(e_all * xhat_own, axis=-1, keepdims=True)
    )

    everywhere = jnp.stack(
        [
            jnp.sum(d_first * xhat, axis=0),
            jnp.sum(d_first, axis=0),
            jnp.sum(d_second * xhat, axis=0),
            jnp.sum(d_second, axis=0),
            jnp.sum(cot_own, axis=0),
        ]
    )
    everywhere = everywhere.reshape(5, rows * cols, part).transpose(1, 0, 2).reshape(rows * cols, -1)

    def by_half(own, other):
        first = jnp.where(y == 0, own, other)
        second = jnp.where(y == 0, other, own)
        return jnp.concatenate([first, second]).reshape(cols, -1)

    local = jnp.concatenate([by_half(pb_own, pb_oth), by_half(ub_own, ub_oth)], axis=1)
    local = lax.dynamic_update_slice(
        jnp.zeros((rows * cols, local.shape[1]), F32), local, (r * cols, 0)
    )
    sums = lax.all_to_all(
        jnp.concatenate([everywhere, local], axis=1), both, 0, 0, tiled=True
    ).sum(axis=0)
    pieces = [sums[i * part : (i + 1) * part] for i in range(5)]
    project_shift_grad = sums[5 * part : 5 * part + lengths[0]]
    up_shift_grad = sums[5 * part + lengths[0] :]
    return (
        output,
        input_grad[None],
        project_done,
        project_shift_grad,
        mix_done,
        pieces[4],
        up_done,
        up_shift_grad,
        down_done,
        pieces[4],
        pieces[0],
        pieces[1],
        pieces[2],
        pieces[3],
    )


def solution(mesh):
    return jax.shard_map(
        on_device,
        mesh=mesh,
        in_specs=(
            P("col", "row", None),
            P("col", "row"),
            P("col", "row", None),
            P("row", "col"),
            P(("row", "col")),
            P("col", "row"),
            P(("row", "col")),
            P("row", "col"),
            P(("row", "col")),
            P("col", "row"),
            P(("row", "col")),
            P(("row", "col")),
            P(("row", "col")),
            P(("row", "col")),
            P(("row", "col")),
        ),
        out_specs=(
            P("col", "row", None),
            P("col", "row", None),
            P("row", "col"),
            P(("row", "col")),
            P("col", "row"),
            P(("row", "col")),
            P("row", "col"),
            P(("row", "col")),
            P("col", "row"),
            P(("row", "col")),
            P(("row", "col")),
            P(("row", "col")),
            P(("row", "col")),
            P(("row", "col")),
        ),
        check_vma=False,
    )
```

time: 1160 us -> 212 us (0.18)
  waiting for transfers between devices: 797 us -> 49.1 us
  blocking collectives: 220 us -> 0 us
  starting transfers between devices: 1.32 us -> 51.6 us
  matrix products: 64.2 us -> 36.7 us
  between operations: 16.8 us -> 3.03 us
    unnamed x32 -> x0, waiting for transfers between devices: 481 us -> none
    reduce_scatter x7 -> x0, waiting for transfers between devices: 316 us -> none  [the longest x1 88.4 us: scatter_grads(): lax.psum_scatter(up_grad, 'col', scatter_dimension=1, tiled=True)]
    all_gather x14 -> x0, blocking collectives: 208 us -> none  [the longest x1 31.7 us: gather_params(): lax.all_gather(parted[2], 'col', axis=0, tiled=True)]
    ppermute x0 -> x24, waiting for transfers between devices: none -> 43.2 us  [the longest x8 21.7 us: collect(): lax.ppermute(grads[k], both, [(home(i, k), i) for i in everyone])]
    ppermute x0 -> x24, starting transfers between devices: none -> 41 us  [the longest x8 14.1 us: collect(): lax.ppermute(grads[k], both, [(home(i, k), i) for i in everyone])]
    unnamed x71 -> x224, local copies, waits for them, and re-layouts: 28.9 us -> 6.36 us
    dot_general x17 -> x36, matrix products: 56.7 us -> 36.7 us  [dot(): return lax.dot_general(a, b, (dims, ((), ())), preferred_element_type=F32)]
    slice x2 -> x52, local copies, waits for them, and re-layouts: 0.75 us -> 14.9 us  [the longest x3 2.41 us: pack_project(): b[:half, 128:]]
  transfers between devices with their start and end apart: 22 -> 26, of which waited for: 16 -> 7; matrix products, arithmetic and copies ran while one was open for 10% -> 21% of each run, Pallas kernels for 0% -> 0%
where the time goes in v1:
time: 212 us; the launch traced here: 211 us
  starting transfers between devices  51.6 us (24%)
  waiting for transfers between devices  49.1 us (23%)
  local copies, waits for them, and re-layouts  38.1 us (18%)
  matrix products  36.7 us (17%)
  other arithmetic  32.4 us (15%)
  between operations  3.03 us (1%)
    dot_general x36, matrix products, dot(): return lax.dot_general(a, b, (dims, ((), ())), preferred_element_type=F32)  36.7 us
    ppermute x8, waiting for transfers between devices, collect(): lax.ppermute(grads[k], both, [(home(i, k), i) for i in everyone])  21.7 us
    ppermute x8, starting transfers between devices, collect(): lax.ppermute(grads[k], both, [(home(i, k), i) for i in everyone])  14.1 us
    ppermute x8, starting transfers between devices, spread(): lax.ppermute(block, both, [(i, home(i, k)) for i in everyone])  13.1 us
    ppermute x2, waiting for transfers between devices, spread(): return (own, lax.ppermute(own, 'col', [(i, i ^ 1) for i in range(cols)]))  12.6 us
    ppermute x4, waiting for transfers between devices, flip(): return lax.ppermute(value, 'row', [(i, i ^ bit) for i in range(rows)])  8.94 us
    ppermute x4, starting transfers between devices, flip(): return lax.ppermute(value, 'row', [(i, i ^ bit) for i in range(rows)])  8.57 us
    all_to_all x1, starting transfers between devices, on_device(): lax.all_to_all(jnp.broadcast_to(small[None], (rows * cols, small.shape[0]...  7.01 us
  transfers between devices with their start and end apart: 26, of which 7 were waited for; matrix products, arithmetic and copies ran while one was open for 21% of the time, Pallas kernels for 0%

profile of v1, /device:TPU:0, one launch (start us, length us, event | category | flops | bytes accessed | tf_op | source)
XLA Modules:
  0.0 210.9 jit_solution(8056744722025026955)
XLA Ops:
  3.3 5.1 %collective-permute-start.10 = (bf16[256,128]{0,1:T(8,128)(2,1)S(1)}, bf16[256,128]{0,1:T(8,128)(2,1)S(1)}, u32[]{:S(2)}, u32[]{:S(2)}) collective-permute-start(bf16[256,128]{0,1:T(8,128)(2,1)S(1)} %pad_maximum_fusion.20), channel_id=1, source_target_pairs={{0,6},{1,7},{2,14},{3,15},{4,22},{5,23},{6,30},{7,31},{8,4},{9,5},... | collective-permute-start | bytes 196616 | tf_op jit(solution)/shard_map/ppermute | solution.py:182
  8.4 1.5 collective-permute-start.9
  11.2 5.4 %concatenate.237 = bf16[720]{0:T(1024)(128)(2,1)S(1)} concatenate(bf16[16]{0:T(256)(128)(2,1)} %param.27, bf16[16]{0:T(256)(128)(2,1)} %param.28, bf16[16]{0:T(256)(128)(2,1)} %param.29, bf16[16]{0:T(256)(128)(2,1)} %param.30, bf16[16]{0:T(256)(128)(2,1)} %param.22, bf16[16]{0:T(256)(128)(2,1)} %param.26, bf16[48]{0:T(256)(128)(2,1)} %param.20, bf16[64]{0:T(256)(128)(2,1)} %param.24, ...), dimensions={0} | concatenate | bytes 2880 | tf_op jit(solution)/shard_map/concatenate | solution.py:261
  18.9 7.0 %all-to-all-start = ((bf16[32,2,360]{2,1,0:T(2,128)(2,1)}), bf16[32,2,360]{2,1,0:T(2,128)(2,1)S(1)}, u32[]{:S(2)}, u32[]{:S(2)}) async-start(bf16[32,2,360]{2,1,0:T(2,128)(2,1)} %reshape.308), calls=%async_computation | async-start | bytes 98304 | tf_op jit(solution)/shard_map/all_to_all | solution.py:275
  27.6 3.7 %collective-permute-start.5 = (bf16[512,128]{1,0:T(8,128)(2,1)S(1)}, bf16[512,128]{1,0:T(8,128)(2,1)S(1)}, u32[]{:S(2)}, u32[]{:S(2)}) collective-permute-start(bf16[512,128]{1,0:T(8,128)(2,1)S(1)} %pad_maximum_fusion.16), channel_id=1, source_target_pairs={{0,6},{1,7},{2,14},{3,15},{4,22},{5,23},{6,30},{7,31},{8,4},{9,5},... | collective-permute-start | bytes 393224 | tf_op jit(solution)/shard_map/ppermute | solution.py:182
  34.2 1.5 collective-permute-start.4
  36.4 4.4 %collective-permute-start = (bf16[2,256,512]{2,1,0:T(8,128)(2,1)S(1)}, bf16[2,256,512]{2,1,0:T(8,128)(2,1)S(1)}, u32[]{:S(2)}, u32[]{:S(2)}) collective-permute-start(bf16[2,256,512]{2,1,0:T(8,128)(2,1)S(1)} %constant_dynamic-update-slice_fusion.1), channel_id=1, source_target_pairs={{0,16},{8,24},{16,0},{24,8},{1,17},{9,25},{17,1},{25,9},{2,18},{10... | collective-permute-start | bytes 1572872 | tf_op jit(solution)/shard_map/ppermute | solution.py:171
  48.5 1.5 collective-permute-start.11
  50.1 6.2 %collective-permute-done = bf16[2,256,512]{2,1,0:T(8,128)(2,1)S(1)} collective-permute-done((bf16[2,256,512]{2,1,0:T(8,128)(2,1)S(1)}, bf16[2,256,512]{2,1,0:T(8,128)(2,1)S(1)}, u32[]{:S(2)}, u32[]{:S(2)}) %collective-permute-start) | collective-permute-done | bytes 524320 | tf_op jit(solution)/shard_map/ppermute | solution.py:171
  56.6 1.5 collective-permute-start.6
  58.4 12.6 %collective-permute-done.6 = bf16[4,512,128]{2,1,0:T(8,128)(2,1)S(1)} collective-permute-done((bf16[4,512,128]{2,1,0:T(8,128)(2,1)S(1)}, bf16[4,512,128]{2,1,0:T(8,128)(2,1)S(1)}, u32[]{:S(2)}, u32[]{:S(2)}) %collective-permute-start.6) | collective-permute-done | bytes 524320 | tf_op jit(solution)/shard_map/ppermute | solution.py:185
  76.5 1.8 fusion.68
  79.4 1.9 fusion.86
  86.6 1.8 fusion.69
  95.6 1.5 convolution_convert_fusion.1
  108.6 1.8 fusion.85
  111.5 1.7 fusion.67
  123.7 1.5 collective-permute-start.19
  133.0 1.7 convolution_add_fusion.1
  134.8 2.7 %multiply_reduce_fusion.2 = (f32[512]{0:T(512)S(1)}, f32[512]{0:T(512)S(1)}, f32[512]{0:T(512)S(1)}, f32[512]{0:T(512)S(1)}, f32[1024,512]{1,0:T(8,128)}) fusion(f32[1024]{0:T(1024)S(1)} %bitcast.332, f32[1024]{0:T(1024)S(1)} %bitcast.330, bf16[2,4,256,512]{3,2,1,0:T(8,128)(2,1)S(1)} %pad_maximum_fusion.1, f32[1024,512]{1,0:T(8,128)S(1)} %convolution_add_fusion.1, ...), kind=kOutput, calls=%fused_computation.27 | convolution fusion | flops 277346304 | bytes 8146944 | tf_op jit(solution)/shard_map/dot_general | solution.py:26
  137.9 3.5 %add_add_fusion = f32[1024,512]{1,0:T(8,128)S(1)} fusion(f32[1024,512]{1,0:T(8,128)} %fusion.69, f32[1024,512]{1,0:T(8,128)} %fusion.68, f32[1024,512]{1,0:T(8,128)} %fusion.67, bf16[1024,64]{0,1:T(8,128)(2,1)S(1)} %copy-done.12, bf16[64,128]{0,1:T(8,128)(2,1)S(1)} %copy-done.21, bf16[64,128]{0,1:T(8,128)(2,1)S(1)} %copy-done.23, ...), kind=kOutput, calls=%fused_computation.30 | convolution fusion | flops 68943872 | bytes 8585216 | tf_op jit(solution)/shard_map/dot_general | solution.py:26
  146.0 5.7 %collective-permute-start.18 = (bf16[256,128]{0,1:T(8,128)(2,1)S(1)}, bf16[256,128]{0,1:T(8,128)(2,1)S(1)}, u32[]{:S(2)}, u32[]{:S(2)}) collective-permute-start(bf16[256,128]{0,1:T(8,128)(2,1)S(1)} %get-tuple-element.173), channel_id=1, source_target_pairs={{6,0},{7,1},{14,2},{15,3},{22,4},{23,5},{30,6},{31,7},{4,8},{5,9},... | collective-permute-start | bytes 196616 | tf_op jit(solution)/shard_map/ppermute | solution.py:192
  151.9 4.3 %collective-permute-done.18 = bf16[256,128]{0,1:T(8,128)(2,1)S(1)} collective-permute-done((bf16[256,128]{0,1:T(8,128)(2,1)S(1)}, bf16[256,128]{0,1:T(8,128)(2,1)S(1)}, u32[]{:S(2)}, u32[]{:S(2)}) %collective-permute-start.18) | collective-permute-done | bytes 65568 | tf_op jit(solution)/shard_map/ppermute | solution.py:192
  156.1 4.9 %collective-permute-done.17 = bf16[256,128]{0,1:T(8,128)(2,1)S(1)} collective-permute-done((bf16[256,128]{0,1:T(8,128)(2,1)S(1)}, bf16[256,128]{0,1:T(8,128)(2,1)S(1)}, u32[]{:S(2)}, u32[]{:S(2)}) %collective-permute-start.17) | collective-permute-done | bytes 65568 | tf_op jit(solution)/shard_map/ppermute | solution.py:192
  163.0 1.6 collective-permute-start.20
  164.6 5.4 %collective-permute-start.23 = (bf16[512,128]{1,0:T(8,128)(2,1)}, bf16[512,128]{1,0:T(8,128)(2,1)S(1)}, u32[]{:S(2)}, u32[]{:S(2)}) collective-permute-start(bf16[512,128]{1,0:T(8,128)(2,1)} %get-tuple-element.94), channel_id=1, source_target_pairs={{6,0},{7,1},{14,2},{15,3},{22,4},{23,5},{30,6},{31,7},{4,8},{5,9},... | collective-permute-start | bytes 393224 | tf_op jit(solution)/shard_map/ppermute | solution.py:192
  172.5 4.0 %collective-permute-start.13 = (bf16[2,256,512]{2,1,0:T(8,128)(2,1)}, bf16[2,256,512]{2,1,0:T(8,128)(2,1)}, u32[]{:S(2)}, u32[]{:S(2)}) collective-permute-start(bf16[2,256,512]{2,1,0:T(8,128)(2,1)} %fusion.19), channel_id=1, source_target_pairs={{0,16},{8,24},{16,0},{24,8},{1,17},{9,25},{17,1},{25,9},{2,18},{10... | collective-permute-start | bytes 1572872 | tf_op jit(solution)/shard_map/ppermute | solution.py:171
  178.0 12.6 %collective-permute-done.22 = bf16[512,128]{1,0:T(8,128)(2,1)S(1)} collective-permute-done((bf16[512,128]{1,0:T(8,128)(2,1)}, bf16[512,128]{1,0:T(8,128)(2,1)S(1)}, u32[]{:S(2)}, u32[]{:S(2)}) %collective-permute-start.22) | collective-permute-done | bytes 131104 | tf_op jit(solution)/shard_map/ppermute | solution.py:192
  190.7 2.8 %collective-permute-done.13 = bf16[2,256,512]{2,1,0:T(8,128)(2,1)} collective-permute-done((bf16[2,256,512]{2,1,0:T(8,128)(2,1)}, bf16[2,256,512]{2,1,0:T(8,128)(2,1)}, u32[]{:S(2)}, u32[]{:S(2)}) %collective-permute-start.13) | collective-permute-done | bytes 524320 | tf_op jit(solution)/shard_map/ppermute | solution.py:171
  193.5 1.8 fusion.23
  197.8 3.6 %all-to-all-start.1 = ((f32[32,1,192]{2,1,0:T(1,128)}), f32[32,1,192]{2,1,0:T(1,128)S(1)}, u32[]{:S(2)}, u32[]{:S(2)}) async-start(f32[32,1,192]{2,1,0:T(1,128)} %all_to_all.14), calls=%async_computation.1 | async-start | bytes 65536 | tf_op jit(solution)/shard_map/all_to_all | solution.py:367
  202.8 5.9 %all-to-all-done.1 = f32[32,1,192]{2,1,0:T(1,128)S(1)} async-done(((f32[32,1,192]{2,1,0:T(1,128)}), f32[32,1,192]{2,1,0:T(1,128)S(1)}, u32[]{:S(2)}, u32[]{:S(2)}) %all-to-all-start.1) | async-done | bytes 24608 | tf_op jit(solution)/shard_map/all_to_all | solution.py:367
  (450 shorter events, 85.2 us)
Async XLA Ops:
  3.3 30.9 %collective-permute-start.10 = (bf16[256,128]{0,1:T(8,128)(2,1)S(1)}, bf16[256,128]{0,1:T(8,128)(2,1)S(1)}, u32[]{:S(2)}, u32[]{:S(2)}) collective-permute-start(bf16[256,128]{0,1:T(8,128)(2,1)S(1)} %pad_maximum_fusion.20), channel_id=1, source_target_pairs={{0,6},{1,7},{2,14},{3,15},{4,22},{5,23},{6,30},{7,31},{8,4},{9,5},... | collective-permute-start | bytes 196616 | tf_op jit(solution)/shard_map/ppermute | solution.py:182
  8.4 27.3 %collective-permute-start.9 = (bf16[256,128]{0,1:T(8,128)(2,1)S(1)}, bf16[256,128]{0,1:T(8,128)(2,1)S(1)}, u32[]{:S(2)}, u32[]{:S(2)}) collective-permute-start(bf16[256,128]{0,1:T(8,128)(2,1)S(1)} %pad_maximum_fusion.20), channel_id=1, source_target_pairs={{0,4},{1,5},{2,12},{3,13},{4,20},{5,21},{6,28},{7,29},{8,6},{9,7},... | collective-permute-start | bytes 196616 | tf_op jit(solution)/shard_map/ppermute | solution.py:182
  9.9 25.8 %collective-permute-start.8 = (bf16[256,128]{0,1:T(8,128)(2,1)S(1)}, bf16[256,128]{0,1:T(8,128)(2,1)S(1)}, u32[]{:S(2)}, u32[]{:S(2)}) collective-permute-start(bf16[256,128]{0,1:T(8,128)(2,1)S(1)} %pad_maximum_fusion.20), channel_id=1, source_target_pairs={{0,2},{1,3},{2,10},{3,11},{4,18},{5,19},{6,26},{7,27},{8,0},{9,1},... | collective-permute-start | bytes 196616 | tf_op jit(solution)/shard_map/ppermute | solution.py:182
  9.9 26.5 %collective-permute-start.7 = (bf16[256,128]{0,1:T(8,128)(2,1)S(1)}, bf16[256,128]{0,1:T(8,128)(2,1)S(1)}, u32[]{:S(2)}, u32[]{:S(2)}) collective-permute-start(bf16[256,128]{0,1:T(8,128)(2,1)S(1)} %pad_maximum_fusion.20), channel_id=1, source_target_pairs={{0,0},{1,1},{2,8},{3,9},{4,16},{5,17},{6,24},{7,25},{8,2},{9,3},{1... | collective-permute-start | bytes 196616 | tf_op jit(solution)/shard_map/ppermute | solution.py:182
  18.9 24.0 %all-to-all-start = ((bf16[32,2,360]{2,1,0:T(2,128)(2,1)}), bf16[32,2,360]{2,1,0:T(2,128)(2,1)S(1)}, u32[]{:S(2)}, u32[]{:S(2)}) async-start(bf16[32,2,360]{2,1,0:T(2,128)(2,1)} %reshape.308), calls=%async_computation | async-start | bytes 98304 | tf_op jit(solution)/shard_map/all_to_all | solution.py:275
  27.6 20.9 %collective-permute-start.5 = (bf16[512,128]{1,0:T(8,128)(2,1)S(1)}, bf16[512,128]{1,0:T(8,128)(2,1)S(1)}, u32[]{:S(2)}, u32[]{:S(2)}) collective-permute-start(bf16[512,128]{1,0:T(8,128)(2,1)S(1)} %pad_maximum_fusion.16), channel_id=1, source_target_pairs={{0,6},{1,7},{2,14},{3,15},{4,22},{5,23},{6,30},{7,31},{8,4},{9,5},... | collective-permute-start | bytes 393224 | tf_op jit(solution)/shard_map/ppermute | solution.py:182
  34.2 15.8 %collective-permute-start.4 = (bf16[512,128]{1,0:T(8,128)(2,1)S(1)}, bf16[512,128]{1,0:T(8,128)(2,1)S(1)}, u32[]{:S(2)}, u32[]{:S(2)}) collective-permute-start(bf16[512,128]{1,0:T(8,128)(2,1)S(1)} %pad_maximum_fusion.16), channel_id=1, source_target_pairs={{0,4},{1,5},{2,12},{3,13},{4,20},{5,21},{6,28},{7,29},{8,6},{9,7},... | collective-permute-start | bytes 393224 | tf_op jit(solution)/shard_map/ppermute | solution.py:182
  35.7 14.3 %collective-permute-start.3 = (bf16[512,128]{1,0:T(8,128)(2,1)S(1)}, bf16[512,128]{1,0:T(8,128)(2,1)S(1)}, u32[]{:S(2)}, u32[]{:S(2)}) collective-permute-start(bf16[512,128]{1,0:T(8,128)(2,1)S(1)} %pad_maximum_fusion.16), channel_id=1, source_target_pairs={{0,2},{1,3},{2,10},{3,11},{4,18},{5,19},{6,26},{7,27},{8,0},{9,1},... | collective-permute-start | bytes 393224 | tf_op jit(solution)/shard_map/ppermute | solution.py:182
  35.7 14.3 %collective-permute-start.2 = (bf16[512,128]{1,0:T(8,128)(2,1)S(1)}, bf16[512,128]{1,0:T(8,128)(2,1)S(1)}, u32[]{:S(2)}, u32[]{:S(2)}) collective-permute-start(bf16[512,128]{1,0:T(8,128)(2,1)S(1)} %pad_maximum_fusion.16), channel_id=1, source_target_pairs={{0,0},{1,1},{2,8},{3,9},{4,16},{5,17},{6,24},{7,25},{8,2},{9,3},{1... | collective-permute-start | bytes 393224 | tf_op jit(solution)/shard_map/ppermute | solution.py:182
  36.4 19.8 %collective-permute-start = (bf16[2,256,512]{2,1,0:T(8,128)(2,1)S(1)}, bf16[2,256,512]{2,1,0:T(8,128)(2,1)S(1)}, u32[]{:S(2)}, u32[]{:S(2)}) collective-permute-start(bf16[2,256,512]{2,1,0:T(8,128)(2,1)S(1)} %constant_dynamic-update-slice_fusion.1), channel_id=1, source_target_pairs={{0,16},{8,24},{16,0},{24,8},{1,17},{9,25},{17,1},{25,9},{2,18},{10... | collective-permute-start | bytes 1572872 | tf_op jit(solution)/shard_map/ppermute | solution.py:171
  48.5 9.7 %collective-permute-start.11 = (bf16[4,256,128]{1,2,0:T(8,128)(2,1)S(1)}, bf16[4,256,128]{1,2,0:T(8,128)(2,1)S(1)}, u32[]{:S(2)}, u32[]{:S(2)}) collective-permute-start(bf16[4,256,128]{1,2,0:T(8,128)(2,1)S(1)} %pad_maximum_fusion.14), channel_id=1, source_target_pairs={{0,1},{1,0},{2,3},{3,2},{4,5},{5,4},{6,7},{7,6},{8,9},{9,8},{10,11... | collective-permute-start | bytes 786440 | tf_op jit(solution)/shard_map/ppermute | solution.py:185
  56.4 14.6 %collective-permute-start.1 = (bf16[2,2,256,512]{3,2,1,0:T(8,128)(2,1)S(1)}, bf16[2,2,256,512]{3,2,1,0:T(8,128)(2,1)S(1)}, u32[]{:S(2)}, u32[]{:S(2)}) collective-permute-start(bf16[2,2,256,512]{3,2,1,0:T(8,128)(2,1)S(1)} %pad_maximum_fusion.2), channel_id=1, source_target_pairs={{0,8},{8,0},{16,24},{24,16},{1,9},{9,1},{17,25},{25,17},{2,10},{10... | collective-permute-start | bytes 3145736 | tf_op jit(solution)/shard_map/ppermute | solution.py:171
  56.5 54.0 %copy-start.63 = (bf16[128,128]{1,0:T(8,128)(2,1)}, bf16[128,128]{1,0:T(8,128)(2,1)S(1)}, u32[]{:S(2)}) copy-start(bf16[128,128]{1,0:T(8,128)(2,1)S(1)} %get-tuple-element.125) | copy-start | bytes 98308
  56.5 54.0 %copy-start.65 = (bf16[128,128]{1,0:T(8,128)(2,1)}, bf16[128,128]{1,0:T(8,128)(2,1)S(1)}, u32[]{:S(2)}) copy-start(bf16[128,128]{1,0:T(8,128)(2,1)S(1)} %get-tuple-element.126) | copy-start | bytes 98308
  56.5 54.0 %copy-start.67 = (bf16[128,128]{1,0:T(8,128)(2,1)}, bf16[128,128]{1,0:T(8,128)(2,1)S(1)}, u32[]{:S(2)}) copy-start(bf16[128,128]{1,0:T(8,128)(2,1)S(1)} %get-tuple-element.127) | copy-start | bytes 98308
  56.5 54.0 %copy-start.69 = (bf16[128,128]{1,0:T(8,128)(2,1)}, bf16[128,128]{1,0:T(8,128)(2,1)S(1)}, u32[]{:S(2)}) copy-start(bf16[128,128]{1,0:T(8,128)(2,1)S(1)} %get-tuple-element.128) | copy-start | bytes 98308
  56.5 54.0 %copy-start.71 = (bf16[128,128]{1,0:T(8,128)(2,1)}, bf16[128,128]{1,0:T(8,128)(2,1)S(1)}, u32[]{:S(2)}) copy-start(bf16[128,128]{1,0:T(8,128)(2,1)S(1)} %get-tuple-element.129) | copy-start | bytes 98308
  56.5 54.0 %copy-start.73 = (bf16[128,128]{1,0:T(8,128)(2,1)}, bf16[128,128]{1,0:T(8,128)(2,1)S(1)}, u32[]{:S(2)}) copy-start(bf16[128,128]{1,0:T(8,128)(2,1)S(1)} %get-tuple-element.130) | copy-start | bytes 98308
  56.6 14.4 %collective-permute-start.6 = (bf16[4,512,128]{2,1,0:T(8,128)(2,1)S(1)}, bf16[4,512,128]{2,1,0:T(8,128)(2,1)S(1)}, u32[]{:S(2)}, u32[]{:S(2)}) collective-permute-start(bf16[4,512,128]{2,1,0:T(8,128)(2,1)S(1)} %pad_maximum_fusion.6), channel_id=1, source_target_pairs={{0,1},{1,0},{2,3},{3,2},{4,5},{5,4},{6,7},{7,6},{8,9},{9,8},{10,11... | collective-permute-start | bytes 1572872 | tf_op jit(solution)/shard_map/ppermute | solution.py:185
  123.7 37.4 %collective-permute-start.19 = (bf16[4,512,128]{2,1,0:T(8,128)(2,1)}, bf16[4,512,128]{2,1,0:T(8,128)(2,1)}, u32[]{:S(2)}, u32[]{:S(2)}) collective-permute-start(bf16[4,512,128]{2,1,0:T(8,128)(2,1)} %pad_maximum_fusion.9), channel_id=1, source_target_pairs={{0,1},{1,0},{2,3},{3,2},{4,5},{5,4},{6,7},{7,6},{8,9},{9,8},{10,11... | collective-permute-start | bytes 1572872 | tf_op jit(solution)/shard_map/ppermute | solution.py:188
  132.3 11.9 %collective-permute-start.14 = (bf16[4,256,128]{1,2,0:T(8,128)(2,1)}, bf16[4,256,128]{1,2,0:T(8,128)(2,1)}, u32[]{:S(2)}, u32[]{:S(2)}) collective-permute-start(bf16[4,256,128]{1,2,0:T(8,128)(2,1)} %pad_maximum_fusion.15), channel_id=1, source_target_pairs={{0,1},{1,0},{2,3},{3,2},{4,5},{5,4},{6,7},{7,6},{8,9},{9,8},{10,11... | collective-permute-start | bytes 786440 | tf_op jit(solution)/shard_map/ppermute | solution.py:188
  141.8 28.9 %collective-permute-start.12 = (bf16[2,2,256,512]{3,2,1,0:T(8,128)(2,1)S(1)}, bf16[2,2,256,512]{3,2,1,0:T(8,128)(2,1)S(1)}, u32[]{:S(2)}, u32[]{:S(2)}) collective-permute-start(bf16[2,2,256,512]{3,2,1,0:T(8,128)(2,1)S(1)} %pad_maximum_fusion.3), channel_id=1, source_target_pairs={{0,8},{8,0},{16,24},{24,16},{1,9},{9,1},{17,25},{25,17},{2,10},{10... | collective-permute-start | bytes 3145736 | tf_op jit(solution)/shard_map/ppermute | solution.py:171
  145.3 6.4 %collective-permute-start.15 = (bf16[256,128]{0,1:T(8,128)(2,1)S(1)}, bf16[256,128]{0,1:T(8,128)(2,1)S(1)}, u32[]{:S(2)}, u32[]{:S(2)}) collective-permute-start(bf16[256,128]{0,1:T(8,128)(2,1)S(1)} %get-tuple-element.172), channel_id=1, source_target_pairs={{0,0},{1,1},{8,2},{9,3},{16,4},{17,5},{24,6},{25,7},{2,8},{3,9},{1... | collective-permute-start | bytes 196616 | tf_op jit(solution)/shard_map/ppermute | solution.py:192
  146.0 10.1 %collective-permute-start.18 = (bf16[256,128]{0,1:T(8,128)(2,1)S(1)}, bf16[256,128]{0,1:T(8,128)(2,1)S(1)}, u32[]{:S(2)}, u32[]{:S(2)}) collective-permute-start(bf16[256,128]{0,1:T(8,128)(2,1)S(1)} %get-tuple-element.173), channel_id=1, source_target_pairs={{6,0},{7,1},{14,2},{15,3},{22,4},{23,5},{30,6},{31,7},{4,8},{5,9},... | collective-permute-start | bytes 196616 | tf_op jit(solution)/shard_map/ppermute | solution.py:192
  151.7 9.3 %collective-permute-start.17 = (bf16[256,128]{0,1:T(8,128)(2,1)S(1)}, bf16[256,128]{0,1:T(8,128)(2,1)S(1)}, u32[]{:S(2)}, u32[]{:S(2)}) collective-permute-start(bf16[256,128]{0,1:T(8,128)(2,1)S(1)} %get-tuple-element.174), channel_id=1, source_target_pairs={{4,0},{5,1},{12,2},{13,3},{20,4},{21,5},{28,6},{29,7},{6,8},{7,9},... | collective-permute-start | bytes 196616 | tf_op jit(solution)/shard_map/ppermute | solution.py:192
  151.7 9.3 %collective-permute-start.16 = (bf16[256,128]{0,1:T(8,128)(2,1)S(1)}, bf16[256,128]{0,1:T(8,128)(2,1)S(1)}, u32[]{:S(2)}, u32[]{:S(2)}) collective-permute-start(bf16[256,128]{0,1:T(8,128)(2,1)S(1)} %get-tuple-element.175), channel_id=1, source_target_pairs={{2,0},{3,1},{10,2},{11,3},{18,4},{19,5},{26,6},{27,7},{0,8},{1,9},... | collective-permute-start | bytes 196616 | tf_op jit(solution)/shard_map/ppermute | solution.py:192
  163.0 15.0 %collective-permute-start.20 = (bf16[512,128]{1,0:T(8,128)(2,1)}, bf16[512,128]{1,0:T(8,128)(2,1)S(1)}, u32[]{:S(2)}, u32[]{:S(2)}) collective-permute-start(bf16[512,128]{1,0:T(8,128)(2,1)} %get-tuple-element.93), channel_id=1, source_target_pairs={{0,0},{1,1},{8,2},{9,3},{16,4},{17,5},{24,6},{25,7},{2,8},{3,9},{1... | collective-permute-start | bytes 393224 | tf_op jit(solution)/shard_map/ppermute | solution.py:192
  164.6 13.5 %collective-permute-start.23 = (bf16[512,128]{1,0:T(8,128)(2,1)}, bf16[512,128]{1,0:T(8,128)(2,1)S(1)}, u32[]{:S(2)}, u32[]{:S(2)}) collective-permute-start(bf16[512,128]{1,0:T(8,128)(2,1)} %get-tuple-element.94), channel_id=1, source_target_pairs={{6,0},{7,1},{14,2},{15,3},{22,4},{23,5},{30,6},{31,7},{4,8},{5,9},... | collective-permute-start | bytes 393224 | tf_op jit(solution)/shard_map/ppermute | solution.py:192
  170.0 20.6 %collective-permute-start.22 = (bf16[512,128]{1,0:T(8,128)(2,1)}, bf16[512,128]{1,0:T(8,128)(2,1)S(1)}, u32[]{:S(2)}, u32[]{:S(2)}) collective-permute-start(bf16[512,128]{1,0:T(8,128)(2,1)} %get-tuple-element.95), channel_id=1, source_target_pairs={{4,0},{5,1},{12,2},{13,3},{20,4},{21,5},{28,6},{29,7},{6,8},{7,9},... | collective-permute-start | bytes 393224 | tf_op jit(solution)/shard_map/ppermute | solution.py:192
  170.7 19.9 %collective-permute-start.21 = (bf16[512,128]{1,0:T(8,128)(2,1)S(1)}, bf16[512,128]{1,0:T(8,128)(2,1)S(1)}, u32[]{:S(2)}, u32[]{:S(2)}) collective-permute-start(bf16[512,128]{1,0:T(8,128)(2,1)S(1)} %get-tuple-element.96), channel_id=1, source_target_pairs={{2,0},{3,1},{10,2},{11,3},{18,4},{19,5},{26,6},{27,7},{0,8},{1,9},... | collective-permute-start | bytes 393224 | tf_op jit(solution)/shard_map/ppermute | solution.py:192
  172.5 21.0 %collective-permute-start.13 = (bf16[2,256,512]{2,1,0:T(8,128)(2,1)}, bf16[2,256,512]{2,1,0:T(8,128)(2,1)}, u32[]{:S(2)}, u32[]{:S(2)}) collective-permute-start(bf16[2,256,512]{2,1,0:T(8,128)(2,1)} %fusion.19), channel_id=1, source_target_pairs={{0,16},{8,24},{16,0},{24,8},{1,17},{9,25},{17,1},{25,9},{2,18},{10... | collective-permute-start | bytes 1572872 | tf_op jit(solution)/shard_map/ppermute | solution.py:171
  197.8 10.8 %all-to-all-start.1 = ((f32[32,1,192]{2,1,0:T(1,128)}), f32[32,1,192]{2,1,0:T(1,128)S(1)}, u32[]{:S(2)}, u32[]{:S(2)}) async-start(f32[32,1,192]{2,1,0:T(1,128)} %all_to_all.14), calls=%async_computation.1 | async-start | bytes 65536 | tf_op jit(solution)/shard_map/all_to_all | solution.py:367
  (99 other events, 579.6 us)

commit v2 on v1

--- a/solution.py
+++ b/solution.py
@@ -1,9 +1,12 @@
+import functools
 import math
 
 import jax
 import jax.numpy as jnp
 import numpy as np
 from jax import lax
+from jax.experimental import pallas as pl
+from jax.experimental.pallas import tpu as pltpu
 from jax.sharding import PartitionSpec as P
 
 HD = 64
@@ -61,86 +64,291 @@
     return jnp.cos(angles), jnp.sin(angles)
 
 
-def rotate(tensor, cosine, sine):
-    half = ROT // 2
-    swapped = jnp.concatenate(
-        [-tensor[:, half:ROT], tensor[:, :half], tensor[:, ROT:]], axis=1
-    )
-    return tensor * cosine + swapped * sine
-
-
-def mlp_half(normed, cot, slots, key, up_shift):
-    blocks = xor_order(slots, key)
-    up = jnp.concatenate([unpack_up(b[:256]) for b in blocks], axis=0)
-    down = jnp.concatenate([b[256:] for b in blocks], axis=1)
-    hidden = dot(normed, up) + up_shift[None, :]
-    cdf = 0.5 * (1.0 + lax.erf(hidden * math.sqrt(0.5)))
-    active = (hidden * cdf).astype(BF)
-    slope = cdf + hidden * jnp.exp(-0.5 * hidden * hidden) * (1.0 / math.sqrt(2 * math.pi))
-    out = dot(active, down)
-    d_hidden = (dot(cot, down, ((1,), (1,))) * slope).astype(BF)
-    down_grad = dot(active, cot, ((0,), (0,)))
-    up_grad = dot(normed, d_hidden, ((0,), (0,)))
-    up_shift_grad = jnp.sum(d_hidden.astype(F32), axis=0)
-    d_second = dot(d_hidden, up, ((1,), (1,)))
-    grads = jnp.stack(
-        [
-            jnp.concatenate(
-                [pack_up(up_grad[128 * g : 128 * g + 128]), down_grad[:, 128 * g : 128 * g + 128]],
-                axis=0,
-            )
-            for g in range(4)
-        ]
-    )
-    return out, d_second, jnp.stack(xor_order(grads, key)), up_shift_grad
-
-
-def att_head(normed, cot, slots, key, shift, cosine, sine, starts):
-    blocks = xor_order(slots, key)
-    project = jnp.concatenate([unpack_project(b[:192]) for b in blocks], axis=0)
-    mix = jnp.concatenate([b[192:] for b in blocks], axis=1)
-    cosine, sine = cosine[:, :HD], sine[:, :HD]
-    projected = dot(normed, project) + shift[None, :]
-    q = rotate(projected[:, :HD], cosine, sine).astype(BF)
-    k = rotate(projected[:, HD : 2 * HD], cosine, sine).astype(BF)
-    v = projected[:, 2 * HD :].astype(BF)
+VMEM_LIMIT = 50 * 1024 * 1024
+
+
+def roll(value, shift):
+    return pltpu.roll(value, shift, 1)
+
+
+def lanes_of(shape):
+    return lax.broadcasted_iota(jnp.int32, shape, 1)
+
+
+def mlp_kernel(
+    where_ref,
+    x_ref,
+    cot_ref,
+    across_ref,
+    far_ref,
+    own_ref,
+    oth_ref,
+    norms_ref,
+    shift_ref,
+    n1_ref,
+    xhat_ref,
+    call_ref,
+    out_ref,
+    e_ref,
+    send_ref,
+    keep_ref,
+    small_ref,
+    up_s,
+    down_s,
+    n2_s,
+    act_s,
+    dh_s,
+    ug_s,
+    dg_s,
+):
+    r, key = where_ref[0], where_ref[1]
+    count = x_ref.shape[0]
+    gains = norms_ref[...]
+    sources = (
+        (x_ref, cot_ref),
+        (far_ref.at[0, 0], far_ref.at[0, 1]),
+        (across_ref.at[0], across_ref.at[1]),
+        (far_ref.at[1, 0], far_ref.at[1, 1]),
+    )
+    for j, (rows_in, grad_in) in enumerate(sources):
+        at = pl.ds(pl.multiple_of((r ^ j) * count, count), count)
+        hat, unused = normalize(rows_in[...].astype(F32))
+        xhat_ref[at, :] = hat.astype(BF)
+        n1_ref[at, :] = (hat * gains[0:1] + gains[1:2]).astype(BF)
+        n2_s[at, :] = (hat * gains[2:3] + gains[3:4]).astype(BF)
+        call_ref[at, :] = grad_in[...]
+    for k in range(4):
+        g = pl.multiple_of((key ^ k) * 128, 128)
+        for h, ref in enumerate((own_ref, oth_ref)):
+            up_s[pl.ds(g, 128), h * 256 : h * 256 + 128] = ref[k, 0:128]
+            up_s[pl.ds(g, 128), h * 256 + 128 : h * 256 + 256] = ref[k, 128:256]
+            down_s[h * 256 : h * 256 + 256, pl.ds(g, 128)] = ref[k, 256:512]
+    up, down = up_s[...], down_s[...]
+    shift = shift_ref[...]
+    sums = [jnp.zeros((1, up.shape[1]), F32)] * 3
+    for t in range(4):
+        at = slice(t * count, t * count + count)
+        hidden = dot(n2_s[at, :], up) + shift
+        cdf = 0.5 + 0.5 * lax.erf(hidden * math.sqrt(0.5))
+        active = (hidden * cdf).astype(BF)
+        slope = cdf + hidden * jnp.exp(-0.5 * hidden * hidden) * (1.0 / math.sqrt(2 * math.pi))
+        act_s[at, :] = active
+        out_ref[at, :] = dot(active, down)
+        d_hidden = (dot(call_ref[at, :], down, ((1,), (1,))) * slope).astype(BF)
+        dh_s[at, :] = d_hidden
+        d_second = dot(d_hidden, up, ((1,), (1,)))
+        e_ref[at, :] = d_second * gains[2:3]
+        sums[0] += jnp.sum(d_hidden.astype(F32), axis=0, keepdims=True)
+        sums[1] += jnp.sum(d_second * xhat_ref[at, :].astype(F32), axis=0, keepdims=True)
+        sums[2] += jnp.sum(d_second, axis=0, keepdims=True)
+    sums.append(jnp.sum(cot_ref[...].astype(F32), axis=0, keepdims=True))
+    for i, row in enumerate(sums):
+        small_ref[i : i + 1, :] = row
+    small_ref[4:8, :] = jnp.zeros((4, small_ref.shape[1]), F32)
+    ug_s[...] = dot(n2_s[...], dh_s[...], ((0,), (0,)))
+    dg_s[...] = dot(act_s[...], call_ref[...], ((0,), (0,)))
+    for k in range(4):
+        g = pl.multiple_of((key ^ k) * 128, 128)
+        for h, ref in enumerate((keep_ref, send_ref)):
+            ref[k, 0:128] = ug_s[pl.ds(g, 128), h * 256 : h * 256 + 128].astype(ref.dtype)
+            ref[k, 128:256] = ug_s[pl.ds(g, 128), h * 256 + 128 : h * 256 + 256].astype(ref.dtype)
+            ref[k, 256:512] = dg_s[h * 256 : h * 256 + 256, pl.ds(g, 128)].astype(ref.dtype)
+
+
+def run_mlp(where, x, cot, across, far, own, oth, norms, shift):
+    count, width = x.shape
+    tall = 4 * count
+    wide = shift.shape[1]
+    shape = jax.ShapeDtypeStruct
+    return pl.pallas_call(
+        mlp_kernel,
+        out_shape=(
+            shape((tall, width), BF),
+            shape((tall, width), BF),
+            shape((tall, width), BF),
+            shape((tall, width), F32),
+            shape((tall, width), F32),
+            shape(own.shape, BF),
+            shape(own.shape, F32),
+            shape((8, wide), F32),
+        ),
+        in_specs=[pl.BlockSpec(memory_space=pltpu.SMEM)]
+        + [pl.BlockSpec(memory_space=pltpu.VMEM)] * 8,
+        out_specs=[pl.BlockSpec(memory_space=pltpu.VMEM)] * 8,
+        scratch_shapes=[
+            pltpu.VMEM((width, wide), BF),
+            pltpu.VMEM((wide, width), BF),
+            pltpu.VMEM((tall, width), BF),
+            pltpu.VMEM((tall, wide), BF),
+            pltpu.VMEM((tall, wide), BF),
+            pltpu.VMEM((width, wide), F32),
+            pltpu.VMEM((wide, width), F32),
+        ],
+        compiler_params=pltpu.CompilerParams(vmem_limit_bytes=VMEM_LIMIT),
+        cost_estimate=pl.CostEstimate(
+            flops=12 * tall * width * wide, bytes_accessed=20 * tall * width, transcendentals=0
+        ),
+        name="feed_forward",
+    )(where, x, cot, across, far, own, oth, norms, shift)
+
+
+def att_kernel(
+    last,
+    where_ref,
+    n1_ref,
+    xhat_ref,
+    cot_ref,
+    slots_ref,
+    shift_ref,
+    cos_ref,
+    sin_ref,
+    starts_ref,
+    norms_ref,
+    out_in,
+    e_in,
+    *refs,
+):
+    if last:
+        near_ref, rest_ref, grads_ref, small_ref = refs[:4]
+    else:
+        out_ref, e_ref, grads_ref, small_ref = refs[:4]
+    w_s, mix_s, q_s, qh_s, k_s, v_s, ctx_s, dctx_s, dq_s, dt_s, dp_s, pg_s, mg_s, out_s, e_s = refs[4:]
+    r, key = where_ref[0], where_ref[1]
+    tall = n1_ref.shape[0]
+    count = tall // 4
     scaling = HD**-0.5
-    count = q.shape[0]
-    place = jnp.arange(count, dtype=jnp.int32)
-    allowed = (place[None, :] >= starts[:, None]) & (place[:, None] >= place[None, :])
-    scores = jnp.where(allowed, dot(q, k, ((1,), (1,))) * scaling, MASKED)
-    exponent = jnp.exp(scores - jnp.max(scores, axis=-1, keepdims=True))
-    probability = exponent / jnp.sum(exponent, axis=-1, keepdims=True)
-    prob_low = probability.astype(BF)
-    context = dot(prob_low, v).astype(BF)
-    out = dot(context, mix)
-    mix_grad = dot(context, cot, ((0,), (0,)))
-    d_context = dot(cot, mix, ((1,), (1,))).astype(BF)
-    d_prob = dot(d_context, v, ((1,), (1,)))
-    d_scores = probability * (d_prob - jnp.sum(d_prob * probability, axis=-1, keepdims=True))
-    d_scores = d_scores.astype(BF)
-    d_q = dot(d_scores, k) * scaling
-    d_k = dot(d_scores, q, ((0,), (0,))) * scaling
-    d_v = dot(prob_low, d_context, ((0,), (0,)))
-    d_projected = jnp.concatenate(
-        [rotate(d_q, cosine, -sine), rotate(d_k, cosine, -sine), d_v], axis=1
-    ).astype(BF)
-    project_grad = dot(normed, d_projected, ((0,), (0,)))
-    shift_grad = jnp.sum(d_projected.astype(F32), axis=0)
-    d_first = dot(d_projected, project, ((1,), (1,)))
-    grads = jnp.stack(
-        [
-            jnp.concatenate(
-                [
-                    pack_project(project_grad[128 * g : 128 * g + 128]),
-                    mix_grad[:, 128 * g : 128 * g + 128],
-                ],
-                axis=0,
-            )
-            for g in range(4)
-        ]
-    )
-    return out, d_first, jnp.stack(xor_order(grads, key)), shift_grad
+    mix_s[64:128, :] = jnp.zeros((64, mix_s.shape[1]), BF)
+    low = lanes_of((64, 128)) < 64
+    for k in range(4):
+        g = pl.multiple_of((key ^ k) * 128, 128)
+        w_s[pl.ds(g, 128), 0:128] = slots_ref[k, 0:128]
+        rest = slots_ref[k, 128:192].astype(F32)
+        w_s[pl.ds(g, 64), 128:256] = jnp.where(low, rest, 0.0).astype(BF)
+        w_s[pl.ds(g + 64, 64), 128:256] = jnp.where(low, roll(rest, 64), 0.0).astype(BF)
+        mix_s[0:64, pl.ds(g, 128)] = slots_ref[k, 192:256]
+    w, mix = w_s[...], mix_s[...]
+    shift = shift_ref[...]
+    lane = lanes_of((count, 128))
+    left = lane < 64
+    first, second = lane % 64 < ROT // 2, lane % 64 < ROT
+    for t in range(4):
+        at = slice(t * count, t * count + count)
+        projected = dot(n1_ref[at, :], w) + shift
+        qk = projected[:, :128]
+        sine = sin_ref[at, :]
+        minus = jnp.where(first, -sine, 0.0)
+        plus = jnp.where(first, 0.0, jnp.where(second, sine, 0.0))
+        qk = qk * cos_ref[at, :] + roll(qk, 120) * minus + roll(qk, 8) * plus
+        turned = roll(qk, 64)
+        q_s[at, :] = jnp.where(left, qk, 0.0).astype(BF)
+        k_s[at, :] = jnp.where(left, turned, 0.0).astype(BF)
+        qh_s[at, :] = jnp.where(left, 0.0, turned).astype(BF)
+        v_s[at, :] = projected[:, 128:].astype(BF)
+        dctx_s[at, :] = dot(cot_ref[at, :], mix, ((1,), (1,))).astype(BF)
+    dt_s[...] = jnp.zeros(dt_s.shape, F32)
+    for t in range(4):
+        at = slice(t * count, t * count + count)
+        keys = (t + 1) * count
+        q, d_context = q_s[at, :], dctx_s[at, :]
+        kk, vv = k_s[0:keys, :], v_s[0:keys, :]
+        scores = dot(q, kk, ((1,), (1,))) * scaling
+        place = lax.broadcasted_iota(jnp.int32, (count, keys), 1)
+        row = lax.broadcasted_iota(jnp.int32, (count, 1), 0) + t * count
+        allowed = (place >= starts_ref[at, :]) & (place <= row)
+        scores = jnp.where(allowed, scores, MASKED)
+        exponent = jnp.exp(scores - jnp.max(scores, axis=-1, keepdims=True))
+        probability = exponent * (1.0 / jnp.sum(exponent, axis=-1, keepdims=True))
+        prob_low = probability.astype(BF)
+        ctx_s[at, :] = dot(prob_low, vv).astype(BF)
+        d_prob = dot(d_context, vv, ((1,), (1,)))
+        weight = jnp.sum(d_prob * probability, axis=-1, keepdims=True)
+        d_scores = (probability * (d_prob - weight)).astype(BF)
+        dq_s[at, :] = dot(d_scores, kk)
+        dt_s[0:128, 0:keys] += dot(qh_s[at, :], d_scores, ((0,), (0,)))
+        dt_s[128:256, 0:keys] += dot(d_context, prob_low, ((0,), (0,)))
+    sums = [jnp.zeros((1, n1_ref.shape[1]), F32)] * 2
+    shift_sum = jnp.zeros((1, 256), F32)
+    gain = norms_ref[0:1, :]
+    for t in range(4):
+        at = slice(t * count, t * count + count)
+        turned = jnp.transpose(dt_s[:, at])
+        qk = (dq_s[at, :] + turned[:, :128]) * scaling
+        sine = sin_ref[at, :]
+        minus = jnp.where(first, sine, 0.0)
+        plus = jnp.where(first, 0.0, jnp.where(second, -sine, 0.0))
+        qk = qk * cos_ref[at, :] + roll(qk, 120) * minus + roll(qk, 8) * plus
+        dp_s[at, 0:128] = qk.astype(BF)
+        dp_s[at, 128:256] = turned[:, 128:].astype(BF)
+        d_projected = dp_s[at, :]
+        shift_sum += jnp.sum(d_projected.astype(F32), axis=0, keepdims=True)
+        d_first = dot(d_projected, w, ((1,), (1,)))
+        sums[0] += jnp.sum(d_first * xhat_ref[at, :].astype(F32), axis=0, keepdims=True)
+        sums[1] += jnp.sum(d_first, axis=0, keepdims=True)
+        e = e_in[at, :] + d_first * gain
+        out = out_in[at, :] + dot(ctx_s[at, :], mix)
+        if last:
+            out_s[at, :] = out
+            e_s[at, :] = e
+        else:
+            out_ref[at, :] = out
+            e_ref[at, :] = e
+    small_ref[...] = jnp.zeros(small_ref.shape, F32)
+    small_ref[0:1, :] = sums[0]
+    small_ref[1:2, :] = sums[1]
+    small_ref[2:3, 0:256] = shift_sum
+    pg_s[...] = dot(n1_ref[...], dp_s[...], ((0,), (0,)))
+    mg_s[...] = dot(ctx_s[...], cot_ref[...], ((0,), (0,)))
+    for k in range(4):
+        g = pl.multiple_of((key ^ k) * 128, 128)
+        grads_ref[k, 0:128] = pg_s[pl.ds(g, 128), 0:128].astype(grads_ref.dtype)
+        top, bottom = pg_s[pl.ds(g, 64), 128:256], pg_s[pl.ds(g + 64, 64), 128:256]
+        grads_ref[k, 128:192] = jnp.where(low, top, roll(bottom, 64)).astype(grads_ref.dtype)
+        grads_ref[k, 192:256] = mg_s[0:64, pl.ds(g, 128)].astype(grads_ref.dtype)
+    if last:
+        for j in range(4):
+            at = pl.ds(pl.multiple_of((r ^ j) * count, count), count)
+            target = near_ref if j % 2 else rest_ref
+            target[j // 2, 0] = out_s[at, :].astype(target.dtype)
+            target[j // 2, 1] = e_s[at, :].astype(target.dtype)
+
+
+def run_att(last, where, n1, xhat, cot, slots, shift, cosine, sine, starts, norms, out, e):
+    tall, width = n1.shape
+    count = tall // 4
+    shape = jax.ShapeDtypeStruct
+    if last:
+        results = (shape((2, 2, count, width), BF), shape((2, 2, count, width), F32))
+    else:
+        results = (shape(out.shape, F32), shape(e.shape, F32))
+    return pl.pallas_call(
+        functools.partial(att_kernel, last),
+        out_shape=results + (shape(slots.shape, F32 if last else BF), shape((8, width), F32)),
+        in_specs=[pl.BlockSpec(memory_space=pltpu.SMEM)]
+        + [pl.BlockSpec(memory_space=pltpu.VMEM)] * 11,
+        out_specs=[pl.BlockSpec(memory_space=pltpu.VMEM)] * 4,
+        scratch_shapes=[
+            pltpu.VMEM((width, 256), BF),
+            pltpu.VMEM((128, width), BF),
+            pltpu.VMEM((tall, 128), BF),
+            pltpu.VMEM((tall, 128), BF),
+            pltpu.VMEM((tall, 128), BF),
+            pltpu.VMEM((tall, 128), BF),
+            pltpu.VMEM((tall, 128), BF),
+            pltpu.VMEM((tall, 128), BF),
+            pltpu.VMEM((tall, 128), F32),
+            pltpu.VMEM((256, tall), F32),
+            pltpu.VMEM((tall, 256), BF),
+            pltpu.VMEM((width, 256), F32),
+            pltpu.VMEM((128, width), F32),
+            pltpu.VMEM((tall, width) if last else (8, 128), F32),
+            pltpu.VMEM((tall, width) if last else (8, 128), F32),
+        ],
+        compiler_params=pltpu.CompilerParams(vmem_limit_bytes=VMEM_LIMIT),
+        cost_estimate=pl.CostEstimate(
+            flops=24 * tall * width * 128, bytes_accessed=24 * tall * width, transcendentals=0
+        ),
+        name="attention_last" if last else "attention_first",
+    )(where, n1, xhat, cot, slots, shift, cosine, sine, starts, norms, out, e)
 
 
 def on_device(
@@ -225,13 +433,10 @@
         whole = halves.transpose(1, 0, 2, 3).reshape(rows, per, -1, wide)
         return deliver(whole.transpose(1, 0, 2, 3))
 
-    act = jnp.stack([inputs[0], cotangent[0]])
-    act_two = jnp.stack([act, flip(act, 2)])
-    act_far = flip(act_two, 1)
-    act_all = jnp.stack([act_two[0], act_far[0], act_two[1], act_far[1]])
-    act_all = jnp.stack(xor_order(act_all, r), axis=1)
-    x_all = act_all[0].reshape(-1, width)
-    cot_all = act_all[1].reshape(-1, width)
+    x_own, cot_own = inputs[0], cotangent[0]
+    act = jnp.stack([x_own, cot_own])
+    across = flip(act, 2)
+    far = flip(jnp.stack([act, across]), 1)
 
     if paired:
         key, y = c // per, c % per
@@ -291,29 +496,28 @@
     starts = (segs[:, :count] * 32 + segs[:, count:]).reshape(-1)
     cosine, sine = rotary_tables(jnp.arange(rows * count, dtype=jnp.int32) - starts)
 
-    xhat, root = normalize(x_all.astype(F32))
-    normed_one = (xhat * norms[0] + norms[1]).astype(BF)
-    normed_two = (xhat * norms[2] + norms[3]).astype(BF)
-
-    out_oth, d2_oth, mlp_send, ub_oth = mlp_half(normed_two, cot_all, mlp_slots[1], key, up_shift[1])
-    out_own, d2_own, mlp_keep, ub_own = mlp_half(normed_two, cot_all, mlp_slots[0], key, up_shift[0])
-    out_a, d1_oth, att_send, pb_oth = att_head(
-        normed_one, cot_all, att_slots[1], key, project_shift[1], cosine, sine, starts
-    )
-    out_b, d1_own, att_keep, pb_own = att_head(
-        normed_one, cot_all, att_slots[0], key, project_shift[0], cosine, sine, starts
-    )
-    d_first, d_second = d1_oth + d1_own, d2_oth + d2_own
-    out_part = out_oth + out_own + out_a + out_b
-    e_part = d_first * norms[0] + d_second * norms[2]
+    where = jnp.stack([r, key]).astype(jnp.int32)
+    n1, xhat, cot_all, out, e, mlp_send, mlp_keep, mlp_small = run_mlp(
+        where, x_own, cot_own, across, far, mlp_slots[0], mlp_slots[1], norms, up_shift.reshape(1, -1)
+    )
+    project_shift = jnp.pad(project_shift, ((0, 0), (0, HD)))
+    shared = (cosine, sine, starts[:, None], norms)
+    out, e, att_send, small_oth = run_att(
+        False, where, n1, xhat, cot_all, att_slots[1], project_shift[1:], *shared, out, e
+    )
+    near, rest, att_keep, small_own = run_att(
+        True, where, n1, xhat, cot_all, att_slots[0], project_shift[:1], *shared, out, e
+    )
+    ub_own, ub_oth = mlp_small[0, : up_shift.shape[1]], mlp_small[0, up_shift.shape[1] :]
+    pb_own, pb_oth = small_own[2, : 3 * HD], small_oth[2, : 3 * HD]
 
     if paired:
-        mlp_done = collect((mlp_keep + bring_other(mlp_send.astype(BF)).astype(F32)).astype(BF))
-        att_done = collect((att_keep + bring_other(att_send.astype(BF)).astype(F32)).astype(BF))
+        mlp_done = collect((mlp_keep + bring_other(mlp_send).astype(F32)).astype(BF))
+        att_done = collect((att_keep + bring_other(att_send).astype(F32)).astype(BF))
         project_done, mix_done = unpack_project(att_done[:192]), att_done[192:]
         up_done, down_done = unpack_up(mlp_done[:256]), mlp_done[256:]
     else:
-        att_grads, mlp_grads = jnp.stack([att_keep, att_send]), jnp.stack([mlp_keep, mlp_send])
+        att_grads, mlp_grads = jnp.stack([att_keep, att_send.astype(F32)]), jnp.stack([mlp_keep, mlp_send.astype(F32)])
         every_pair = [(h, g) for h in range(2) for g in range(rows)]
 
         def regroup(parts):
@@ -328,13 +532,9 @@
         )
         down_done = deliver_rows(regroup([mlp_grads[h, g][256:] for h, g in every_pair]))
 
-    oe = jnp.stack([out_part, e_part]).reshape(2, rows, count, width)
-    chunk = [lax.dynamic_index_in_dim(oe, r ^ j, axis=1, keepdims=False) for j in range(4)]
-    near = flip(jnp.stack([chunk[1], chunk[3]]).astype(BF), 1).astype(F32)
-    mine_sum, far_sum = chunk[0] + near[0], chunk[2] + near[1]
-    total = mine_sum + flip(far_sum.astype(BF), 2).astype(F32)
-    x_own = inputs[0].astype(F32)
-    cot_own = cotangent[0].astype(F32)
+    mine = rest + flip(near, 1).astype(F32)
+    total = mine[0] + flip(mine[1].astype(BF), 2).astype(F32)
+    x_own, cot_own = x_own.astype(F32), cot_own.astype(F32)
     output = (x_own + total[0] + norms[4] + norms[5]).astype(BF)[None]
     e_all = total[1]
     xhat_own, root_own = normalize(x_own)
@@ -344,15 +544,7 @@
         - xhat_own * jnp.mean(e_all * xhat_own, axis=-1, keepdims=True)
     )
 
-    everywhere = jnp.stack(
-        [
-            jnp.sum(d_first * xhat, axis=0),
-            jnp.sum(d_first, axis=0),
-            jnp.sum(d_second * xhat, axis=0),
-            jnp.sum(d_second, axis=0),
-            jnp.sum(cot_own, axis=0),
-        ]
-    )
+    everywhere = jnp.concatenate([small_own[:2] + small_oth[:2], mlp_small[1:4]])
     everywhere = everywhere.reshape(5, rows * cols, part).transpose(1, 0, 2).reshape(rows * cols, -1)
 
     def by_half(own, other):

time: 212 us -> 175 us (0.83)
  matrix products: 36.7 us -> 0 us
  Pallas kernels: 0 us -> 31.6 us
  other arithmetic: 32.4 us -> 13.8 us
  local copies, waits for them, and re-layouts: 38.1 us -> 21.3 us
  waiting for transfers between devices: 49.1 us -> 58.5 us
  starting transfers between devices: 51.6 us -> 48.3 us
    dot_general x36 -> x0, matrix products: 36.7 us -> none  [dot(): return lax.dot_general(a, b, (dims, ((), ())), preferred_element_type=F32)]
    pallas_call x0 -> x3, Pallas kernels: none -> 31.6 us  [the longest x2 22.7 us: run_att(): pl.pallas_call(functools.partial(att_kernel, last), out_shape=results + (...]
    another operation x24 -> x2, other arithmetic: 9.83 us -> 1.18 us  [the longest x1 1.1 us: on_device(): far = flip(jnp.stack([act, across]), 1)]
    ppermute x4, waiting for transfers between devices: 8.94 us -> 17.3 us  [flip(): return lax.ppermute(value, 'row', [(i, i ^ bit) for i in range(rows)])]
    convert_element_type x9 -> x2, other arithmetic: 8.79 us -> 1.67 us  [the longest x1 1.61 us: on_device(): (mlp_keep + bring_other(mlp_send).astype(F32)).astype(BF)]
    ppermute x8, starting transfers between devices: 13.1 us -> 18.9 us  [spread(): lax.ppermute(block, both, [(i, home(i, k)) for i in everyone])]
    slice x23 -> x3, local copies, waits for them, and re-layouts: 3.37 us -> 0.01 us  [the longest x1 0.01 us: on_device(): project_shift[1:]]
    ppermute x8, starting transfers between devices: 14.1 us -> 10.8 us  [collect(): lax.ppermute(grads[k], both, [(home(i, k), i) for i in everyone])]
  transfers between devices with their start and end apart: 26 -> 26, of which waited for: 7 -> 6; matrix products, arithmetic and copies ran while one was open for 21% -> 15% of each run, Pallas kernels for 0% -> 5%
where the time goes in v2:
time: 175 us
  waiting for transfers between devices  58.5 us (33%)
  starting transfers between devices  48.3 us (28%)
  Pallas kernels  31.6 us (18%)
  local copies, waits for them, and re-layouts  21.3 us (12%)
  other arithmetic  13.8 us (8%)
    pallas_call x2, Pallas kernels, run_att(): pl.pallas_call(functools.partial(att_kernel, last), out_shape=results + (...  22.7 us
    ppermute x8, waiting for transfers between devices, collect(): lax.ppermute(grads[k], both, [(home(i, k), i) for i in everyone])  20.8 us
    ppermute x8, starting transfers between devices, spread(): lax.ppermute(block, both, [(i, home(i, k)) for i in everyone])  18.9 us
    ppermute x4, waiting for transfers between devices, flip(): return lax.ppermute(value, 'row', [(i, i ^ bit) for i in range(rows)])  17.3 us
    ppermute x2, waiting for transfers between devices, spread(): return (own, lax.ppermute(own, 'col', [(i, i ^ 1) for i in range(cols)]))  15.3 us
    ppermute x8, starting transfers between devices, collect(): lax.ppermute(grads[k], both, [(home(i, k), i) for i in everyone])  10.8 us
    pallas_call x1, Pallas kernels, run_mlp(): pl.pallas_call(mlp_kernel, out_shape=(shape((tall, width), BF), shape((ta...  8.93 us
    unnamed x37, local copies, waits for them, and re-layouts  7.21 us
  transfers between devices with their start and end apart: 26, of which 6 were waited for; matrix products, arithmetic and copies ran while one was open for 15% of the time, Pallas kernels for 5%

profile of v2, /device:TPU:0, one launch (start us, length us, event | category | flops | bytes accessed | tf_op | source)
XLA Modules:
  0.0 174.6 jit_solution(4738071100430943798)
XLA Ops:
  4.1 4.3 %collective-permute-start.8 = (bf16[256,128]{1,0:T(8,128)(2,1)S(1)}, bf16[256,128]{1,0:T(8,128)(2,1)S(1)}, u32[]{:S(2)}, u32[]{:S(2)}) collective-permute-start(bf16[256,128]{1,0:T(8,128)(2,1)S(1)} %pad_maximum_fusion.5), channel_id=1, source_target_pairs={{0,2},{1,3},{2,10},{3,11},{4,18},{5,19},{6,26},{7,27},{8,0},{9,1},... | collective-permute-start | bytes 196616 | tf_op jit(solution)/shard_map/ppermute | solution.py:390
  8.4 3.4 %collective-permute-start.9 = (bf16[256,128]{1,0:T(8,128)(2,1)S(1)}, bf16[256,128]{1,0:T(8,128)(2,1)S(1)}, u32[]{:S(2)}, u32[]{:S(2)}) collective-permute-start(bf16[256,128]{1,0:T(8,128)(2,1)S(1)} %pad_maximum_fusion.5), channel_id=1, source_target_pairs={{0,4},{1,5},{2,12},{3,13},{4,20},{5,21},{6,28},{7,29},{8,6},{9,7},... | collective-permute-start | bytes 196616 | tf_op jit(solution)/shard_map/ppermute | solution.py:390
  11.8 1.7 collective-permute-start.10
  14.2 5.4 %concatenate.39 = bf16[720]{0:T(1024)(128)(2,1)S(1)} concatenate(bf16[16]{0:T(256)(128)(2,1)} %param.27, bf16[16]{0:T(256)(128)(2,1)} %param.28, bf16[16]{0:T(256)(128)(2,1)} %param.29, bf16[16]{0:T(256)(128)(2,1)} %param.30, bf16[16]{0:T(256)(128)(2,1)} %param.22, bf16[16]{0:T(256)(128)(2,1)} %param.26, bf16[48]{0:T(256)(128)(2,1)} %param.20, bf16[64]{0:T(256)(128)(2,1)} %param.24, ...), dimensions={0} | concatenate | bytes 2880 | tf_op jit(solution)/shard_map/concatenate | solution.py:466
  21.8 4.2 %all-to-all-start = ((bf16[32,2,360]{2,1,0:T(2,128)(2,1)}), bf16[32,2,360]{2,1,0:T(2,128)(2,1)S(1)}, u32[]{:S(2)}, u32[]{:S(2)}) async-start(bf16[32,2,360]{2,1,0:T(2,128)(2,1)} %reshape.206), calls=%async_computation | async-start | bytes 98304 | tf_op jit(solution)/shard_map/all_to_all | solution.py:480
  30.8 3.1 %collective-permute-start.3 = (bf16[512,128]{1,0:T(8,128)(2,1)S(1)}, bf16[512,128]{1,0:T(8,128)(2,1)S(1)}, u32[]{:S(2)}, u32[]{:S(2)}) collective-permute-start(bf16[512,128]{1,0:T(8,128)(2,1)S(1)} %pad_maximum_fusion.3), channel_id=1, source_target_pairs={{0,2},{1,3},{2,10},{3,11},{4,18},{5,19},{6,26},{7,27},{8,0},{9,1},... | collective-permute-start | bytes 393224 | tf_op jit(solution)/shard_map/ppermute | solution.py:390
  33.9 3.5 %collective-permute-start.4 = (bf16[512,128]{1,0:T(8,128)(2,1)S(1)}, bf16[512,128]{1,0:T(8,128)(2,1)S(1)}, u32[]{:S(2)}, u32[]{:S(2)}) collective-permute-start(bf16[512,128]{1,0:T(8,128)(2,1)S(1)} %pad_maximum_fusion.3), channel_id=1, source_target_pairs={{0,4},{1,5},{2,12},{3,13},{4,20},{5,21},{6,28},{7,29},{8,6},{9,7},... | collective-permute-start | bytes 393224 | tf_op jit(solution)/shard_map/ppermute | solution.py:390
  37.4 1.6 collective-permute-start.5
  39.1 1.3 collective-permute-start
  41.2 15.2 %collective-permute-done.across_ref = bf16[2,256,512]{2,1,0:T(8,128)(2,1)S(1)} collective-permute-done((bf16[2,256,512]{2,1,0:T(8,128)(2,1)S(1)}, bf16[2,256,512]{2,1,0:T(8,128)(2,1)S(1)}, u32[]{:S(2)}, u32[]{:S(2)}) %collective-permute-start) | collective-permute-done | bytes 524320 | tf_op jit(solution)/shard_map/ppermute | solution.py:379
  57.9 1.6 collective-permute-start.11
  60.7 1.9 %multiply_sine_fusion = (f32[1024,128]{1,0:T(8,128)S(1)}, f32[1024,128]{1,0:T(8,128)S(1)}) fusion(f32[128]{0:T(128)S(1)} %copy-done.9, f32[1024]{0:T(1024)S(1)} %subtract_convert_fusion), kind=kLoop, calls=%fused_computation.6 | loop fusion | flops 131072 | bytes 1053184 | tf_op jit(solution)/shard_map/sin | solution.py:64
  62.6 15.3 %collective-permute-done.6.oth_ref = bf16[4,512,128]{2,1,0:T(8,128)(2,1)S(1)} collective-permute-done((bf16[4,512,128]{2,1,0:T(8,128)(2,1)S(1)}, bf16[4,512,128]{2,1,0:T(8,128)(2,1)S(1)}, u32[]{:S(2)}, u32[]{:S(2)}) %collective-permute-start.6) | collective-permute-done | bytes 524320 | tf_op jit(solution)/shard_map/ppermute | solution.py:393
  79.7 8.9 %feed_forward.1 = (bf16[1024,512]{1,0:T(8,128)(2,1)S(1)}, bf16[1024,512]{1,0:T(8,128)(2,1)}, bf16[1024,512]{1,0:T(8,128)(2,1)}, f32[1024,512]{1,0:T(8,128)}, f32...) custom-call(s32[2]{0:T(128)S(1)} %pad_add_fusion.where_ref, ...), custom_call_target="tpu_custom_call" | custom-call | flops 3221225472 | bytes 10485760 | tf_op jit(solution)/shard_map/feed_forward/pallas_call | solution.py:163
  88.6 11.5 %attention_first.1 = (f32[1024,512]{1,0:T(8,128)}, f32[1024,512]{1,0:T(8,128)}, bf16[4,256,128]{2,1,0:T(8,128)(2,1)S(1)}, f32[8,512]{1,0:T(8,128)S(1)}) custom-call(s32[2]{0:T(128)S(1)} %pad_add_fusion.where_ref, bf16[1024,512]{1,0:T(8,128)(2,1)S(1)} %get-tuple-element.30.n1_ref, bf16[1024,512]{1,0:T(8,128)(2,1)} %get-tuple-element.31.xhat_ref, ...), custom_call_target="tpu_custom_call" | custom-call | flops 1610612736 | bytes 12582912 | tf_op jit(solution)/shard_map/attention_first/pallas_call | solution.py:323
  100.8 11.2 %attention_last.1 = (bf16[2,2,256,512]{3,2,1,0:T(8,128)(2,1)S(1)}, f32[2,2,256,512]{3,2,1,0:T(8,128)}, f32[4,256,128]{2,1,0:T(8,128)S(1)}, f32[8,512]{1,0:T(8,128)S(1)}) custom-call(s32[2]{0:T(128)S(1)} %pad_add_fusion.where_ref, bf16[1024,512]{1,0:T(8,128)(2,1)} %copy-done.1, bf16[1024,512]{1,0:T(8,128)(2,1)} %get-tuple-element.31.xhat_ref, ...), custom_call_target="tpu_custom_call" | custom-call | flops 1610612736 | bytes 12582912 | tf_op jit(solution)/shard_map/attention_last/pallas_call | solution.py:323
  113.7 1.5 collective-permute-start.14
  115.9 2.8 %all-to-all-start.1 = ((f32[32,1,192]{2,1,0:T(1,128)}), f32[32,1,192]{2,1,0:T(1,128)S(1)}, u32[]{:S(2)}, u32[]{:S(2)}) async-start(f32[32,1,192]{2,1,0:T(1,128)} %all_to_all.14), calls=%async_computation.1 | async-start | bytes 65536 | tf_op jit(solution)/shard_map/all_to_all | solution.py:559
  119.0 1.8 %collective-permute-start.19 = (bf16[4,512,128]{2,1,0:T(8,128)(2,1)S(1)}, bf16[4,512,128]{2,1,0:T(8,128)(2,1)}, u32[]{:S(2)}, u32[]{:S(2)}) collective-permute-start(bf16[4,512,128]{2,1,0:T(8,128)(2,1)S(1)} %get-tuple-element.45), channel_id=1, source_target_pairs={{0,1},{1,0},{2,3},{3,2},{4,5},{5,4},{6,7},{7,6},{8,9},{9,8},{10,11... | collective-permute-start | bytes 1572872 | tf_op jit(solution)/shard_map/ppermute | solution.py:396
  120.8 5.1 %all-to-all-done.1 = f32[32,1,192]{2,1,0:T(1,128)S(1)} async-done(((f32[32,1,192]{2,1,0:T(1,128)}), f32[32,1,192]{2,1,0:T(1,128)S(1)}, u32[]{:S(2)}, u32[]{:S(2)}) %all-to-all-start.1) | async-done | bytes 24608 | tf_op jit(solution)/shard_map/all_to_all | solution.py:559
  126.7 1.9 %collective-permute-start.16 = (bf16[256,128]{1,0:T(8,128)(2,1)S(1)}, bf16[256,128]{1,0:T(8,128)(2,1)S(1)}, u32[]{:S(2)}, u32[]{:S(2)}) collective-permute-start(bf16[256,128]{1,0:T(8,128)(2,1)S(1)} %get-tuple-element.117), channel_id=1, source_target_pairs={{2,0},{3,1},{10,2},{11,3},{18,4},{19,5},{26,6},{27,7},{0,8},{1,9},... | collective-permute-start | bytes 196616 | tf_op jit(solution)/shard_map/ppermute | solution.py:400
  128.6 2.6 %collective-permute-start.17 = (bf16[256,128]{1,0:T(8,128)(2,1)S(1)}, bf16[256,128]{1,0:T(8,128)(2,1)S(1)}, u32[]{:S(2)}, u32[]{:S(2)}) collective-permute-start(bf16[256,128]{1,0:T(8,128)(2,1)S(1)} %get-tuple-element.116), channel_id=1, source_target_pairs={{4,0},{5,1},{12,2},{13,3},{20,4},{21,5},{28,6},{29,7},{6,8},{7,9},... | collective-permute-start | bytes 196616 | tf_op jit(solution)/shard_map/ppermute | solution.py:400
  133.3 1.3 collective-permute-start.12
  134.6 6.9 %collective-permute-done.17 = bf16[256,128]{1,0:T(8,128)(2,1)S(1)} collective-permute-done((bf16[256,128]{1,0:T(8,128)(2,1)S(1)}, bf16[256,128]{1,0:T(8,128)(2,1)S(1)}, u32[]{:S(2)}, u32[]{:S(2)}) %collective-permute-start.17) | collective-permute-done | bytes 65568 | tf_op jit(solution)/shard_map/ppermute | solution.py:400
  143.0 1.6 add_convert_fusion
  145.4 1.8 %collective-permute-start.21 = (bf16[512,128]{1,0:T(8,128)(2,1)S(1)}, bf16[512,128]{1,0:T(8,128)(2,1)S(1)}, u32[]{:S(2)}, u32[]{:S(2)}) collective-permute-start(bf16[512,128]{1,0:T(8,128)(2,1)S(1)} %get-tuple-element.111), channel_id=1, source_target_pairs={{2,0},{3,1},{10,2},{11,3},{18,4},{19,5},{26,6},{27,7},{0,8},{1,9},... | collective-permute-start | bytes 393224 | tf_op jit(solution)/shard_map/ppermute | solution.py:400
  147.2 2.2 %collective-permute-start.22 = (bf16[512,128]{1,0:T(8,128)(2,1)S(1)}, bf16[512,128]{1,0:T(8,128)(2,1)S(1)}, u32[]{:S(2)}, u32[]{:S(2)}) collective-permute-start(bf16[512,128]{1,0:T(8,128)(2,1)S(1)} %get-tuple-element.110), channel_id=1, source_target_pairs={{4,0},{5,1},{12,2},{13,3},{20,4},{21,5},{28,6},{29,7},{6,8},{7,9},... | collective-permute-start | bytes 393224 | tf_op jit(solution)/shard_map/ppermute | solution.py:400
  150.0 1.6 convert_add_fusion
  151.6 3.5 %collective-permute-start.13 = (bf16[2,256,512]{2,1,0:T(8,128)(2,1)S(1)}, bf16[2,256,512]{2,1,0:T(8,128)(2,1)S(1)}, u32[]{:S(2)}, u32[]{:S(2)}) collective-permute-start(bf16[2,256,512]{2,1,0:T(8,128)(2,1)S(1)} %fusion.14), channel_id=1, source_target_pairs={{0,16},{8,24},{16,0},{24,8},{1,17},{9,25},{17,1},{25,9},{2,18},{10... | collective-permute-start | bytes 1572872 | tf_op jit(solution)/shard_map/ppermute | solution.py:379
  155.1 13.8 %collective-permute-done.22 = bf16[512,128]{1,0:T(8,128)(2,1)S(1)} collective-permute-done((bf16[512,128]{1,0:T(8,128)(2,1)S(1)}, bf16[512,128]{1,0:T(8,128)(2,1)S(1)}, u32[]{:S(2)}, u32[]{:S(2)}) %collective-permute-start.22) | collective-permute-done | bytes 131104 | tf_op jit(solution)/shard_map/ppermute | solution.py:400
  170.4 2.1 %collective-permute-done.13 = bf16[2,256,512]{2,1,0:T(8,128)(2,1)S(1)} collective-permute-done((bf16[2,256,512]{2,1,0:T(8,128)(2,1)S(1)}, bf16[2,256,512]{2,1,0:T(8,128)(2,1)S(1)}, u32[]{:S(2)}, u32[]{:S(2)}) %collective-permute-start.13) | collective-permute-done | bytes 524320 | tf_op jit(solution)/shard_map/ppermute | solution.py:379
  173.0 1.1 fusion.13
  (145 shorter events, 27.8 us)
Async XLA Ops:
  0.6 29.8 %copy-start = (bf16[1,256,512]{2,1,0:T(8,128)(2,1)S(1)}, bf16[1,256,512]{2,1,0:T(8,128)(2,1)}, u32[]{:S(2)}) copy-start(bf16[1,256,512]{2,1,0:T(8,128)(2,1)} %param.16) | copy-start | bytes 786436
  0.7 30.0 %copy-start.2 = (bf16[1,256,512]{2,1,0:T(8,128)(2,1)S(1)}, bf16[1,256,512]{2,1,0:T(8,128)(2,1)}, u32[]{:S(2)}) copy-start(bf16[1,256,512]{2,1,0:T(8,128)(2,1)} %param.18) | copy-start | bytes 786436
  3.4 27.4 %collective-permute-start.7 = (bf16[256,128]{1,0:T(8,128)(2,1)S(1)}, bf16[256,128]{1,0:T(8,128)(2,1)S(1)}, u32[]{:S(2)}, u32[]{:S(2)}) collective-permute-start(bf16[256,128]{1,0:T(8,128)(2,1)S(1)} %pad_maximum_fusion.5), channel_id=1, source_target_pairs={{0,0},{1,1},{2,8},{3,9},{4,16},{5,17},{6,24},{7,25},{8,2},{9,3},{1... | collective-permute-start | bytes 196616 | tf_op jit(solution)/shard_map/ppermute | solution.py:390
  4.1 29.9 %collective-permute-start.8 = (bf16[256,128]{1,0:T(8,128)(2,1)S(1)}, bf16[256,128]{1,0:T(8,128)(2,1)S(1)}, u32[]{:S(2)}, u32[]{:S(2)}) collective-permute-start(bf16[256,128]{1,0:T(8,128)(2,1)S(1)} %pad_maximum_fusion.5), channel_id=1, source_target_pairs={{0,2},{1,3},{2,10},{3,11},{4,18},{5,19},{6,26},{7,27},{8,0},{9,1},... | collective-permute-start | bytes 196616 | tf_op jit(solution)/shard_map/ppermute | solution.py:390
  8.4 29.0 %collective-permute-start.9 = (bf16[256,128]{1,0:T(8,128)(2,1)S(1)}, bf16[256,128]{1,0:T(8,128)(2,1)S(1)}, u32[]{:S(2)}, u32[]{:S(2)}) collective-permute-start(bf16[256,128]{1,0:T(8,128)(2,1)S(1)} %pad_maximum_fusion.5), channel_id=1, source_target_pairs={{0,4},{1,5},{2,12},{3,13},{4,20},{5,21},{6,28},{7,29},{8,6},{9,7},... | collective-permute-start | bytes 196616 | tf_op jit(solution)/shard_map/ppermute | solution.py:390
  11.8 27.3 %collective-permute-start.10 = (bf16[256,128]{1,0:T(8,128)(2,1)S(1)}, bf16[256,128]{1,0:T(8,128)(2,1)S(1)}, u32[]{:S(2)}, u32[]{:S(2)}) collective-permute-start(bf16[256,128]{1,0:T(8,128)(2,1)S(1)} %pad_maximum_fusion.5), channel_id=1, source_target_pairs={{0,6},{1,7},{2,14},{3,15},{4,22},{5,23},{6,30},{7,31},{8,4},{9,5},... | collective-permute-start | bytes 196616 | tf_op jit(solution)/shard_map/ppermute | solution.py:390
  21.8 18.5 %all-to-all-start = ((bf16[32,2,360]{2,1,0:T(2,128)(2,1)}), bf16[32,2,360]{2,1,0:T(2,128)(2,1)S(1)}, u32[]{:S(2)}, u32[]{:S(2)}) async-start(bf16[32,2,360]{2,1,0:T(2,128)(2,1)} %reshape.206), calls=%async_computation | async-start | bytes 98304 | tf_op jit(solution)/shard_map/all_to_all | solution.py:480
  27.7 30.2 %collective-permute-start.2 = (bf16[512,128]{1,0:T(8,128)(2,1)S(1)}, bf16[512,128]{1,0:T(8,128)(2,1)S(1)}, u32[]{:S(2)}, u32[]{:S(2)}) collective-permute-start(bf16[512,128]{1,0:T(8,128)(2,1)S(1)} %pad_maximum_fusion.3), channel_id=1, source_target_pairs={{0,0},{1,1},{2,8},{3,9},{4,16},{5,17},{6,24},{7,25},{8,2},{9,3},{1... | collective-permute-start | bytes 393224 | tf_op jit(solution)/shard_map/ppermute | solution.py:390
  30.8 28.7 %collective-permute-start.3 = (bf16[512,128]{1,0:T(8,128)(2,1)S(1)}, bf16[512,128]{1,0:T(8,128)(2,1)S(1)}, u32[]{:S(2)}, u32[]{:S(2)}) collective-permute-start(bf16[512,128]{1,0:T(8,128)(2,1)S(1)} %pad_maximum_fusion.3), channel_id=1, source_target_pairs={{0,2},{1,3},{2,10},{3,11},{4,18},{5,19},{6,26},{7,27},{8,0},{9,1},... | collective-permute-start | bytes 393224 | tf_op jit(solution)/shard_map/ppermute | solution.py:390
  33.9 25.6 %collective-permute-start.4 = (bf16[512,128]{1,0:T(8,128)(2,1)S(1)}, bf16[512,128]{1,0:T(8,128)(2,1)S(1)}, u32[]{:S(2)}, u32[]{:S(2)}) collective-permute-start(bf16[512,128]{1,0:T(8,128)(2,1)S(1)} %pad_maximum_fusion.3), channel_id=1, source_target_pairs={{0,4},{1,5},{2,12},{3,13},{4,20},{5,21},{6,28},{7,29},{8,6},{9,7},... | collective-permute-start | bytes 393224 | tf_op jit(solution)/shard_map/ppermute | solution.py:390
  37.4 22.1 %collective-permute-start.5 = (bf16[512,128]{1,0:T(8,128)(2,1)S(1)}, bf16[512,128]{1,0:T(8,128)(2,1)S(1)}, u32[]{:S(2)}, u32[]{:S(2)}) collective-permute-start(bf16[512,128]{1,0:T(8,128)(2,1)S(1)} %pad_maximum_fusion.3), channel_id=1, source_target_pairs={{0,6},{1,7},{2,14},{3,15},{4,22},{5,23},{6,30},{7,31},{8,4},{9,5},... | collective-permute-start | bytes 393224 | tf_op jit(solution)/shard_map/ppermute | solution.py:390
  39.1 17.3 %collective-permute-start = (bf16[2,256,512]{2,1,0:T(8,128)(2,1)S(1)}, bf16[2,256,512]{2,1,0:T(8,128)(2,1)S(1)}, u32[]{:S(2)}, u32[]{:S(2)}) collective-permute-start(bf16[2,256,512]{2,1,0:T(8,128)(2,1)S(1)} %constant_dynamic-update-slice_fusion), channel_id=1, source_target_pairs={{0,16},{8,24},{16,0},{24,8},{1,17},{9,25},{17,1},{25,9},{2,18},{10... | collective-permute-start | bytes 1572872 | tf_op jit(solution)/shard_map/ppermute | solution.py:379
  41.0 19.7 %copy-start.9 = (f32[128]{0:T(128)S(1)}, f32[128]{0:T(128)}, u32[]{:S(2)}) copy-start(f32[128]{0:T(128)} %constant.80.clone) | copy-start | bytes 1540
  57.5 21.2 %collective-permute-start.1 = (bf16[2,2,256,512]{3,2,1,0:T(8,128)(2,1)}, bf16[2,2,256,512]{3,2,1,0:T(8,128)(2,1)}, u32[]{:S(2)}, u32[]{:S(2)}) collective-permute-start(bf16[2,2,256,512]{3,2,1,0:T(8,128)(2,1)} %pad_maximum_fusion), channel_id=1, source_target_pairs={{0,8},{8,0},{16,24},{24,16},{1,9},{9,1},{17,25},{25,17},{2,10},{10... | collective-permute-start | bytes 3145736 | tf_op jit(solution)/shard_map/ppermute | solution.py:379
  57.9 30.7 %collective-permute-start.11 = (bf16[4,256,128]{2,1,0:T(8,128)(2,1)S(1)}, bf16[4,256,128]{2,1,0:T(8,128)(2,1)S(1)}, u32[]{:S(2)}, u32[]{:S(2)}) collective-permute-start(bf16[4,256,128]{2,1,0:T(8,128)(2,1)S(1)} %pad_maximum_fusion.2.slots_ref), channel_id=1, source_target_pairs={{0,1},{1,0},{2,3},{3,2},{4,5},{5,4},{6,7},{7,6},{8,9},{9,8},{10,11... | collective-permute-start | bytes 786440 | tf_op jit(solution)/shard_map/ppermute | solution.py:393
  59.6 18.3 %collective-permute-start.6 = (bf16[4,512,128]{2,1,0:T(8,128)(2,1)S(1)}, bf16[4,512,128]{2,1,0:T(8,128)(2,1)S(1)}, u32[]{:S(2)}, u32[]{:S(2)}) collective-permute-start(bf16[4,512,128]{2,1,0:T(8,128)(2,1)S(1)} %pad_maximum_fusion.1.own_ref), channel_id=1, source_target_pairs={{0,1},{1,0},{2,3},{3,2},{4,5},{5,4},{6,7},{7,6},{8,9},{9,8},{10,11... | collective-permute-start | bytes 1572872 | tf_op jit(solution)/shard_map/ppermute | solution.py:393
  88.6 11.5 %copy-start.1 = (bf16[1024,512]{1,0:T(8,128)(2,1)}, bf16[1024,512]{1,0:T(8,128)(2,1)S(1)}, u32[]{:S(2)}) copy-start(bf16[1024,512]{1,0:T(8,128)(2,1)S(1)} %get-tuple-element.30.n1_ref) | copy-start | bytes 3145732
  113.0 20.3 %copy-start.4 = (bf16[2,2,256,512]{3,2,1,0:T(8,128)(2,1)S(1)}, bf16[2,2,256,512]{3,2,1,0:T(8,128)(2,1)}, u32[]{:S(2)}) copy-start(bf16[2,2,256,512]{3,2,1,0:T(8,128)(2,1)} %copy-done.3) | copy-start | bytes 3145732
  113.7 12.3 %collective-permute-start.14 = (bf16[4,256,128]{2,1,0:T(8,128)(2,1)}, bf16[4,256,128]{2,1,0:T(8,128)(2,1)S(1)}, u32[]{:S(2)}, u32[]{:S(2)}) collective-permute-start(bf16[4,256,128]{2,1,0:T(8,128)(2,1)} %copy-done.7), channel_id=1, source_target_pairs={{0,1},{1,0},{2,3},{3,2},{4,5},{5,4},{6,7},{7,6},{8,9},{9,8},{10,11... | collective-permute-start | bytes 786440 | tf_op jit(solution)/shard_map/ppermute | solution.py:396
  115.9 10.0 %all-to-all-start.1 = ((f32[32,1,192]{2,1,0:T(1,128)}), f32[32,1,192]{2,1,0:T(1,128)S(1)}, u32[]{:S(2)}, u32[]{:S(2)}) async-start(f32[32,1,192]{2,1,0:T(1,128)} %all_to_all.14), calls=%async_computation.1 | async-start | bytes 65536 | tf_op jit(solution)/shard_map/all_to_all | solution.py:559
  119.0 24.0 %collective-permute-start.19 = (bf16[4,512,128]{2,1,0:T(8,128)(2,1)S(1)}, bf16[4,512,128]{2,1,0:T(8,128)(2,1)}, u32[]{:S(2)}, u32[]{:S(2)}) collective-permute-start(bf16[4,512,128]{2,1,0:T(8,128)(2,1)S(1)} %get-tuple-element.45), channel_id=1, source_target_pairs={{0,1},{1,0},{2,3},{3,2},{4,5},{5,4},{6,7},{7,6},{8,9},{9,8},{10,11... | collective-permute-start | bytes 1572872 | tf_op jit(solution)/shard_map/ppermute | solution.py:396
  126.1 7.2 %collective-permute-start.15 = (bf16[256,128]{1,0:T(8,128)(2,1)S(1)}, bf16[256,128]{1,0:T(8,128)(2,1)S(1)}, u32[]{:S(2)}, u32[]{:S(2)}) collective-permute-start(bf16[256,128]{1,0:T(8,128)(2,1)S(1)} %get-tuple-element.114), channel_id=1, source_target_pairs={{0,0},{1,1},{8,2},{9,3},{16,4},{17,5},{24,6},{25,7},{2,8},{3,9},{1... | collective-permute-start | bytes 196616 | tf_op jit(solution)/shard_map/ppermute | solution.py:400
  126.7 7.8 %collective-permute-start.16 = (bf16[256,128]{1,0:T(8,128)(2,1)S(1)}, bf16[256,128]{1,0:T(8,128)(2,1)S(1)}, u32[]{:S(2)}, u32[]{:S(2)}) collective-permute-start(bf16[256,128]{1,0:T(8,128)(2,1)S(1)} %get-tuple-element.117), channel_id=1, source_target_pairs={{2,0},{3,1},{10,2},{11,3},{18,4},{19,5},{26,6},{27,7},{0,8},{1,9},... | collective-permute-start | bytes 196616 | tf_op jit(solution)/shard_map/ppermute | solution.py:400
  128.6 12.9 %collective-permute-start.17 = (bf16[256,128]{1,0:T(8,128)(2,1)S(1)}, bf16[256,128]{1,0:T(8,128)(2,1)S(1)}, u32[]{:S(2)}, u32[]{:S(2)}) collective-permute-start(bf16[256,128]{1,0:T(8,128)(2,1)S(1)} %get-tuple-element.116), channel_id=1, source_target_pairs={{4,0},{5,1},{12,2},{13,3},{20,4},{21,5},{28,6},{29,7},{6,8},{7,9},... | collective-permute-start | bytes 196616 | tf_op jit(solution)/shard_map/ppermute | solution.py:400
  131.2 10.3 %collective-permute-start.18 = (bf16[256,128]{1,0:T(8,128)(2,1)S(1)}, bf16[256,128]{1,0:T(8,128)(2,1)S(1)}, u32[]{:S(2)}, u32[]{:S(2)}) collective-permute-start(bf16[256,128]{1,0:T(8,128)(2,1)S(1)} %get-tuple-element.115), channel_id=1, source_target_pairs={{6,0},{7,1},{14,2},{15,3},{22,4},{23,5},{30,6},{31,7},{4,8},{5,9},... | collective-permute-start | bytes 196616 | tf_op jit(solution)/shard_map/ppermute | solution.py:400
  132.2 42.0 %copy-start.10 = (f32[16]{0:T(128)}, f32[16]{0:T(128)S(1)}, u32[]{:S(2)}) copy-start(f32[16]{0:T(128)S(1)} %get-tuple-element.162) | copy-start | bytes 196
  133.3 16.7 %collective-permute-start.12 = (bf16[2,2,256,512]{3,2,1,0:T(8,128)(2,1)S(1)}, bf16[2,2,256,512]{3,2,1,0:T(8,128)(2,1)}, u32[]{:S(2)}, u32[]{:S(2)}) collective-permute-start(bf16[2,2,256,512]{3,2,1,0:T(8,128)(2,1)S(1)} %copy-done.4), channel_id=1, source_target_pairs={{0,8},{8,0},{16,24},{24,16},{1,9},{9,1},{17,25},{25,17},{2,10},{10... | collective-permute-start | bytes 3145736 | tf_op jit(solution)/shard_map/ppermute | solution.py:379
  144.7 10.4 %collective-permute-start.20 = (bf16[512,128]{1,0:T(8,128)(2,1)S(1)}, bf16[512,128]{1,0:T(8,128)(2,1)S(1)}, u32[]{:S(2)}, u32[]{:S(2)}) collective-permute-start(bf16[512,128]{1,0:T(8,128)(2,1)S(1)} %get-tuple-element.108), channel_id=1, source_target_pairs={{0,0},{1,1},{8,2},{9,3},{16,4},{17,5},{24,6},{25,7},{2,8},{3,9},{1... | collective-permute-start | bytes 393224 | tf_op jit(solution)/shard_map/ppermute | solution.py:400
  145.4 9.8 %collective-permute-start.21 = (bf16[512,128]{1,0:T(8,128)(2,1)S(1)}, bf16[512,128]{1,0:T(8,128)(2,1)S(1)}, u32[]{:S(2)}, u32[]{:S(2)}) collective-permute-start(bf16[512,128]{1,0:T(8,128)(2,1)S(1)} %get-tuple-element.111), channel_id=1, source_target_pairs={{2,0},{3,1},{10,2},{11,3},{18,4},{19,5},{26,6},{27,7},{0,8},{1,9},... | collective-permute-start | bytes 393224 | tf_op jit(solution)/shard_map/ppermute | solution.py:400
  147.2 21.8 %collective-permute-start.22 = (bf16[512,128]{1,0:T(8,128)(2,1)S(1)}, bf16[512,128]{1,0:T(8,128)(2,1)S(1)}, u32[]{:S(2)}, u32[]{:S(2)}) collective-permute-start(bf16[512,128]{1,0:T(8,128)(2,1)S(1)} %get-tuple-element.110), channel_id=1, source_target_pairs={{4,0},{5,1},{12,2},{13,3},{20,4},{21,5},{28,6},{29,7},{6,8},{7,9},... | collective-permute-start | bytes 393224 | tf_op jit(solution)/shard_map/ppermute | solution.py:400
  149.4 19.5 %collective-permute-start.23 = (bf16[512,128]{1,0:T(8,128)(2,1)S(1)}, bf16[512,128]{1,0:T(8,128)(2,1)S(1)}, u32[]{:S(2)}, u32[]{:S(2)}) collective-permute-start(bf16[512,128]{1,0:T(8,128)(2,1)S(1)} %get-tuple-element.109), channel_id=1, source_target_pairs={{6,0},{7,1},{14,2},{15,3},{22,4},{23,5},{30,6},{31,7},{4,8},{5,9},... | collective-permute-start | bytes 393224 | tf_op jit(solution)/shard_map/ppermute | solution.py:400
  151.6 20.8 %collective-permute-start.13 = (bf16[2,256,512]{2,1,0:T(8,128)(2,1)S(1)}, bf16[2,256,512]{2,1,0:T(8,128)(2,1)S(1)}, u32[]{:S(2)}, u32[]{:S(2)}) collective-permute-start(bf16[2,256,512]{2,1,0:T(8,128)(2,1)S(1)} %fusion.14), channel_id=1, source_target_pairs={{0,16},{8,24},{16,0},{24,8},{1,17},{9,25},{17,1},{25,9},{2,18},{10... | collective-permute-start | bytes 1572872 | tf_op jit(solution)/shard_map/ppermute | solution.py:379
  (5 other events, 10.5 us)

commit v3 on v2

v3 whole, which is shorter than its diff:
```python
import functools
import math

import jax
import jax.numpy as jnp
import numpy as np
from jax import lax
from jax.experimental import pallas as pl
from jax.experimental.pallas import tpu as pltpu
from jax.sharding import PartitionSpec as P

HD = 64
ROT = 16
EPS = 1e-05
MASKED = -1e30
BF = jnp.bfloat16
F32 = jnp.float32


def normalize(rows_in):
    average = jnp.mean(rows_in, axis=-1, keepdims=True)
    centred = rows_in - average
    spread = jnp.mean(centred * centred, axis=-1, keepdims=True)
    root = lax.rsqrt(spread + EPS)
    return centred * root, root


def dot(a, b, dims=((1,), (0,))):
    return lax.dot_general(a, b, (dims, ((), ())), preferred_element_type=F32)


def pack_att(project, mix):
    return jnp.concatenate([project.T, mix], axis=0)


def pack_mlp(up, down):
    return jnp.concatenate([up[:, :128], up[:, 128:], down], axis=0)


def unpack_up(p):
    return jnp.concatenate([p[:128], p[128:256]], axis=1)


def rotary_tables(positions):
    lane = np.arange(2 * HD) % HD
    frequency = np.where(lane < ROT, 10000.0 ** (-(lane % (ROT // 2)) * 2.0 / ROT), 0.0)
    angles = positions[:, None].astype(F32) * jnp.asarray(frequency, F32)[None, :]
    return jnp.cos(angles), jnp.sin(angles)


VMEM_LIMIT = 24 << 20


def roll(value, shift):
    return pltpu.roll(value, shift, 1)


def lanes_of(shape):
    return lax.broadcasted_iota(jnp.int32, shape, 1)


VMEM = pl.BlockSpec(memory_space=pltpu.VMEM)
SMEM = pl.BlockSpec(memory_space=pltpu.SMEM)
SHAPE = jax.ShapeDtypeStruct
LINES = 8


def call(kernel, name, work, operands, results, scratch):
    return pl.pallas_call(
        kernel,
        out_shape=results,
        in_specs=[SMEM] + [VMEM] * (len(operands) - 1),
        out_specs=[VMEM] * len(results),
        scratch_shapes=[pltpu.VMEM(size, dtype) for size, dtype in scratch],
        compiler_params=pltpu.CompilerParams(vmem_limit_bytes=VMEM_LIMIT),
        cost_estimate=pl.CostEstimate(flops=work, bytes_accessed=work // 400, transcendentals=0),
        name=name,
    )(*operands)


def fetch_in(sources, held, sems):
    copies = [
        pltpu.make_async_copy(source, target, sems.at[i])
        for i, (source, target) in enumerate(zip(sources, held))
    ]
    for copy in copies:
        copy.start()
    for copy in copies:
        copy.wait()


def prepare_kernel(paired, *refs):
    sources, (small_ref, *packs), held = refs[:13], refs[13 : 14 + 2 * paired], refs[14 + 2 * paired :]
    line, sems = held[13], held[14]
    fetch_in(sources, held, sems)
    seg_ref, project_ref, mix_ref, up_ref, down_ref, *vectors = held[:13]
    if paired:
        att, mlp = packs
        att[0:192, :] = project_ref[...]
        att[192:256, :] = mix_ref[...]
        mlp[0:128, :] = up_ref[:, 0:128]
        mlp[128:256, :] = up_ref[:, 128:256]
        mlp[256:512, :] = down_ref[...]
    line[...] = jnp.zeros(line.shape, F32)
    part = vectors[0].shape[1]
    for i in range(6):
        line[0:1, i * part : (i + 1) * part] = vectors[i][...].astype(F32)
    line[1:2, 0 : vectors[6].shape[1]] = vectors[6][...].astype(F32)
    line[2:3, 0 : vectors[7].shape[1]] = vectors[7][...].astype(F32)
    seg = seg_ref[...]
    blocks = seg.shape[1] // 128
    for i in range(blocks):
        piece = seg[:, i * 128 : (i + 1) * 128]
        line[3 + i : 4 + i, :] = (piece >> 5).astype(F32)
        line[3 + blocks + i : 4 + blocks + i, :] = (piece & 31).astype(F32)
    full = line[...].astype(BF)
    for i in range(small_ref.shape[0]):
        small_ref[i] = full


def run_local(kernel, name, work, sources, results, scratch):
    return pl.pallas_call(
        kernel,
        out_shape=results,
        in_specs=[pl.BlockSpec(memory_space=pl.ANY)] * len(sources),
        out_specs=[VMEM] * len(results),
        scratch_shapes=[pltpu.VMEM(v.shape, v.dtype) for v in sources]
        + scratch
        + [pltpu.SemaphoreType.DMA((len(sources),))],
        compiler_params=pltpu.CompilerParams(vmem_limit_bytes=60 << 20),
        cost_estimate=pl.CostEstimate(flops=work, bytes_accessed=1 << 20, transcendentals=0),
        name=name,
    )(*sources)


def layout_kernel(rows, cols, sizes, where_ref, every_ref, norms_ref, project_ref, up_ref, starts_ref):
    c, y, group = where_ref[2], where_ref[3], where_ref[4]
    part, project, up = sizes
    copies = every_ref.shape[0]

    def spread_out(block, lane_of, row_of, wide):
        lane = lax.broadcasted_iota(jnp.int32, (128, wide), 0)
        place = lax.broadcasted_iota(jnp.int32, (128, wide), 1)
        picked = dot(block, jnp.where(lane == lane_of(place), 1.0, 0.0).astype(BF))
        device = lax.broadcasted_iota(jnp.int32, (copies, wide), 0)
        place = lax.broadcasted_iota(jnp.int32, (copies, wide), 1)
        return jnp.sum(jnp.where(device == row_of(place), picked, 0.0), axis=0, keepdims=True)

    def line(i):
        return every_ref[:, i, :]

    wide = norms_ref.shape[1]
    rows_of = [line(i) for i in range(LINES)]
    for i in range(6):
        norms_ref[i : i + 1, :] = spread_out(
            rows_of[0], lambda n: i * part + n % part, lambda n: n // part, wide
        )
    norms_ref[6:8, :] = jnp.zeros((2, wide), F32)
    half = cols // 2
    for h in range(2):
        begin = group * cols + (h ^ y) * half
        project_ref[h : h + 1, :] = spread_out(
            rows_of[1],
            lambda n: n % project,
            lambda n: jnp.where(n < half * project, begin + n // project, -1),
            256,
        )
        up_ref[:, h * 256 : h * 256 + 256] = spread_out(
            rows_of[2], lambda n: n % up, lambda n: begin + n // up, 256
        )
    device = lax.broadcasted_iota(jnp.int32, (copies, 128), 0)
    eye = lax.broadcasted_iota(jnp.int32, (128, 128), 0) == lanes_of((128, 128))
    count = starts_ref.shape[0] // rows
    blocks = count // 128
    for g in range(rows):
        here = device == g * cols + c
        for b in range(blocks):
            coarse, fine = rows_of[3 + b].astype(F32), rows_of[3 + blocks + b].astype(F32)
            value = jnp.sum(jnp.where(here, coarse * 32.0 + fine, 0.0), axis=0, keepdims=True)
            column = jnp.sum(jnp.where(eye, value, 0.0), axis=1, keepdims=True)
            begin = g * count + b * 128
            starts_ref[begin : begin + 128, :] = column.astype(jnp.int32)


def mlp_kernel(
    where_ref,
    n2_ref,
    xhat_ref,
    cot_ref,
    own_ref,
    oth_ref,
    norms_ref,
    shift_ref,
    out_ref,
    e_ref,
    send_ref,
    keep_ref,
    small_ref,
    up_s,
    down_s,
    act_s,
    dh_s,
    ug_s,
    dg_s,
):
    r, key = where_ref[0], where_ref[1]
    count = n2_ref.shape[0] // 4
    gain = norms_ref[2:3, :]
    for k in range(4):
        g = pl.multiple_of((key ^ k) * 128, 128)
        for h, ref in enumerate((own_ref, oth_ref)):
            b = ref.shape[1] - 512
            up_s[pl.ds(g, 128), h * 256 : h * 256 + 128] = ref[k, b : b + 128]
            up_s[pl.ds(g, 128), h * 256 + 128 : h * 256 + 256] = ref[k, b + 128 : b + 256]
            down_s[h * 256 : h * 256 + 256, pl.ds(g, 128)] = ref[k, b + 256 : b + 512]
    up, down = up_s[...], down_s[...]
    shift = shift_ref[...]
    sums = [jnp.zeros((1, up.shape[1]), F32)] * 3
    for t in range(4):
        at = slice(t * count, t * count + count)
        hidden = dot(n2_ref[at, :], up) + shift
        cdf = 0.5 + 0.5 * lax.erf(hidden * math.sqrt(0.5))
        active = (hidden * cdf).astype(BF)
        slope = cdf + hidden * jnp.exp(-0.5 * hidden * hidden) * (1.0 / math.sqrt(2 * math.pi))
        act_s[at, :] = active
        out_ref[at, :] = dot(active, down).astype(BF)
        d_hidden = (dot(cot_ref[at, :], down, ((1,), (1,))) * slope).astype(BF)
        dh_s[at, :] = d_hidden
        d_second = dot(d_hidden, up, ((1,), (1,)))
        e_ref[at, :] = (d_second * gain).astype(BF)
        sums[0] += jnp.sum(d_hidden.astype(F32), axis=0, keepdims=True)
        sums[1] += jnp.sum(d_second * xhat_ref[at, :].astype(F32), axis=0, keepdims=True)
        sums[2] += jnp.sum(d_second, axis=0, keepdims=True)
    mine = cot_ref[pl.ds(pl.multiple_of(r * count, count), count), :]
    sums.append(jnp.sum(mine.astype(F32), axis=0, keepdims=True))
    for i, row in enumerate(sums):
        small_ref[i : i + 1, :] = row
    small_ref[4:8, :] = jnp.zeros((4, small_ref.shape[1]), F32)
    ug_s[...] = dot(n2_ref[...], dh_s[...], ((0,), (0,)))
    dg_s[...] = dot(act_s[...], cot_ref[...], ((0,), (0,)))
    for k in range(4):
        g = pl.multiple_of((key ^ k) * 128, 128)
        for h, ref in enumerate((keep_ref, send_ref)):
            ref[k, 0:128] = ug_s[pl.ds(g, 128), h * 256 : h * 256 + 128].astype(ref.dtype)
            ref[k, 128:256] = ug_s[pl.ds(g, 128), h * 256 + 128 : h * 256 + 256].astype(ref.dtype)
            ref[k, 256:512] = dg_s[h * 256 : h * 256 + 256, pl.ds(g, 128)].astype(ref.dtype)


def run_mlp(where, n2, xhat, cot, own, oth, norms, shift):
    tall, width = n2.shape
    wide = shift.shape[1]
    return call(
        mlp_kernel,
        "feed_forward",
        1 << 35,
        (where, n2, xhat, cot, own, oth, norms, shift),
        (
            SHAPE((tall, width), BF),
            SHAPE((tall, width), BF),
            SHAPE(oth.shape, BF),
            SHAPE(oth.shape, F32),
            SHAPE((8, wide), F32),
        ),
        (
            ((width, wide), BF),
            ((wide, width), BF),
            ((tall, wide), BF),
            ((tall, wide), BF),
            ((width, wide), F32),
            ((wide, width), F32),
        ),
    )


def head(key, n1_ref, cot_ref, slots_ref, shift, cos_ref, sin_ref, starts_ref, w, mix, ctx, dp, grads_ref, scratch):
    q_s, qh_s, k_s, v_s, dctx_s, dq_s, dt_s, pg_s, mg_s = scratch
    tall = n1_ref.shape[0]
    count = tall // 4
    scaling = HD**-0.5
    w[192:256, :] = jnp.zeros((64, w.shape[1]), BF)
    mix[64:128, :] = jnp.zeros((64, mix.shape[1]), BF)
    for k in range(4):
        g = pl.multiple_of((key ^ k) * 128, 128)
        w[0:192, pl.ds(g, 128)] = slots_ref[k, 0:192]
        mix[0:64, pl.ds(g, 128)] = slots_ref[k, 192:256]
    lane = lanes_of((count, 128))
    left = lane < 64
    first, second = lane % 64 < ROT // 2, lane % 64 < ROT

    def turn(qk, at, sign):
        sine = sin_ref[at, :] * sign
        minus = jnp.where(first, -sine, 0.0)
        plus = jnp.where(first, 0.0, jnp.where(second, sine, 0.0))
        return qk * cos_ref[at, :] + roll(qk, 120) * minus + roll(qk, 8) * plus

    for t in range(4):
        at = slice(t * count, t * count + count)
        projected = dot(n1_ref[at, :], w[...], ((1,), (1,))) + shift
        qk = turn(projected[:, :128], at, 1.0)
        turned = roll(qk, 64)
        q_s[at, :] = jnp.where(left, qk, 0.0).astype(BF)
        k_s[at, :] = jnp.where(left, turned, 0.0).astype(BF)
        qh_s[at, :] = jnp.where(left, 0.0, turned).astype(BF)
        v_s[at, :] = projected[:, 128:].astype(BF)
        dctx_s[at, :] = dot(cot_ref[at, :], mix[...], ((1,), (1,))).astype(BF)
    dt_s[...] = jnp.zeros(dt_s.shape, F32)
    for t in range(4):
        at = slice(t * count, t * count + count)
        keys = (t + 1) * count
        q, d_context = q_s[at, :], dctx_s[at, :]
        kk, vv = k_s[0:keys, :], v_s[0:keys, :]
        scores = dot(q, kk, ((1,), (1,))) * scaling
        place = lax.broadcasted_iota(jnp.int32, (count, keys), 1)
        row = lax.broadcasted_iota(jnp.int32, (count, 1), 0) + t * count
        allowed = (place >= starts_ref[at, :]) & (place <= row)
        scores = jnp.where(allowed, scores, MASKED)
        exponent = jnp.exp(scores - jnp.max(scores, axis=-1, keepdims=True))
        probability = exponent * (1.0 / jnp.sum(exponent, axis=-1, keepdims=True))
        prob_low = probability.astype(BF)
        ctx[at, :] = dot(prob_low, vv).astype(BF)
        d_prob = dot(d_context, vv, ((1,), (1,)))
        weight = jnp.sum(d_prob * probability, axis=-1, keepdims=True)
        d_scores = (probability * (d_prob - weight)).astype(BF)
        dq_s[at, :] = dot(d_scores, kk)
        dt_s[0:128, 0:keys] += dot(qh_s[at, :], d_scores, ((0,), (0,)))
        dt_s[128:256, 0:keys] += dot(d_context, prob_low, ((0,), (0,)))
    shift_sum = jnp.zeros((1, 256), F32)
    for t in range(4):
        at = slice(t * count, t * count + count)
        turned = jnp.transpose(dt_s[:, at])
        qk = turn((dq_s[at, :] + turned[:, :128]) * scaling, at, -1.0)
        dp[at, 0:128] = qk.astype(BF)
        dp[at, 128:256] = turned[:, 128:].astype(BF)
        shift_sum += jnp.sum(dp[at, :].astype(F32), axis=0, keepdims=True)
    pg_s[...] = dot(dp[...], n1_ref[...], ((0,), (0,)))
    mg_s[...] = dot(ctx[...], cot_ref[...], ((0,), (0,)))
    for k in range(4):
        g = pl.multiple_of((key ^ k) * 128, 128)
        grads_ref[k, 0:192] = pg_s[0:192, pl.ds(g, 128)].astype(grads_ref.dtype)
        grads_ref[k, 192:256] = mg_s[0:64, pl.ds(g, 128)].astype(grads_ref.dtype)
    return shift_sum


def head_scratch(tall, width):
    return (
        ((tall, 128), BF),
        ((tall, 128), BF),
        ((tall, 128), BF),
        ((tall, 128), BF),
        ((tall, 128), BF),
        ((tall, 128), F32),
        ((256, tall), F32),
        ((256, width), F32),
        ((128, width), F32),
    )


def first_kernel(
    where_ref,
    x0_ref,
    x1_ref,
    x2_ref,
    x3_ref,
    cot0_ref,
    cot1_ref,
    cot2_ref,
    cot3_ref,
    slots_ref,
    shift_ref,
    cos_ref,
    sin_ref,
    starts_ref,
    norms_ref,
    n1_ref,
    n2_ref,
    xhat_ref,
    cot_ref,
    w_ref,
    mix_ref,
    ctx_ref,
    dp_ref,
    grads_ref,
    small_ref,
    *scratch,
):
    r, key = where_ref[0], where_ref[1]
    count = x0_ref.shape[0]
    norms = norms_ref[...]
    grads_in = (cot0_ref, cot1_ref, cot2_ref, cot3_ref)
    for j, source in enumerate((x0_ref, x1_ref, x2_ref, x3_ref)):
        at = pl.ds(pl.multiple_of((r ^ j) * count, count), count)
        hat, unused = normalize(source[...].astype(F32))
        xhat_ref[at, :] = hat.astype(BF)
        n1_ref[at, :] = (hat * norms[0:1] + norms[1:2]).astype(BF)
        n2_ref[at, :] = (hat * norms[2:3] + norms[3:4]).astype(BF)
        cot_ref[at, :] = grads_in[j][...]
    small_ref[...] = jnp.zeros(small_ref.shape, F32)
    small_ref[0:1, 0:256] = head(
        key,
        n1_ref,
        cot_ref,
        slots_ref,
        shift_ref[0:1, :],
        cos_ref,
        sin_ref,
        starts_ref,
        w_ref,
        mix_ref,
        ctx_ref,
        dp_ref,
        grads_ref,
        scratch,
    )


def run_first(where, chunks, slots, shift, cosine, sine, starts, norms):
    count, width = chunks[0].shape
    tall = 4 * count
    return call(
        first_kernel,
        "attention_first",
        1 << 35,
        (where, *chunks, slots, shift, cosine, sine, starts, norms),
        (
            SHAPE((tall, width), BF),
            SHAPE((tall, width), BF),
            SHAPE((tall, width), BF),
            SHAPE((tall, width), BF),
            SHAPE((256, width), BF),
            SHAPE((128, width), BF),
            SHAPE((tall, 128), BF),
            SHAPE((tall, 256), BF),
            SHAPE((4, 256, 128), F32),
            SHAPE((8, width), F32),
        ),
        head_scratch(tall, width),
    )


def second_kernel(
    where_ref,
    n1_ref,
    cot_ref,
    slots_ref,
    shift_ref,
    cos_ref,
    sin_ref,
    starts_ref,
    w_ref,
    mix_ref,
    ctx_ref,
    dp_ref,
    grads_ref,
    small_ref,
    *scratch,
):
    small_ref[...] = jnp.zeros(small_ref.shape, F32)
    small_ref[0:1, 0:256] = head(
        where_ref[1],
        n1_ref,
        cot_ref,
        slots_ref,
        shift_ref[1:2, :],
        cos_ref,
        sin_ref,
        starts_ref,
        w_ref,
        mix_ref,
        ctx_ref,
        dp_ref,
        grads_ref,
        scratch,
    )


def run_second(where, n1, cot, slots, shift, cosine, sine, starts):
    tall, width = n1.shape
    return call(
        second_kernel,
        "attention_second",
        1 << 35,
        (where, n1, cot, slots, shift, cosine, sine, starts),
        (
            SHAPE((256, width), BF),
            SHAPE((128, width), BF),
            SHAPE((tall, 128), BF),
            SHAPE((tall, 256), BF),
            SHAPE((4, 256, 128), BF),
            SHAPE((8, width), F32),
        ),
        head_scratch(tall, width),
    )


def join_kernel(
    where_ref,
    xhat_ref,
    norms_ref,
    w_a,
    mix_a,
    ctx_a,
    dp_a,
    w_b,
    mix_b,
    ctx_b,
    dp_b,
    out_in,
    e_in,
    near_ref,
    rest_ref,
    small_ref,
):
    r = where_ref[0]
    count = xhat_ref.shape[0] // 4
    sums = [jnp.zeros((1, xhat_ref.shape[1]), F32)] * 2
    gain = norms_ref[0:1, :]
    for j in range(4):
        at = pl.ds(pl.multiple_of((r ^ j) * count, count), count)
        d_first = dot(dp_a[at, :], w_a[...]) + dot(dp_b[at, :], w_b[...])
        sums[0] += jnp.sum(d_first * xhat_ref[at, :].astype(F32), axis=0, keepdims=True)
        sums[1] += jnp.sum(d_first, axis=0, keepdims=True)
        out = dot(ctx_a[at, :], mix_a[...]) + dot(ctx_b[at, :], mix_b[...])
        target = near_ref if j % 2 else rest_ref
        target[j // 2, 0] = (out_in[at, :].astype(F32) + out).astype(target.dtype)
        target[j // 2, 1] = (e_in[at, :].astype(F32) + d_first * gain).astype(target.dtype)
    small_ref[...] = jnp.zeros(small_ref.shape, F32)
    small_ref[0:1, :] = sums[0]
    small_ref[1:2, :] = sums[1]


def run_join(where, xhat, norms, first, second, out, e):
    tall, width = xhat.shape
    count = tall // 4
    return call(
        join_kernel,
        "join",
        1 << 35,
        (where, xhat, norms, *first, *second, out, e),
        (
            SHAPE((2, 2, count, width), BF),
            SHAPE((2, 2, count, width), F32),
            SHAPE((8, width), F32),
        ),
        (),
    )


def merge_kernel(unused, att_keep, att_come, mlp_keep, mlp_come, *outs):
    for k in range(4):
        outs[k][0:256, :] = (att_keep[k] + att_come[k].astype(F32)).astype(BF)
        outs[k][256:768, :] = (mlp_keep[k] + mlp_come[k].astype(F32)).astype(BF)


def collect_kernel(unused, a_ref, b_ref, c_ref, d_ref, project_ref, mix_ref, up_ref, down_ref):
    def total(begin, end):
        refs = (a_ref, b_ref, c_ref, d_ref)
        return sum(ref[begin:end, :].astype(F32) for ref in refs)

    project_ref[...] = total(0, 192)
    mix_ref[...] = total(192, 256)
    up_ref[:, 0:128] = total(256, 384)
    up_ref[:, 128:256] = total(384, 512)
    down_ref[...] = total(512, 768)


def on_device(
    inputs,
    seg_start,
    cotangent,
    project_weight,
    project_bias,
    output_weight,
    output_bias,
    up_weight,
    up_bias,
    down_weight,
    down_bias,
    first_gain,
    first_bias,
    second_gain,
    second_bias,
):
    rows, cols = lax.axis_size("row"), lax.axis_size("col")
    per = cols // rows
    r, c = lax.axis_index("row"), lax.axis_index("col")
    both = ("row", "col")
    count, width = inputs.shape[1], inputs.shape[2]
    paired = per == 2

    def flip(value, bit):
        return lax.ppermute(value, "row", [(i, i ^ bit) for i in range(rows)])

    def group_of(i):
        return (i % 2) * 2 + i // 2

    def home(i, k):
        rr, cc = divmod(i, cols)
        z, y = divmod(cc, per)
        return group_of(z) * cols + (rr ^ k) * per + y

    everyone = range(rows * cols)

    def beside(value):
        return lax.ppermute(value, "col", [(i, i ^ 1) for i in range(cols)])

    def spread(block):
        return [lax.ppermute(block, both, [(i, home(i, k)) for i in everyone]) for k in range(rows)]

    def bring(blocks):
        return [
            lax.ppermute(b, both, [(home(i, k), i) for i in everyone]) for k, b in enumerate(blocks)
        ]

    def slot_of(i):
        rr, cc = divmod(i, cols)
        return group_of(cc // per) * cols + (cc % per) * rows + rr

    def fetch(block):
        moved = lax.ppermute(block, both, [(i, slot_of(i)) for i in everyone])
        whole = lax.all_gather(moved, "col", axis=0)
        return whole.reshape((per, rows) + block.shape)

    def fetch_columns(block):
        whole = fetch(block).transpose(1, 2, 0, 3).reshape(rows, block.shape[0], 2, -1)
        return whole.transpose(2, 0, 1, 3)

    def fetch_rows(block):
        whole = fetch(block).transpose(1, 0, 2, 3).reshape(rows, 2, -1, block.shape[1])
        return whole.transpose(1, 0, 2, 3)

    def deliver(blocks):
        flat = blocks.reshape((cols,) + blocks.shape[2:]).astype(BF)
        mine = lax.psum_scatter(flat, "col", scatter_dimension=0, tiled=False)
        return lax.ppermute(mine, both, [(slot_of(i), i) for i in everyone]).astype(F32)

    def deliver_columns(halves):
        deep = halves.shape[2]
        whole = halves.transpose(1, 2, 0, 3).reshape(rows, deep, per, -1)
        return deliver(whole.transpose(2, 0, 1, 3))

    def deliver_rows(halves):
        wide = halves.shape[3]
        whole = halves.transpose(1, 0, 2, 3).reshape(rows, per, -1, wide)
        return deliver(whole.transpose(1, 0, 2, 3))

    if paired:
        key, y = c // per, c % per
    else:
        key, y = jnp.int32(0), jnp.int32(0)
    group = group_of(r)
    where = jnp.stack([r, key, c, y, group]).astype(jnp.int32)
    part, project_len, up_len = first_gain.shape[0], project_bias.shape[0], up_bias.shape[0]
    copies = rows * cols
    x_own, cot_own = inputs[0], cotangent[0]
    x_across, cot_across = flip(x_own, 2), flip(cot_own, 2)
    x_far, cot_far = flip(x_own, 1), flip(cot_own, 1)
    chunks = (x_own, x_far, x_across, flip(x_across, 1))
    chunks += (cot_own, cot_far, cot_across, flip(cot_across, 1))
    vectors = (
        first_gain,
        first_bias,
        second_gain,
        second_bias,
        output_bias,
        down_bias,
        project_bias,
        up_bias,
    )
    results = [SHAPE((copies, LINES, 128), BF)]
    if paired:
        results += [SHAPE((256, 128), BF), SHAPE((512, 128), BF)]
    small, *packs = run_local(
        functools.partial(prepare_kernel, paired),
        "prepare",
        1 << 20,
        (seg_start, project_weight.T, output_weight, up_weight, down_weight)
        + tuple(v[None] for v in vectors),
        results,
        [pltpu.VMEM((LINES, 128), F32)],
    )
    every = lax.all_to_all(small, both, 0, 0, tiled=True)
    if paired:
        att_own, mlp_own = jnp.stack(spread(packs[0])), jnp.stack(spread(packs[1]))
        att_slots = att_own, beside(att_own)
        mlp_slots = mlp_own, beside(mlp_own)
    else:
        ups, downs = fetch_columns(up_weight), fetch_rows(down_weight)
        projects, mixes = fetch_columns(project_weight), fetch_rows(output_weight)
        mlp_slots = [
            jnp.stack(
                [pack_mlp(ups[h, g], downs[h, g]) for g in range(rows)]
            )
            for h in range(2)
        ]
        att_slots = [
            jnp.stack(
                [pack_att(projects[h, g], mixes[h, g]) for g in range(rows)]
            )
            for h in range(2)
        ]

    norms, project_shift, up_shift, starts = call(
        functools.partial(layout_kernel, rows, cols, (part, project_len, up_len)),
        "layout",
        1 << 24,
        (where, every),
        (
            SHAPE((8, width), F32),
            SHAPE((2, 256), F32),
            SHAPE((1, 512), F32),
            SHAPE((rows * count, 1), jnp.int32),
        ),
        (),
    )
    cosine, sine = rotary_tables(jnp.arange(rows * count, dtype=jnp.int32) - starts[:, 0])

    n1, n2, xhat, cot_all, *first, att_keep, small_own = run_first(
        where, chunks, att_slots[0], project_shift, cosine, sine, starts, norms
    )
    *second, att_send, small_oth = run_second(
        where, n1, cot_all, att_slots[1], project_shift, cosine, sine, starts
    )
    out, e, mlp_send, mlp_keep, mlp_small = run_mlp(
        where, n2, xhat, cot_all, mlp_slots[0], mlp_slots[1], norms, up_shift
    )
    near, rest, small_join = run_join(where, xhat, norms, first, second, out, e)
    ub_own, ub_oth = mlp_small[0, :256], mlp_small[0, 256:]
    pb_own, pb_oth = small_own[0, : 3 * HD], small_oth[0, : 3 * HD]

    mine = rest + flip(near, 1).astype(F32)
    total = mine[0] + flip(mine[1].astype(BF), 2).astype(F32)
    x_own, cot_own = inputs[0].astype(F32), cotangent[0].astype(F32)
    output = (x_own + total[0] + norms[4] + norms[5]).astype(BF)[None]
    e_all = total[1]
    xhat_own, root_own = normalize(x_own)
    input_grad = cot_own + root_own * (
        e_all
        - jnp.mean(e_all, axis=-1, keepdims=True)
        - xhat_own * jnp.mean(e_all * xhat_own, axis=-1, keepdims=True)
    )

    if paired:
        blocks = call(
            merge_kernel,
            "merge",
            1 << 26,
            (where, att_keep, beside(att_send), mlp_keep, beside(mlp_send)),
            (SHAPE((768, 128), BF),) * 4,
            (),
        )
    else:
        att_grads, mlp_grads = jnp.stack([att_keep, att_send.astype(F32)]), jnp.stack([mlp_keep, mlp_send.astype(F32)])
        every_pair = [(h, g) for h in range(2) for g in range(rows)]

        def regroup(parts):
            return jnp.stack(parts).reshape((2, rows) + parts[0].shape)

        project_done = deliver_columns(
            regroup([att_grads[h, g][:192].T for h, g in every_pair])
        )
        mix_done = deliver_rows(regroup([att_grads[h, g][192:] for h, g in every_pair]))
        up_done = deliver_columns(
            regroup([unpack_up(mlp_grads[h, g][:256]) for h, g in every_pair])
        )
        down_done = deliver_rows(regroup([mlp_grads[h, g][256:] for h, g in every_pair]))

    everywhere = jnp.concatenate([small_join[:2], mlp_small[1:4]])
    everywhere = everywhere.reshape(5, rows * cols, part).transpose(1, 0, 2).reshape(rows * cols, -1)

    def by_half(own, other):
        first = jnp.where(y == 0, own, other)
        second = jnp.where(y == 0, other, own)
        return jnp.concatenate([first, second]).reshape(cols, -1)

    local = jnp.concatenate([by_half(pb_own, pb_oth), by_half(ub_own, ub_oth)], axis=1)
    local = lax.dynamic_update_slice(
        jnp.zeros((rows * cols, local.shape[1]), F32), local, (group * cols, 0)
    )
    small = jnp.concatenate([everywhere, local], axis=1)
    if paired:
        small, blocks = lax.optimization_barrier((small, blocks))
    sums = lax.all_to_all(small, both, 0, 0, tiled=True).sum(axis=0)
    if paired:
        project_done, mix_done, up_done, down_done = call(
            collect_kernel,
            "collect",
            1 << 26,
            (where, *bring(blocks)),
            (
                SHAPE(project_weight.shape[::-1], F32),
                SHAPE(output_weight.shape, F32),
                SHAPE(up_weight.shape, F32),
                SHAPE(down_weight.shape, F32),
            ),
            (),
        )
        project_done = project_done.T
    pieces = [sums[i * part : (i + 1) * part] for i in range(5)]
    project_shift_grad = sums[5 * part : 5 * part + project_len]
    up_shift_grad = sums[5 * part + project_len :]
    return (
        output,
        input_grad[None],
        project_done,
        project_shift_grad,
        mix_done,
        pieces[4],
        up_done,
        up_shift_grad,
        down_done,
        pieces[4],
        pieces[0],
        pieces[1],
        pieces[2],
        pieces[3],
    )


def solution(mesh):
    return jax.shard_map(
        on_device,
        mesh=mesh,
        in_specs=(
            P("col", "row", None),
            P("col", "row"),
            P("col", "row", None),
            P("row", "col"),
            P(("row", "col")),
            P("col", "row"),
            P(("row", "col")),
            P("row", "col"),
            P(("row", "col")),
            P("col", "row"),
            P(("row", "col")),
            P(("row", "col")),
            P(("row", "col")),
            P(("row", "col")),
            P(("row", "col")),
        ),
        out_specs=(
            P("col", "row", None),
            P("col", "row", None),
            P("row", "col"),
            P(("row", "col")),
            P("col", "row"),
            P(("row", "col")),
            P("row", "col"),
            P(("row", "col")),
            P("col", "row"),
            P(("row", "col")),
            P(("row", "col")),
            P(("row", "col")),
            P(("row", "col")),
            P(("row", "col")),
        ),
        check_vma=False,
    )
```

time: 175 us -> 134 us (0.77)
  the two profiles are of different devices: /device:TPU:0 before, /device:TPU:25 now
where the time goes in v3:
time: 134 us; the launch traced here: 133 us
  starting transfers between devices  58 us (43%)
  waiting for transfers between devices  29.5 us (22%)
  Pallas kernels  27.6 us (21%)
  other arithmetic  9.38 us (7%)
  local copies, waits for them, and re-layouts  7.8 us (6%)
    pallas_call x7, Pallas kernels, call(): pl.pallas_call(kernel, out_shape=results, in_specs=[SMEM] + [VMEM] * (len...  25.7 us
    ppermute x4, waiting for transfers between devices, bring(): lax.ppermute(b, both, [(home(i, k), i) for i in everyone])  20.1 us
    ppermute x8, starting transfers between devices, spread(): lax.ppermute(block, both, [(i, home(i, k)) for i in everyone])  19.9 us
    ppermute x8, starting transfers between devices, flip(): return lax.ppermute(value, 'row', [(i, i ^ bit) for i in range(rows)])  11.2 us
    all_to_all x1, starting transfers between devices, on_device(): sums = lax.all_to_all(small, both, 0, 0, tiled=True).sum(axis=0)  9.23 us
    ppermute x4, starting transfers between devices, bring(): lax.ppermute(b, both, [(home(i, k), i) for i in everyone])  8.84 us
    ppermute x4, waiting for transfers between devices, beside(): return lax.ppermute(value, 'col', [(i, i ^ 1) for i in range(cols)])  7.01 us
    all_to_all x1, starting transfers between devices, on_device(): every = lax.all_to_all(small, both, 0, 0, tiled=True)  5.87 us
  transfers between devices with their start and end apart: 26, of which 7 were waited for; matrix products, arithmetic and copies ran while one was open for 9% of the time, Pallas kernels for 13%

profile of v3, /device:TPU:25, one launch (start us, length us, event | category | flops | bytes accessed | tf_op | source)
XLA Modules:
  0.0 133.4 jit_solution(1389465800007975752)
XLA Ops:
  0.7 1.8 %prepare.1 = (bf16[32,8,128]{2,1,0:T(8,128)(2,1)}, bf16[256,128]{1,0:T(8,128)(2,1)}, bf16[512,128]{1,0:T(8,128)(2,1)}) custom-call(s32[1,256]{1,0:T(1,128)} %refs_0_.1, bf16[192,128]{1,0:T(8,128)(2,1)} %bitcast.56, bf16[64,128]{1,0:T(8,128)(2,1)} %refs_2_.1, bf16[128,256]{1,0:T(8,128)(2,1)} %refs_3_.1, bf16[256,128]{1,0:T(8,128)(2,1)} %refs_4_.1, ...), custom_call_target="tpu_custom_call" | custom-call | flops 1048576 | bytes 1048576 | tf_op jit(solution)/shard_map/prepare/pallas_call | solution.py:122
  2.5 3.0 %collective-permute-start.9 = (bf16[256,128]{1,0:T(8,128)(2,1)}, bf16[256,128]{1,0:T(8,128)(2,1)S(1)}, u32[]{:S(2)}, u32[]{:S(2)}) collective-permute-start(bf16[256,128]{1,0:T(8,128)(2,1)} %get-tuple-element.58), channel_id=1, source_target_pairs={{0,6},{1,7},{2,22},{3,23},{4,14},{5,15},{6,30},{7,31},{8,4},{9,5},... | collective-permute-start | bytes 196616 | tf_op jit(solution)/shard_map/ppermute | solution.py:607
  5.7 5.0 %collective-permute-start.7 = (bf16[256,128]{1,0:T(8,128)(2,1)}, bf16[256,128]{1,0:T(8,128)(2,1)S(1)}, u32[]{:S(2)}, u32[]{:S(2)}) collective-permute-start(bf16[256,128]{1,0:T(8,128)(2,1)} %get-tuple-element.58), channel_id=1, source_target_pairs={{0,2},{1,3},{2,18},{3,19},{4,10},{5,11},{6,26},{7,27},{8,0},{9,1},... | collective-permute-start | bytes 196616 | tf_op jit(solution)/shard_map/ppermute | solution.py:607
  10.7 1.9 %collective-permute-start.6 = (bf16[256,128]{1,0:T(8,128)(2,1)}, bf16[256,128]{1,0:T(8,128)(2,1)S(1)}, u32[]{:S(2)}, u32[]{:S(2)}) collective-permute-start(bf16[256,128]{1,0:T(8,128)(2,1)} %get-tuple-element.58), channel_id=1, source_target_pairs={{0,0},{1,1},{2,16},{3,17},{4,8},{5,9},{6,24},{7,25},{8,2},{9,3},{1... | collective-permute-start | bytes 196616 | tf_op jit(solution)/shard_map/ppermute | solution.py:607
  12.7 1.4 %collective-permute-start.1 = (bf16[256,512]{1,0:T(8,128)(2,1)}, bf16[256,512]{1,0:T(8,128)(2,1)S(1)}, u32[]{:S(2)}, u32[]{:S(2)}) collective-permute-start(bf16[256,512]{1,0:T(8,128)(2,1)} %bitcast.40), channel_id=1, source_target_pairs={{0,16},{8,24},{16,0},{24,8},{1,17},{9,25},{17,1},{25,9},{2,18},{10... | collective-permute-start | bytes 786440 | tf_op jit(solution)/shard_map/ppermute | solution.py:591
  14.1 5.9 %all-to-all-start = ((bf16[32,8,128]{2,1,0:T(8,128)(2,1)}), bf16[32,8,128]{2,1,0:T(8,128)(2,1)S(1)}, u32[]{:S(2)}, u32[]{:S(2)}) async-start(bf16[32,8,128]{2,1,0:T(8,128)(2,1)} %get-tuple-element.59), calls=%async_computation | async-start | bytes 131072 | tf_op jit(solution)/shard_map/all_to_all | solution.py:681
  20.2 3.0 %collective-permute-start.14 = (bf16[512,128]{1,0:T(8,128)(2,1)}, bf16[512,128]{1,0:T(8,128)(2,1)S(1)}, u32[]{:S(2)}, u32[]{:S(2)}) collective-permute-start(bf16[512,128]{1,0:T(8,128)(2,1)} %get-tuple-element.75), channel_id=1, source_target_pairs={{0,6},{1,7},{2,22},{3,23},{4,14},{5,15},{6,30},{7,31},{8,4},{9,5},... | collective-permute-start | bytes 393224 | tf_op jit(solution)/shard_map/ppermute | solution.py:607
  23.5 4.5 %collective-permute-start.12 = (bf16[512,128]{1,0:T(8,128)(2,1)}, bf16[512,128]{1,0:T(8,128)(2,1)S(1)}, u32[]{:S(2)}, u32[]{:S(2)}) collective-permute-start(bf16[512,128]{1,0:T(8,128)(2,1)} %get-tuple-element.75), channel_id=1, source_target_pairs={{0,2},{1,3},{2,18},{3,19},{4,10},{5,11},{6,26},{7,27},{8,0},{9,1},... | collective-permute-start | bytes 393224 | tf_op jit(solution)/shard_map/ppermute | solution.py:607
  28.1 1.7 %all-to-all-done.every_ref = bf16[32,8,128]{2,1,0:T(8,128)(2,1)S(1)} async-done(((bf16[32,8,128]{2,1,0:T(8,128)(2,1)}), bf16[32,8,128]{2,1,0:T(8,128)(2,1)S(1)}, u32[]{:S(2)}, u32[]{:S(2)}) %all-to-all-start) | async-done | bytes 65568 | tf_op jit(solution)/shard_map/all_to_all | solution.py:681
  30.9 1.9 %collective-permute-start.11 = (bf16[512,128]{1,0:T(8,128)(2,1)}, bf16[512,128]{1,0:T(8,128)(2,1)S(1)}, u32[]{:S(2)}, u32[]{:S(2)}) collective-permute-start(bf16[512,128]{1,0:T(8,128)(2,1)} %get-tuple-element.75), channel_id=1, source_target_pairs={{0,0},{1,1},{2,16},{3,17},{4,8},{5,9},{6,24},{7,25},{8,2},{9,3},{1... | collective-permute-start | bytes 393224 | tf_op jit(solution)/shard_map/ppermute | solution.py:607
  32.9 1.2 collective-permute-start.3
  34.7 2.5 %multiply_sine_fusion = (f32[1024,128]{1,0:T(8,128)S(1)}, f32[1024,128]{1,0:T(8,128)S(1)}) fusion(f32[128]{0:T(128)} %constant.61.clone, f32[1024]{0:T(1024)S(1)} %convert_reduce_fusion.1), kind=kLoop, calls=%fused_computation.4 | loop fusion | flops 131072 | bytes 1053184 | tf_op jit(solution)/shard_map/sin | solution.py:48
  38.3 1.2 collective-permute-start.15
  39.5 7.6 %attention_first.1 = (bf16[1024,512]{1,0:T(8,128)(2,1)S(1)}, bf16[1024,512]{1,0:T(8,128)(2,1)S(1)}, bf16[1024,512]{1,0:T(8,128)(2,1)S(1)}, bf16[1024,512]{1,0:T(...) custom-call(s32[5]{0:T(128)S(1)} %stack.53.where_ref.unused, ...), custom_call_target="tpu_custom_call" | custom-call | flops 34359738368 | bytes 85899344 | tf_op jit(solution)/shard_map/attention_first/pallas_call | solution.py:69
  47.2 6.5 %attention_second.1 = (bf16[256,512]{1,0:T(8,128)(2,1)S(1)}, bf16[128,512]{1,0:T(8,128)(2,1)S(1)}, bf16[1024,128]{1,0:T(8,128)(2,1)S(1)}, bf16[1024,256]{1,0:T(8...) custom-call(s32[5]{0:T(128)S(1)} %stack.53.where_ref.unused, ...), custom_call_target="tpu_custom_call" | custom-call | flops 34359738368 | bytes 85899344 | tf_op jit(solution)/shard_map/attention_second/pallas_call | solution.py:69
  54.1 5.3 %feed_forward.1 = (bf16[1024,512]{1,0:T(8,128)(2,1)S(1)}, bf16[1024,512]{1,0:T(8,128)(2,1)S(1)}, bf16[4,512,128]{2,1,0:T(8,128)(2,1)S(1)}, f32[4,512,128]{2,1,0:T(8,128)S(1)}, f32[8,512]{1,0:T(8,128)S(1)}) custom-call(s32[5]{0:T(128)S(1)} %stack.53.where_ref.unused, bf16[1024,512]{1,0:T(8,128)(2,1)S(1)} %get-tuple-element.74.n2_ref, ...), custom_call_target="tpu_custom_call" | custom-call | flops 34359738368 | bytes 85899344 | tf_op jit(solution)/shard_map/feed_forward/pallas_call | solution.py:69
  60.2 2.9 %join.1 = (bf16[2,2,256,512]{3,2,1,0:T(8,128)(2,1)}, f32[2,2,256,512]{3,2,1,0:T(8,128)S(1)}, f32[8,512]{1,0:T(8,128)S(1)}) custom-call(s32[5]{0:T(128)S(1)} %stack.53.where_ref.unused, bf16[1024,512]{1,0:T(8,128)(2,1)S(1)} %get-tuple-element.63.xhat_ref, f32[8,512]{1,0:T(8,128)S(1)} %get-tuple-element.62.norms_ref, ...), custom_call_target="tpu_custom_call" | custom-call | flops 34359738368 | bytes 85899344 | tf_op jit(solution)/shard_map/join/pallas_call | solution.py:69
  63.1 3.7 %collective-permute-start.16 = (bf16[2,2,256,512]{3,2,1,0:T(8,128)(2,1)}, bf16[2,2,256,512]{3,2,1,0:T(8,128)(2,1)}, u32[]{:S(2)}, u32[]{:S(2)}) collective-permute-start(bf16[2,2,256,512]{3,2,1,0:T(8,128)(2,1)} %get-tuple-element.80), channel_id=1, source_target_pairs={{0,8},{8,0},{16,24},{24,16},{1,9},{9,1},{17,25},{25,17},{2,10},{10... | collective-permute-start | bytes 3145736 | tf_op jit(solution)/shard_map/ppermute | solution.py:591
  69.6 1.2 collective-permute-start.19
  70.8 3.0 %convert_add_fusion = f32[2,2,256,512]{3,2,1,0:T(8,128)} fusion(f32[2,2,256,512]{3,2,1,0:T(8,128)S(1)} %get-tuple-element.79, bf16[2,2,256,512]{3,2,1,0:T(8,128)(2,1)} %collective-permute-done.16), kind=kLoop, calls=%fused_computation | loop fusion | flops 1048576 | bytes 5242880 | tf_op jit(solution)/shard_map/add | solution.py:730
  73.9 2.1 %fusion.14 = bf16[2,256,512]{2,1,0:T(8,128)(2,1)} fusion(f32[2,2,256,512]{3,2,1,0:T(8,128)} %convert_add_fusion), kind=kLoop, calls=%fused_computation.23 | loop fusion | bytes 1048576 | tf_op jit(solution)/shard_map/convert_element_type | solution.py:731
  75.9 4.1 %collective-permute-start.17 = (bf16[2,256,512]{2,1,0:T(8,128)(2,1)}, bf16[2,256,512]{2,1,0:T(8,128)(2,1)S(1)}, u32[]{:S(2)}, u32[]{:S(2)}) collective-permute-start(bf16[2,256,512]{2,1,0:T(8,128)(2,1)} %fusion.14), channel_id=1, source_target_pairs={{0,16},{8,24},{16,0},{24,8},{1,17},{9,25},{17,1},{25,9},{2,18},{10... | collective-permute-start | bytes 1572872 | tf_op jit(solution)/shard_map/ppermute | solution.py:591
  80.2 6.6 %collective-permute-done.19.mlp_come = bf16[4,512,128]{2,1,0:T(8,128)(2,1)S(1)} collective-permute-done((bf16[4,512,128]{2,1,0:T(8,128)(2,1)}, bf16[4,512,128]{2,1,0:T(8,128)(2,1)S(1)}, u32[]{:S(2)}, u32[]{:S(2)}) %collective-permute-start.19) | collective-permute-done | bytes 524320 | tf_op jit(solution)/shard_map/ppermute | solution.py:604
  86.8 1.2 merge.1
  88.6 9.2 %all-to-all-start.1 = ((f32[32,1,192]{2,1,0:T(1,128)}), f32[32,1,192]{2,1,0:T(1,128)S(1)}, u32[]{:S(2)}, u32[]{:S(2)}) async-start(f32[32,1,192]{2,1,0:T(1,128)} %all_to_all.10), calls=%async_computation.1 | async-start | bytes 65536 | tf_op jit(solution)/shard_map/all_to_all | solution.py:782
  97.8 3.0 %collective-permute-start.20 = (bf16[768,128]{1,0:T(8,128)(2,1)S(1)}, bf16[768,128]{1,0:T(8,128)(2,1)S(1)}, u32[]{:S(2)}, u32[]{:S(2)}) collective-permute-start(bf16[768,128]{1,0:T(8,128)(2,1)S(1)} %get-tuple-element.93), channel_id=1, source_target_pairs={{0,0},{1,1},{16,2},{17,3},{8,4},{9,5},{24,6},{25,7},{2,8},{3,9},{1... | collective-permute-start | bytes 589832 | tf_op jit(solution)/shard_map/ppermute | solution.py:611
  102.7 4.0 %collective-permute-start.23 = (bf16[768,128]{1,0:T(8,128)(2,1)S(1)}, bf16[768,128]{1,0:T(8,128)(2,1)S(1)}, u32[]{:S(2)}, u32[]{:S(2)}) collective-permute-start(bf16[768,128]{1,0:T(8,128)(2,1)S(1)} %get-tuple-element.96), channel_id=1, source_target_pairs={{6,0},{7,1},{22,2},{23,3},{14,4},{15,5},{30,6},{31,7},{4,8},{5,9},... | collective-permute-start | bytes 589832 | tf_op jit(solution)/shard_map/ppermute | solution.py:611
  108.5 5.2 %collective-permute-done.21.b_ref = bf16[768,128]{1,0:T(8,128)(2,1)S(1)} collective-permute-done((bf16[768,128]{1,0:T(8,128)(2,1)S(1)}, bf16[768,128]{1,0:T(8,128)(2,1)S(1)}, u32[]{:S(2)}, u32[]{:S(2)}) %collective-permute-start.21) | collective-permute-done | bytes 196640 | tf_op jit(solution)/shard_map/ppermute | solution.py:611
  114.6 14.0 %collective-permute-done.23.d_ref = bf16[768,128]{1,0:T(8,128)(2,1)S(1)} collective-permute-done((bf16[768,128]{1,0:T(8,128)(2,1)S(1)}, bf16[768,128]{1,0:T(8,128)(2,1)S(1)}, u32[]{:S(2)}, u32[]{:S(2)}) %collective-permute-start.23) | collective-permute-done | bytes 196640 | tf_op jit(solution)/shard_map/ppermute | solution.py:611
  128.6 1.3 collect.1
  129.9 1.4 %fusion = f32[2,256,512]{2,1,0:T(8,128)S(1)} fusion(f32[2,2,256,512]{3,2,1,0:T(8,128)} %convert_add_fusion, bf16[2,256,512]{2,1,0:T(8,128)(2,1)S(1)} %collective-permute-done.17), kind=kLoop, calls=%fused_computation.3 | loop fusion | flops 524288 | bytes 2621440 | tf_op jit(solution)/shard_map/add | solution.py:731
  131.7 1.1 fusion.13
  (82 shorter events, 13.6 us)
Async XLA Ops:
  0.7 38.8 %copy-start.3 = (bf16[1,256,512]{2,1,0:T(8,128)(2,1)S(1)}, bf16[1,256,512]{2,1,0:T(8,128)(2,1)}, u32[]{:S(2)}) copy-start(bf16[1,256,512]{2,1,0:T(8,128)(2,1)} %param.18) | copy-start | bytes 786436
  0.7 38.8 %copy-start = (bf16[1,256,512]{2,1,0:T(8,128)(2,1)S(1)}, bf16[1,256,512]{2,1,0:T(8,128)(2,1)}, u32[]{:S(2)}) copy-start(bf16[1,256,512]{2,1,0:T(8,128)(2,1)} %param.16) | copy-start | bytes 786436
  2.5 10.2 %collective-permute-start.9 = (bf16[256,128]{1,0:T(8,128)(2,1)}, bf16[256,128]{1,0:T(8,128)(2,1)S(1)}, u32[]{:S(2)}, u32[]{:S(2)}) collective-permute-start(bf16[256,128]{1,0:T(8,128)(2,1)} %get-tuple-element.58), channel_id=1, source_target_pairs={{0,6},{1,7},{2,22},{3,23},{4,14},{5,15},{6,30},{7,31},{8,4},{9,5},... | collective-permute-start | bytes 196616 | tf_op jit(solution)/shard_map/ppermute | solution.py:607
  5.5 14.6 %collective-permute-start.8 = (bf16[256,128]{1,0:T(8,128)(2,1)}, bf16[256,128]{1,0:T(8,128)(2,1)S(1)}, u32[]{:S(2)}, u32[]{:S(2)}) collective-permute-start(bf16[256,128]{1,0:T(8,128)(2,1)} %get-tuple-element.58), channel_id=1, source_target_pairs={{0,4},{1,5},{2,20},{3,21},{4,12},{5,13},{6,28},{7,29},{8,6},{9,7},... | collective-permute-start | bytes 196616 | tf_op jit(solution)/shard_map/ppermute | solution.py:607
  5.7 17.5 %collective-permute-start.7 = (bf16[256,128]{1,0:T(8,128)(2,1)}, bf16[256,128]{1,0:T(8,128)(2,1)S(1)}, u32[]{:S(2)}, u32[]{:S(2)}) collective-permute-start(bf16[256,128]{1,0:T(8,128)(2,1)} %get-tuple-element.58), channel_id=1, source_target_pairs={{0,2},{1,3},{2,18},{3,19},{4,10},{5,11},{6,26},{7,27},{8,0},{9,1},... | collective-permute-start | bytes 196616 | tf_op jit(solution)/shard_map/ppermute | solution.py:607
  10.7 12.8 %collective-permute-start.6 = (bf16[256,128]{1,0:T(8,128)(2,1)}, bf16[256,128]{1,0:T(8,128)(2,1)S(1)}, u32[]{:S(2)}, u32[]{:S(2)}) collective-permute-start(bf16[256,128]{1,0:T(8,128)(2,1)} %get-tuple-element.58), channel_id=1, source_target_pairs={{0,0},{1,1},{2,16},{3,17},{4,8},{5,9},{6,24},{7,25},{8,2},{9,3},{1... | collective-permute-start | bytes 196616 | tf_op jit(solution)/shard_map/ppermute | solution.py:607
  12.6 21.6 %collective-permute-start.4 = (bf16[256,512]{1,0:T(8,128)(2,1)}, bf16[256,512]{1,0:T(8,128)(2,1)S(1)}, u32[]{:S(2)}, u32[]{:S(2)}) collective-permute-start(bf16[256,512]{1,0:T(8,128)(2,1)} %bitcast.43), channel_id=1, source_target_pairs={{0,16},{8,24},{16,0},{24,8},{1,17},{9,25},{17,1},{25,9},{2,18},{10... | collective-permute-start | bytes 786440 | tf_op jit(solution)/shard_map/ppermute | solution.py:591
  12.7 21.9 %collective-permute-start.1 = (bf16[256,512]{1,0:T(8,128)(2,1)}, bf16[256,512]{1,0:T(8,128)(2,1)S(1)}, u32[]{:S(2)}, u32[]{:S(2)}) collective-permute-start(bf16[256,512]{1,0:T(8,128)(2,1)} %bitcast.40), channel_id=1, source_target_pairs={{0,16},{8,24},{16,0},{24,8},{1,17},{9,25},{17,1},{25,9},{2,18},{10... | collective-permute-start | bytes 786440 | tf_op jit(solution)/shard_map/ppermute | solution.py:591
  14.1 15.6 %all-to-all-start = ((bf16[32,8,128]{2,1,0:T(8,128)(2,1)}), bf16[32,8,128]{2,1,0:T(8,128)(2,1)S(1)}, u32[]{:S(2)}, u32[]{:S(2)}) async-start(bf16[32,8,128]{2,1,0:T(8,128)(2,1)} %get-tuple-element.59), calls=%async_computation | async-start | bytes 131072 | tf_op jit(solution)/shard_map/all_to_all | solution.py:681
  20.2 10.8 %collective-permute-start.14 = (bf16[512,128]{1,0:T(8,128)(2,1)}, bf16[512,128]{1,0:T(8,128)(2,1)S(1)}, u32[]{:S(2)}, u32[]{:S(2)}) collective-permute-start(bf16[512,128]{1,0:T(8,128)(2,1)} %get-tuple-element.75), channel_id=1, source_target_pairs={{0,6},{1,7},{2,22},{3,23},{4,14},{5,15},{6,30},{7,31},{8,4},{9,5},... | collective-permute-start | bytes 393224 | tf_op jit(solution)/shard_map/ppermute | solution.py:607
  23.2 9.7 %collective-permute-start.13 = (bf16[512,128]{1,0:T(8,128)(2,1)}, bf16[512,128]{1,0:T(8,128)(2,1)S(1)}, u32[]{:S(2)}, u32[]{:S(2)}) collective-permute-start(bf16[512,128]{1,0:T(8,128)(2,1)} %get-tuple-element.75), channel_id=1, source_target_pairs={{0,4},{1,5},{2,20},{3,21},{4,12},{5,13},{6,28},{7,29},{8,6},{9,7},... | collective-permute-start | bytes 393224 | tf_op jit(solution)/shard_map/ppermute | solution.py:607
  23.5 10.5 %collective-permute-start.12 = (bf16[512,128]{1,0:T(8,128)(2,1)}, bf16[512,128]{1,0:T(8,128)(2,1)S(1)}, u32[]{:S(2)}, u32[]{:S(2)}) collective-permute-start(bf16[512,128]{1,0:T(8,128)(2,1)} %get-tuple-element.75), channel_id=1, source_target_pairs={{0,2},{1,3},{2,18},{3,19},{4,10},{5,11},{6,26},{7,27},{8,0},{9,1},... | collective-permute-start | bytes 393224 | tf_op jit(solution)/shard_map/ppermute | solution.py:607
  30.9 6.9 %collective-permute-start.11 = (bf16[512,128]{1,0:T(8,128)(2,1)}, bf16[512,128]{1,0:T(8,128)(2,1)S(1)}, u32[]{:S(2)}, u32[]{:S(2)}) collective-permute-start(bf16[512,128]{1,0:T(8,128)(2,1)} %get-tuple-element.75), channel_id=1, source_target_pairs={{0,0},{1,1},{2,16},{3,17},{4,8},{5,9},{6,24},{7,25},{8,2},{9,3},{1... | collective-permute-start | bytes 393224 | tf_op jit(solution)/shard_map/ppermute | solution.py:607
  32.9 5.4 %collective-permute-start.3 = (bf16[256,512]{1,0:T(8,128)(2,1)}, bf16[256,512]{1,0:T(8,128)(2,1)S(1)}, u32[]{:S(2)}, u32[]{:S(2)}) collective-permute-start(bf16[256,512]{1,0:T(8,128)(2,1)} %bitcast.44), channel_id=1, source_target_pairs={{0,8},{8,0},{16,24},{24,16},{1,9},{9,1},{17,25},{25,17},{2,10},{10... | collective-permute-start | bytes 786440 | tf_op jit(solution)/shard_map/ppermute | solution.py:591
  34.1 5.4 %collective-permute-start = (bf16[256,512]{1,0:T(8,128)(2,1)}, bf16[256,512]{1,0:T(8,128)(2,1)S(1)}, u32[]{:S(2)}, u32[]{:S(2)}) collective-permute-start(bf16[256,512]{1,0:T(8,128)(2,1)} %bitcast.41), channel_id=1, source_target_pairs={{0,8},{8,0},{16,24},{24,16},{1,9},{9,1},{17,25},{25,17},{2,10},{10... | collective-permute-start | bytes 786440 | tf_op jit(solution)/shard_map/ppermute | solution.py:591
  34.2 5.3 %collective-permute-start.5 = (bf16[256,512]{1,0:T(8,128)(2,1)S(1)}, bf16[256,512]{1,0:T(8,128)(2,1)S(1)}, u32[]{:S(2)}, u32[]{:S(2)}) collective-permute-start(bf16[256,512]{1,0:T(8,128)(2,1)S(1)} %collective-permute-done.4.cot2_ref), channel_id=1, source_target_pairs={{0,8},{8,0},{16,24},{24,16},{1,9},{9,1},{17,25},{25,17},{2,10},{10... | collective-permute-start | bytes 786440 | tf_op jit(solution)/shard_map/ppermute | solution.py:591
  34.6 4.9 %collective-permute-start.2 = (bf16[256,512]{1,0:T(8,128)(2,1)S(1)}, bf16[256,512]{1,0:T(8,128)(2,1)S(1)}, u32[]{:S(2)}, u32[]{:S(2)}) collective-permute-start(bf16[256,512]{1,0:T(8,128)(2,1)S(1)} %collective-permute-done.1.x2_ref), channel_id=1, source_target_pairs={{0,8},{8,0},{16,24},{24,16},{1,9},{9,1},{17,25},{25,17},{2,10},{10... | collective-permute-start | bytes 786440 | tf_op jit(solution)/shard_map/ppermute | solution.py:591
  37.9 9.3 %collective-permute-start.10 = (bf16[4,256,128]{2,1,0:T(8,128)(2,1)S(1)}, bf16[4,256,128]{2,1,0:T(8,128)(2,1)S(1)}, u32[]{:S(2)}, u32[]{:S(2)}) collective-permute-start(bf16[4,256,128]{2,1,0:T(8,128)(2,1)S(1)} %pad_maximum_fusion.1.slots_ref), channel_id=1, source_target_pairs={{0,1},{1,0},{2,3},{3,2},{4,5},{5,4},{6,7},{7,6},{8,9},{9,8},{10,11... | collective-permute-start | bytes 786440 | tf_op jit(solution)/shard_map/ppermute | solution.py:604
  38.3 15.8 %collective-permute-start.15 = (bf16[4,512,128]{2,1,0:T(8,128)(2,1)S(1)}, bf16[4,512,128]{2,1,0:T(8,128)(2,1)S(1)}, u32[]{:S(2)}, u32[]{:S(2)}) collective-permute-start(bf16[4,512,128]{2,1,0:T(8,128)(2,1)S(1)} %pad_maximum_fusion.own_ref), channel_id=1, source_target_pairs={{0,1},{1,0},{2,3},{3,2},{4,5},{5,4},{6,7},{7,6},{8,9},{9,8},{10,11... | collective-permute-start | bytes 1572872 | tf_op jit(solution)/shard_map/ppermute | solution.py:604
  47.1 6.5 %copy-start.1 = (f32[4,256,128]{2,1,0:T(8,128)}, f32[4,256,128]{2,1,0:T(8,128)S(1)}, u32[]{:S(2)}) copy-start(f32[4,256,128]{2,1,0:T(8,128)S(1)} %get-tuple-element.85.att_keep) | copy-start | bytes 1572868
  53.7 5.7 %copy-start.6 = (bf16[4,256,128]{2,1,0:T(8,128)(2,1)}, bf16[4,256,128]{2,1,0:T(8,128)(2,1)S(1)}, u32[]{:S(2)}) copy-start(bf16[4,256,128]{2,1,0:T(8,128)(2,1)S(1)} %get-tuple-element.86) | copy-start | bytes 786436
  63.1 7.7 %collective-permute-start.16 = (bf16[2,2,256,512]{3,2,1,0:T(8,128)(2,1)}, bf16[2,2,256,512]{3,2,1,0:T(8,128)(2,1)}, u32[]{:S(2)}, u32[]{:S(2)}) collective-permute-start(bf16[2,2,256,512]{3,2,1,0:T(8,128)(2,1)} %get-tuple-element.80), channel_id=1, source_target_pairs={{0,8},{8,0},{16,24},{24,16},{1,9},{9,1},{17,25},{25,17},{2,10},{10... | collective-permute-start | bytes 3145736 | tf_op jit(solution)/shard_map/ppermute | solution.py:591
  67.4 12.8 %collective-permute-start.18 = (bf16[4,256,128]{2,1,0:T(8,128)(2,1)}, bf16[4,256,128]{2,1,0:T(8,128)(2,1)}, u32[]{:S(2)}, u32[]{:S(2)}) collective-permute-start(bf16[4,256,128]{2,1,0:T(8,128)(2,1)} %copy-done.6), channel_id=1, source_target_pairs={{0,1},{1,0},{2,3},{3,2},{4,5},{5,4},{6,7},{7,6},{8,9},{9,8},{10,11... | collective-permute-start | bytes 786440 | tf_op jit(solution)/shard_map/ppermute | solution.py:604
  69.6 17.2 %collective-permute-start.19 = (bf16[4,512,128]{2,1,0:T(8,128)(2,1)}, bf16[4,512,128]{2,1,0:T(8,128)(2,1)S(1)}, u32[]{:S(2)}, u32[]{:S(2)}) collective-permute-start(bf16[4,512,128]{2,1,0:T(8,128)(2,1)} %copy-done.5), channel_id=1, source_target_pairs={{0,1},{1,0},{2,3},{3,2},{4,5},{5,4},{6,7},{7,6},{8,9},{9,8},{10,11... | collective-permute-start | bytes 1572872 | tf_op jit(solution)/shard_map/ppermute | solution.py:604
  70.8 16.0 %copy-start.2 = (f32[4,256,128]{2,1,0:T(8,128)S(1)}, f32[4,256,128]{2,1,0:T(8,128)}, u32[]{:S(2)}) copy-start(f32[4,256,128]{2,1,0:T(8,128)} %copy-done.1) | copy-start | bytes 1572868
  75.9 54.0 %collective-permute-start.17 = (bf16[2,256,512]{2,1,0:T(8,128)(2,1)}, bf16[2,256,512]{2,1,0:T(8,128)(2,1)S(1)}, u32[]{:S(2)}, u32[]{:S(2)}) collective-permute-start(bf16[2,256,512]{2,1,0:T(8,128)(2,1)} %fusion.14), channel_id=1, source_target_pairs={{0,16},{8,24},{16,0},{24,8},{1,17},{9,25},{17,1},{25,9},{2,18},{10... | collective-permute-start | bytes 1572872 | tf_op jit(solution)/shard_map/ppermute | solution.py:591
  88.6 18.1 %all-to-all-start.1 = ((f32[32,1,192]{2,1,0:T(1,128)}), f32[32,1,192]{2,1,0:T(1,128)S(1)}, u32[]{:S(2)}, u32[]{:S(2)}) async-start(f32[32,1,192]{2,1,0:T(1,128)} %all_to_all.10), calls=%async_computation.1 | async-start | bytes 65536 | tf_op jit(solution)/shard_map/all_to_all | solution.py:782
  97.8 10.6 %collective-permute-start.20 = (bf16[768,128]{1,0:T(8,128)(2,1)S(1)}, bf16[768,128]{1,0:T(8,128)(2,1)S(1)}, u32[]{:S(2)}, u32[]{:S(2)}) collective-permute-start(bf16[768,128]{1,0:T(8,128)(2,1)S(1)} %get-tuple-element.93), channel_id=1, source_target_pairs={{0,0},{1,1},{16,2},{17,3},{8,4},{9,5},{24,6},{25,7},{2,8},{3,9},{1... | collective-permute-start | bytes 589832 | tf_op jit(solution)/shard_map/ppermute | solution.py:611
  100.9 12.7 %collective-permute-start.21 = (bf16[768,128]{1,0:T(8,128)(2,1)S(1)}, bf16[768,128]{1,0:T(8,128)(2,1)S(1)}, u32[]{:S(2)}, u32[]{:S(2)}) collective-permute-start(bf16[768,128]{1,0:T(8,128)(2,1)S(1)} %get-tuple-element.94), channel_id=1, source_target_pairs={{2,0},{3,1},{18,2},{19,3},{10,4},{11,5},{26,6},{27,7},{0,8},{1,9},... | collective-permute-start | bytes 589832 | tf_op jit(solution)/shard_map/ppermute | solution.py:611
  101.8 12.8 %collective-permute-start.22 = (bf16[768,128]{1,0:T(8,128)(2,1)S(1)}, bf16[768,128]{1,0:T(8,128)(2,1)S(1)}, u32[]{:S(2)}, u32[]{:S(2)}) collective-permute-start(bf16[768,128]{1,0:T(8,128)(2,1)S(1)} %get-tuple-element.95), channel_id=1, source_target_pairs={{4,0},{5,1},{20,2},{21,3},{12,4},{13,5},{28,6},{29,7},{6,8},{7,9},... | collective-permute-start | bytes 589832 | tf_op jit(solution)/shard_map/ppermute | solution.py:611
  102.7 25.9 %collective-permute-start.23 = (bf16[768,128]{1,0:T(8,128)(2,1)S(1)}, bf16[768,128]{1,0:T(8,128)(2,1)S(1)}, u32[]{:S(2)}, u32[]{:S(2)}) collective-permute-start(bf16[768,128]{1,0:T(8,128)(2,1)S(1)} %get-tuple-element.96), channel_id=1, source_target_pairs={{6,0},{7,1},{22,2},{23,3},{14,4},{15,5},{30,6},{31,7},{4,8},{5,9},... | collective-permute-start | bytes 589832 | tf_op jit(solution)/shard_map/ppermute | solution.py:611
  108.5 24.4 %copy-start.7 = (f32[16]{0:T(128)}, f32[16]{0:T(128)S(1)}, u32[]{:S(2)}) copy-start(f32[16]{0:T(128)S(1)} %get-tuple-element.142) | copy-start | bytes 196
  (2 other events, 2.6 us)

commit v4 on v3

--- a/solution.py
+++ b/solution.py
@@ -48,7 +48,7 @@
     return jnp.cos(angles), jnp.sin(angles)
 
 
-VMEM_LIMIT = 24 << 20
+VMEM_LIMIT = 14 << 20
 
 
 def roll(value, shift):
@@ -65,43 +65,76 @@
 LINES = 8
 
 
-def call(kernel, name, work, operands, results, scratch):
+ANY = pl.BlockSpec(memory_space=pl.ANY)
+HBM = pl.BlockSpec(memory_space=pltpu.HBM)
+
+
+def call_streamed(kernel, name, work, operands, results):
+    def body(*refs):
+        count = len(operands)
+        sources, outs, held, sems = refs[:count], refs[count:-count - 1], refs[-count - 1 : -1], refs[-1]
+        wait_all(start_all(list(zip(sources, held)), sems))
+        kernel(*held, *outs)
+
+    return pl.pallas_call(
+        body,
+        out_shape=results,
+        in_specs=[HBM] * len(operands),
+        out_specs=[VMEM] * len(results),
+        scratch_shapes=[pltpu.VMEM(v.shape, v.dtype) for v in operands]
+        + [pltpu.SemaphoreType.DMA((len(operands),))],
+        compiler_params=pltpu.CompilerParams(vmem_limit_bytes=12 << 20),
+        cost_estimate=pl.CostEstimate(flops=work, bytes_accessed=work // 400, transcendentals=0),
+        name=name,
+    )(*operands)
+
+
+def call(kernel, name, work, operands, results, scratch, far=(), copies=0, held=(), limit=VMEM_LIMIT):
+    places = [HBM if any(v is w for w in far) else VMEM for v in operands[1:]]
     return pl.pallas_call(
         kernel,
         out_shape=results,
-        in_specs=[SMEM] + [VMEM] * (len(operands) - 1),
+        in_specs=[SMEM] + places,
         out_specs=[VMEM] * len(results),
-        scratch_shapes=[pltpu.VMEM(size, dtype) for size, dtype in scratch],
-        compiler_params=pltpu.CompilerParams(vmem_limit_bytes=VMEM_LIMIT),
+        scratch_shapes=[pltpu.VMEM(size, dtype) for size, dtype in scratch]
+        + [pltpu.SemaphoreType.DMA((copies,))] * (copies > 0)
+        + [v for size, dtype in held for v in (pltpu.VMEM(size, dtype), pltpu.SemaphoreType.DMA(size[:1]))],
+        compiler_params=pltpu.CompilerParams(vmem_limit_bytes=limit),
         cost_estimate=pl.CostEstimate(flops=work, bytes_accessed=work // 400, transcendentals=0),
         name=name,
     )(*operands)
 
 
-def fetch_in(sources, held, sems):
+def start_all(moves, sems):
     copies = [
-        pltpu.make_async_copy(source, target, sems.at[i])
-        for i, (source, target) in enumerate(zip(sources, held))
+        pltpu.make_async_copy(source, target, sems.at[i]) for i, (source, target) in enumerate(moves)
     ]
     for copy in copies:
         copy.start()
+    return copies
+
+
+def wait_all(copies):
     for copy in copies:
         copy.wait()
 
 
 def prepare_kernel(paired, *refs):
-    sources, (small_ref, *packs), held = refs[:13], refs[13 : 14 + 2 * paired], refs[14 + 2 * paired :]
-    line, sems = held[13], held[14]
-    fetch_in(sources, held, sems)
-    seg_ref, project_ref, mix_ref, up_ref, down_ref, *vectors = held[:13]
+    sources, (small_ref, act_ref, *packs) = refs[:15], refs[15 : 17 + paired]
+    *held, line, sems = refs[17 + paired :]
+    moves = list(zip(sources[2:], held[2:]))
+    moves += [(sources[0], act_ref.at[0]), (sources[1], act_ref.at[1])]
+    copies = start_all(moves, sems)
+    line[...] = jnp.zeros(line.shape, F32)
+    wait_all(copies)
+    unused, unused, seg_ref, project_ref, mix_ref, up_ref, down_ref, *vectors = held
     if paired:
-        att, mlp = packs
-        att[0:192, :] = project_ref[...]
-        att[192:256, :] = mix_ref[...]
-        mlp[0:128, :] = up_ref[:, 0:128]
-        mlp[128:256, :] = up_ref[:, 128:256]
-        mlp[256:512, :] = down_ref[...]
-    line[...] = jnp.zeros(line.shape, F32)
+        pack = packs[0]
+        pack[0:192, :] = project_ref[...]
+        pack[192:256, :] = mix_ref[...]
+        pack[256:384, :] = up_ref[:, 0:128]
+        pack[384:512, :] = up_ref[:, 128:256]
+        pack[512:768, :] = down_ref[...]
     part = vectors[0].shape[1]
     for i in range(6):
         line[0:1, i * part : (i + 1) * part] = vectors[i][...].astype(F32)
@@ -122,7 +155,7 @@
     return pl.pallas_call(
         kernel,
         out_shape=results,
-        in_specs=[pl.BlockSpec(memory_space=pl.ANY)] * len(sources),
+        in_specs=[HBM] * len(sources),
         out_specs=[VMEM] * len(results),
         scratch_shapes=[pltpu.VMEM(v.shape, v.dtype) for v in sources]
         + scratch
@@ -187,7 +220,10 @@
     n2_ref,
     xhat_ref,
     cot_ref,
-    own_ref,
+    own0_ref,
+    own1_ref,
+    own2_ref,
+    own3_ref,
     oth_ref,
     norms_ref,
     shift_ref,
@@ -202,20 +238,27 @@
     dh_s,
     ug_s,
     dg_s,
+    sems,
 ):
     r, key = where_ref[0], where_ref[1]
     count = n2_ref.shape[0] // 4
     gain = norms_ref[2:3, :]
+    owns, others = (own0_ref, own1_ref, own2_ref, own3_ref), [oth_ref.at[k] for k in range(4)]
+    moves = []
     for k in range(4):
         g = pl.multiple_of((key ^ k) * 128, 128)
-        for h, ref in enumerate((own_ref, oth_ref)):
-            b = ref.shape[1] - 512
-            up_s[pl.ds(g, 128), h * 256 : h * 256 + 128] = ref[k, b : b + 128]
-            up_s[pl.ds(g, 128), h * 256 + 128 : h * 256 + 256] = ref[k, b + 128 : b + 256]
-            down_s[h * 256 : h * 256 + 256, pl.ds(g, 128)] = ref[k, b + 256 : b + 512]
+        for h, ref in enumerate((owns[k], others[k])):
+            b = ref.shape[0] - 512
+            left, right = pl.ds(h * 256, 128), pl.ds(h * 256 + 128, 128)
+            moves += [
+                (ref.at[pl.ds(b, 128)], up_s.at[pl.ds(g, 128), left]),
+                (ref.at[pl.ds(b + 128, 128)], up_s.at[pl.ds(g, 128), right]),
+                (ref.at[pl.ds(b + 256, 256)], down_s.at[pl.ds(h * 256, 256), pl.ds(g, 128)]),
+            ]
+    wait_all(start_all(moves, sems))
     up, down = up_s[...], down_s[...]
     shift = shift_ref[...]
-    sums = [jnp.zeros((1, up.shape[1]), F32)] * 3
+    shift_sum = jnp.zeros((1, up.shape[1]), F32)
     for t in range(4):
         at = slice(t * count, t * count + count)
         hidden = dot(n2_ref[at, :], up) + shift
@@ -226,17 +269,18 @@
         out_ref[at, :] = dot(active, down).astype(BF)
         d_hidden = (dot(cot_ref[at, :], down, ((1,), (1,))) * slope).astype(BF)
         dh_s[at, :] = d_hidden
-        d_second = dot(d_hidden, up, ((1,), (1,)))
-        e_ref[at, :] = (d_second * gain).astype(BF)
-        sums[0] += jnp.sum(d_hidden.astype(F32), axis=0, keepdims=True)
-        sums[1] += jnp.sum(d_second * xhat_ref[at, :].astype(F32), axis=0, keepdims=True)
-        sums[2] += jnp.sum(d_second, axis=0, keepdims=True)
+        e_ref[at, :] = (dot(d_hidden, up, ((1,), (1,))) * gain).astype(BF)
+        shift_sum += jnp.sum(d_hidden.astype(F32), axis=0, keepdims=True)
     mine = cot_ref[pl.ds(pl.multiple_of(r * count, count), count), :]
-    sums.append(jnp.sum(mine.astype(F32), axis=0, keepdims=True))
-    for i, row in enumerate(sums):
-        small_ref[i : i + 1, :] = row
-    small_ref[4:8, :] = jnp.zeros((4, small_ref.shape[1]), F32)
-    ug_s[...] = dot(n2_ref[...], dh_s[...], ((0,), (0,)))
+    product = dot(dh_s[...], xhat_ref[...], ((0,), (0,)))
+    weights = jnp.transpose(up.astype(F32))
+    across = jnp.transpose(jnp.broadcast_to(shift_sum, (8, up.shape[1])))[:, 0:1]
+    small_ref[...] = jnp.zeros(small_ref.shape, F32)
+    small_ref[0:1, :] = shift_sum
+    small_ref[1:2, :] = jnp.sum(weights * product, axis=0, keepdims=True)
+    small_ref[2:3, :] = jnp.sum(weights * across, axis=0, keepdims=True)
+    small_ref[3:4, :] = jnp.sum(mine.astype(F32), axis=0, keepdims=True)
+    ug_s[...] = jnp.transpose(product * gain + across * norms_ref[3:4, :])
     dg_s[...] = dot(act_s[...], cot_ref[...], ((0,), (0,)))
     for k in range(4):
         g = pl.multiple_of((key ^ k) * 128, 128)
@@ -253,12 +297,12 @@
         mlp_kernel,
         "feed_forward",
         1 << 35,
-        (where, n2, xhat, cot, own, oth, norms, shift),
+        (where, n2, xhat, cot, *own, *oth, norms, shift),
         (
             SHAPE((tall, width), BF),
             SHAPE((tall, width), BF),
-            SHAPE(oth.shape, BF),
-            SHAPE(oth.shape, F32),
+            SHAPE((4, 512, 128), BF),
+            SHAPE((4, 512, 128), F32),
             SHAPE((8, wide), F32),
         ),
         (
@@ -269,20 +313,16 @@
             ((width, wide), F32),
             ((wide, width), F32),
         ),
-    )
-
-
-def head(key, n1_ref, cot_ref, slots_ref, shift, cos_ref, sin_ref, starts_ref, w, mix, ctx, dp, grads_ref, scratch):
-    q_s, qh_s, k_s, v_s, dctx_s, dq_s, dt_s, pg_s, mg_s = scratch
+        (*own, *oth),
+        24,
+    )
+
+
+def head(key, n1_ref, xhat_ref, cot_ref, norms_ref, shift, cos_ref, sin_ref, starts_ref, w, mix, ctx, dp, grads_ref, scratch):
+    q_s, qh_s, k_s, v_s, dctx_s, dq_s, dt_s, pg_s, mg_s, unused = scratch
     tall = n1_ref.shape[0]
     count = tall // 4
     scaling = HD**-0.5
-    w[192:256, :] = jnp.zeros((64, w.shape[1]), BF)
-    mix[64:128, :] = jnp.zeros((64, mix.shape[1]), BF)
-    for k in range(4):
-        g = pl.multiple_of((key ^ k) * 128, 128)
-        w[0:192, pl.ds(g, 128)] = slots_ref[k, 0:192]
-        mix[0:64, pl.ds(g, 128)] = slots_ref[k, 192:256]
     lane = lanes_of((count, 128))
     left = lane < 64
     first, second = lane % 64 < ROT // 2, lane % 64 < ROT
@@ -332,13 +372,32 @@
         dp[at, 0:128] = qk.astype(BF)
         dp[at, 128:256] = turned[:, 128:].astype(BF)
         shift_sum += jnp.sum(dp[at, :].astype(F32), axis=0, keepdims=True)
-    pg_s[...] = dot(dp[...], n1_ref[...], ((0,), (0,)))
+    product = dot(dp[...], xhat_ref[...], ((0,), (0,)))
+    weights = w[...].astype(F32)
+    across = jnp.transpose(jnp.broadcast_to(shift_sum, (8, 256)))[:, 0:1]
+    gain_sum = jnp.sum(weights * product, axis=0, keepdims=True)
+    bias_sum = jnp.sum(weights * across, axis=0, keepdims=True)
+    pg_s[...] = product * norms_ref[0:1, :] + across * norms_ref[1:2, :]
     mg_s[...] = dot(ctx[...], cot_ref[...], ((0,), (0,)))
     for k in range(4):
         g = pl.multiple_of((key ^ k) * 128, 128)
         grads_ref[k, 0:192] = pg_s[0:192, pl.ds(g, 128)].astype(grads_ref.dtype)
         grads_ref[k, 192:256] = mg_s[0:64, pl.ds(g, 128)].astype(grads_ref.dtype)
-    return shift_sum
+    return shift_sum, gain_sum, bias_sum
+
+
+def fetch_head(key, slots, w, mix, sems):
+    moves = []
+    for k in range(4):
+        g = pl.multiple_of((key ^ k) * 128, 128)
+        moves += [
+            (slots[k].at[pl.ds(0, 192)], w.at[pl.ds(0, 192), pl.ds(g, 128)]),
+            (slots[k].at[pl.ds(192, 64)], mix.at[pl.ds(0, 64), pl.ds(g, 128)]),
+        ]
+    copies = start_all(moves, sems)
+    w[192:256, :] = jnp.zeros((64, w.shape[1]), BF)
+    mix[64:128, :] = jnp.zeros((64, mix.shape[1]), BF)
+    return copies
 
 
 def head_scratch(tall, width):
@@ -357,15 +416,14 @@
 
 def first_kernel(
     where_ref,
-    x0_ref,
-    x1_ref,
-    x2_ref,
-    x3_ref,
-    cot0_ref,
-    cot1_ref,
-    cot2_ref,
-    cot3_ref,
-    slots_ref,
+    act0_ref,
+    act1_ref,
+    act2_ref,
+    act3_ref,
+    slot0_ref,
+    slot1_ref,
+    slot2_ref,
+    slot3_ref,
     shift_ref,
     cos_ref,
     sin_ref,
@@ -384,22 +442,30 @@
     *scratch,
 ):
     r, key = where_ref[0], where_ref[1]
-    count = x0_ref.shape[0]
+    *scratch, act_s, act_sems = scratch
+    count = act0_ref.shape[1]
     norms = norms_ref[...]
-    grads_in = (cot0_ref, cot1_ref, cot2_ref, cot3_ref)
-    for j, source in enumerate((x0_ref, x1_ref, x2_ref, x3_ref)):
+    moves = [(act0_ref, act_s.at[0]), (act1_ref, act_s.at[1])]
+    moves += [(act2_ref, act_s.at[2]), (act3_ref, act_s.at[3])]
+    fetched = start_all(moves, act_sems)
+    copies = fetch_head(key, (slot0_ref, slot1_ref, slot2_ref, slot3_ref), w_ref, mix_ref, scratch[-1])
+    for j in range(4):
+        fetched[j].wait()
+        source = act_s.at[j]
         at = pl.ds(pl.multiple_of((r ^ j) * count, count), count)
-        hat, unused = normalize(source[...].astype(F32))
+        hat, unused = normalize(source[0].astype(F32))
         xhat_ref[at, :] = hat.astype(BF)
         n1_ref[at, :] = (hat * norms[0:1] + norms[1:2]).astype(BF)
         n2_ref[at, :] = (hat * norms[2:3] + norms[3:4]).astype(BF)
-        cot_ref[at, :] = grads_in[j][...]
+        cot_ref[at, :] = source[1]
+    wait_all(copies)
     small_ref[...] = jnp.zeros(small_ref.shape, F32)
-    small_ref[0:1, 0:256] = head(
+    small_ref[0:1, 0:256], small_ref[1:2, :], small_ref[2:3, :] = head(
         key,
         n1_ref,
+        xhat_ref,
         cot_ref,
-        slots_ref,
+        norms_ref,
         shift_ref[0:1, :],
         cos_ref,
         sin_ref,
@@ -414,13 +480,13 @@
 
 
 def run_first(where, chunks, slots, shift, cosine, sine, starts, norms):
-    count, width = chunks[0].shape
+    count, width = chunks[0].shape[1:]
     tall = 4 * count
     return call(
         first_kernel,
         "attention_first",
         1 << 35,
-        (where, *chunks, slots, shift, cosine, sine, starts, norms),
+        (where, *chunks, *slots, shift, cosine, sine, starts, norms),
         (
             SHAPE((tall, width), BF),
             SHAPE((tall, width), BF),
@@ -434,18 +500,24 @@
             SHAPE((8, width), F32),
         ),
         head_scratch(tall, width),
+        (*slots, *chunks),
+        8,
+        (((4, 2, count, width), BF),),
+        14 << 20,
     )
 
 
 def second_kernel(
     where_ref,
     n1_ref,
+    xhat_ref,
     cot_ref,
     slots_ref,
     shift_ref,
     cos_ref,
     sin_ref,
     starts_ref,
+    norms_ref,
     w_ref,
     mix_ref,
     ctx_ref,
@@ -454,12 +526,14 @@
     small_ref,
     *scratch,
 ):
+    wait_all(fetch_head(where_ref[1], [slots_ref.at[k] for k in range(4)], w_ref, mix_ref, scratch[-1]))
     small_ref[...] = jnp.zeros(small_ref.shape, F32)
-    small_ref[0:1, 0:256] = head(
+    small_ref[0:1, 0:256], small_ref[1:2, :], small_ref[2:3, :] = head(
         where_ref[1],
         n1_ref,
+        xhat_ref,
         cot_ref,
-        slots_ref,
+        norms_ref,
         shift_ref[1:2, :],
         cos_ref,
         sin_ref,
@@ -473,13 +547,13 @@
     )
 
 
-def run_second(where, n1, cot, slots, shift, cosine, sine, starts):
+def run_second(where, n1, xhat, cot, slots, shift, cosine, sine, starts, norms):
     tall, width = n1.shape
     return call(
         second_kernel,
         "attention_second",
         1 << 35,
-        (where, n1, cot, slots, shift, cosine, sine, starts),
+        (where, n1, xhat, cot, *slots, shift, cosine, sine, starts, norms),
         (
             SHAPE((256, width), BF),
             SHAPE((128, width), BF),
@@ -489,12 +563,13 @@
             SHAPE((8, width), F32),
         ),
         head_scratch(tall, width),
+        slots,
+        8,
     )
 
 
 def join_kernel(
     where_ref,
-    xhat_ref,
     norms_ref,
     w_a,
     mix_a,
@@ -508,50 +583,106 @@
     e_in,
     near_ref,
     rest_ref,
-    small_ref,
 ):
     r = where_ref[0]
-    count = xhat_ref.shape[0] // 4
-    sums = [jnp.zeros((1, xhat_ref.shape[1]), F32)] * 2
+    count = ctx_a.shape[0] // 4
     gain = norms_ref[0:1, :]
     for j in range(4):
         at = pl.ds(pl.multiple_of((r ^ j) * count, count), count)
         d_first = dot(dp_a[at, :], w_a[...]) + dot(dp_b[at, :], w_b[...])
-        sums[0] += jnp.sum(d_first * xhat_ref[at, :].astype(F32), axis=0, keepdims=True)
-        sums[1] += jnp.sum(d_first, axis=0, keepdims=True)
         out = dot(ctx_a[at, :], mix_a[...]) + dot(ctx_b[at, :], mix_b[...])
         target = near_ref if j % 2 else rest_ref
         target[j // 2, 0] = (out_in[at, :].astype(F32) + out).astype(target.dtype)
         target[j // 2, 1] = (e_in[at, :].astype(F32) + d_first * gain).astype(target.dtype)
-    small_ref[...] = jnp.zeros(small_ref.shape, F32)
-    small_ref[0:1, :] = sums[0]
-    small_ref[1:2, :] = sums[1]
-
-
-def run_join(where, xhat, norms, first, second, out, e):
-    tall, width = xhat.shape
+
+
+def run_join(where, norms, first, second, out, e):
+    tall, width = out.shape
     count = tall // 4
     return call(
         join_kernel,
         "join",
-        1 << 35,
-        (where, xhat, norms, *first, *second, out, e),
+        1 << 24,
+        (where, norms, *first, *second, out, e),
         (
             SHAPE((2, 2, count, width), BF),
             SHAPE((2, 2, count, width), F32),
-            SHAPE((8, width), F32),
         ),
         (),
     )
 
 
-def merge_kernel(unused, att_keep, att_come, mlp_keep, mlp_come, *outs):
+def add_kernel(rest_ref, come_ref, mine_ref, onward_ref):
+    for i in range(2):
+        mine_ref[i] = rest_ref[0, i] + come_ref[0, i].astype(F32)
+        onward_ref[i] = (rest_ref[1, i] + come_ref[1, i].astype(F32)).astype(BF)
+
+
+def finish_kernel(x_ref, cot_ref, mine_ref, come_ref, norms_ref, output_ref, grad_ref):
+    x = x_ref[...].astype(F32)
+    out = mine_ref[0] + come_ref[0].astype(F32)
+    output_ref[...] = (x + out + norms_ref[4:5, :] + norms_ref[5:6, :]).astype(BF)
+    e = mine_ref[1] + come_ref[1].astype(F32)
+    xhat, root = normalize(x)
+    centred = e - jnp.mean(e, axis=-1, keepdims=True)
+    along = xhat * jnp.mean(e * xhat, axis=-1, keepdims=True)
+    grad_ref[...] = cot_ref[...].astype(F32) + root * (centred - along)
+
+
+def share_kernel(cols, sizes, where_ref, mlp_ref, own_ref, oth_ref, out_ref):
+    y, group = where_ref[3], where_ref[4]
+    part, project, up = sizes
+    copies = out_ref.shape[0]
+
+    def cut(row, device_of, lane_of):
+        wide = row.shape[1]
+        place = lax.broadcasted_iota(jnp.int32, (copies, wide), 1)
+        device = lax.broadcasted_iota(jnp.int32, (copies, wide), 0)
+        kept = jnp.where(device == device_of(place), row, 0.0)
+        place = lax.broadcasted_iota(jnp.int32, (wide, 128), 0)
+        lane = lax.broadcasted_iota(jnp.int32, (wide, 128), 1)
+        chosen = jnp.where(lane == lane_of(place), 1.0, 0.0)
+        return jnp.dot(kept, chosen, precision=lax.Precision.HIGHEST, preferred_element_type=F32)
+
+    rows = [own_ref[i : i + 1, :] + oth_ref[i : i + 1, :] for i in (1, 2)]
+    rows += [mlp_ref[i : i + 1, :] for i in (1, 2, 3)]
+    total = jnp.zeros((copies, 128), F32)
+    for i, row in enumerate(rows):
+        total += cut(row, lambda n: n // part, lambda n: i * part + n % part)
+    out_ref[...] = jnp.zeros(out_ref.shape, F32)
+    out_ref[:, 0, :] = total
+    half = cols // 2
+    heads, hidden = jnp.zeros((copies, 128), F32), jnp.zeros((copies, 128), F32)
+    for h, ref in enumerate((own_ref, oth_ref)):
+        begin = group * cols + (h ^ y) * half
+        heads += cut(
+            ref[0:1, 0:256],
+            lambda n: jnp.where(n < half * project, begin + n // project, -1),
+            lambda n: n % project,
+        )
+        hidden += cut(
+            mlp_ref[0:1, h * 256 : h * 256 + 256], lambda n: begin + n // up, lambda n: n % up
+        )
+    out_ref[:, 1, :] = heads
+    out_ref[:, 2, :] = hidden
+
+
+def small_kernel(unused, sums_ref, *outs):
+    total = jnp.sum(sums_ref[...], axis=0)
+    part = outs[0].shape[1]
+    for i in range(5):
+        outs[i][...] = total[0:1, i * part : (i + 1) * part]
+    outs[5][...] = total[1:2, 0 : outs[5].shape[1]]
+    outs[6][...] = total[2:3, 0 : outs[6].shape[1]]
+
+
+def merge_kernel(att_keep, att_come, mlp_keep, mlp_come, *outs):
     for k in range(4):
         outs[k][0:256, :] = (att_keep[k] + att_come[k].astype(F32)).astype(BF)
         outs[k][256:768, :] = (mlp_keep[k] + mlp_come[k].astype(F32)).astype(BF)
 
 
-def collect_kernel(unused, a_ref, b_ref, c_ref, d_ref, project_ref, mix_ref, up_ref, down_ref):
+def collect_kernel(a_ref, b_ref, c_ref, d_ref, project_ref, mix_ref, up_ref, down_ref):
     def total(begin, end):
         refs = (a_ref, b_ref, c_ref, d_ref)
         return sum(ref[begin:end, :].astype(F32) for ref in refs)
@@ -652,10 +783,6 @@
     part, project_len, up_len = first_gain.shape[0], project_bias.shape[0], up_bias.shape[0]
     copies = rows * cols
     x_own, cot_own = inputs[0], cotangent[0]
-    x_across, cot_across = flip(x_own, 2), flip(cot_own, 2)
-    x_far, cot_far = flip(x_own, 1), flip(cot_own, 1)
-    chunks = (x_own, x_far, x_across, flip(x_across, 1))
-    chunks += (cot_own, cot_far, cot_across, flip(cot_across, 1))
     vectors = (
         first_gain,
         first_bias,
@@ -666,23 +793,23 @@
         project_bias,
         up_bias,
     )
-    results = [SHAPE((copies, LINES, 128), BF)]
-    if paired:
-        results += [SHAPE((256, 128), BF), SHAPE((512, 128), BF)]
-    small, *packs = run_local(
+    results = [SHAPE((copies, LINES, 128), BF), SHAPE((2, count, width), BF)]
+    small, act, *packs = run_local(
         functools.partial(prepare_kernel, paired),
         "prepare",
         1 << 20,
-        (seg_start, project_weight.T, output_weight, up_weight, down_weight)
+        (x_own, cot_own, seg_start, project_weight.T, output_weight, up_weight, down_weight)
         + tuple(v[None] for v in vectors),
-        results,
+        results + [SHAPE((768, 128), BF)] * paired,
         [pltpu.VMEM((LINES, 128), F32)],
     )
+    across, far = flip(act, 2), flip(act, 1)
     every = lax.all_to_all(small, both, 0, 0, tiled=True)
     if paired:
-        att_own, mlp_own = jnp.stack(spread(packs[0])), jnp.stack(spread(packs[1]))
-        att_slots = att_own, beside(att_own)
-        mlp_slots = mlp_own, beside(mlp_own)
+        own = spread(packs[0])
+        mlp_slots = own, (beside(jnp.stack([v[256:] for v in own])),)
+        att_slots = own, (beside(jnp.stack([v[:256] for v in own])),)
+        every, across = lax.optimization_barrier((every, across))
     else:
         ups, downs = fetch_columns(up_weight), fetch_rows(down_weight)
         projects, mixes = fetch_columns(project_weight), fetch_rows(output_weight)
@@ -699,10 +826,11 @@
             for h in range(2)
         ]
 
+    chunks = (act, far, across, flip(across, 1))
     norms, project_shift, up_shift, starts = call(
         functools.partial(layout_kernel, rows, cols, (part, project_len, up_len)),
         "layout",
-        1 << 24,
+        1 << 35,
         (where, every),
         (
             SHAPE((8, width), F32),
@@ -712,42 +840,82 @@
         ),
         (),
     )
+    if paired:
+        pass
     cosine, sine = rotary_tables(jnp.arange(rows * count, dtype=jnp.int32) - starts[:, 0])
 
+    if not paired:
+        att_slots = list(att_slots[0]), (att_slots[1],)
+        mlp_slots = list(mlp_slots[0]), (mlp_slots[1],)
     n1, n2, xhat, cot_all, *first, att_keep, small_own = run_first(
         where, chunks, att_slots[0], project_shift, cosine, sine, starts, norms
     )
-    *second, att_send, small_oth = run_second(
-        where, n1, cot_all, att_slots[1], project_shift, cosine, sine, starts
-    )
     out, e, mlp_send, mlp_keep, mlp_small = run_mlp(
         where, n2, xhat, cot_all, mlp_slots[0], mlp_slots[1], norms, up_shift
     )
-    near, rest, small_join = run_join(where, xhat, norms, first, second, out, e)
-    ub_own, ub_oth = mlp_small[0, :256], mlp_small[0, 256:]
-    pb_own, pb_oth = small_own[0, : 3 * HD], small_oth[0, : 3 * HD]
-
-    mine = rest + flip(near, 1).astype(F32)
-    total = mine[0] + flip(mine[1].astype(BF), 2).astype(F32)
-    x_own, cot_own = inputs[0].astype(F32), cotangent[0].astype(F32)
-    output = (x_own + total[0] + norms[4] + norms[5]).astype(BF)[None]
-    e_all = total[1]
-    xhat_own, root_own = normalize(x_own)
-    input_grad = cot_own + root_own * (
-        e_all
-        - jnp.mean(e_all, axis=-1, keepdims=True)
-        - xhat_own * jnp.mean(e_all * xhat_own, axis=-1, keepdims=True)
-    )
-
+    n1, out = lax.optimization_barrier((n1, out))
+    *second, att_send, small_oth = run_second(
+        where, n1, xhat, cot_all, att_slots[1], project_shift, cosine, sine, starts, norms
+    )
+    near, rest = run_join(where, norms, first, second, out, e)
+
+    (small,) = call(
+        functools.partial(share_kernel, cols, (part, project_len, up_len)),
+        "share_small",
+        1 << 24,
+        (where, mlp_small, small_own, small_oth),
+        (SHAPE((copies, LINES, 128), F32),),
+        (),
+    )
     if paired:
-        blocks = call(
+        near, small, mlp_come, att_come = lax.optimization_barrier(
+            (near, small, beside(mlp_send), beside(att_send))
+        )
+
+    if paired:
+        blocks = call_streamed(
             merge_kernel,
             "merge",
             1 << 26,
-            (where, att_keep, beside(att_send), mlp_keep, beside(mlp_send)),
+            (att_keep, att_come, mlp_keep, mlp_come),
             (SHAPE((768, 128), BF),) * 4,
-            (),
         )
+        blocks = bring(blocks)
+    shares = lax.all_to_all(small, both, 0, 0, tiled=True)
+
+    mine, onward = call_streamed(
+        add_kernel,
+        "add_near",
+        1 << 24,
+        (rest, flip(near, 1)),
+        (SHAPE((2, count, width), F32), SHAPE((2, count, width), BF)),
+    )
+    onward = flip(onward, 2)
+    if paired:
+        project_done, mix_done, up_done, down_done = call_streamed(
+            collect_kernel,
+            "collect",
+            1 << 35,
+            tuple(blocks),
+            (
+                SHAPE(project_weight.shape[::-1], F32),
+                SHAPE(output_weight.shape, F32),
+                SHAPE(up_weight.shape, F32),
+                SHAPE(down_weight.shape, F32),
+            ),
+        )
+        project_done, onward, shares = lax.optimization_barrier((project_done, onward, shares))
+        project_done = project_done.T
+    output, input_grad = call_streamed(
+        finish_kernel,
+        "finish",
+        1 << 24,
+        (x_own, cot_own, mine, onward, norms),
+        (SHAPE((count, width), BF), SHAPE((count, width), F32)),
+    )
+
+    if paired:
+        pass
     else:
         att_grads, mlp_grads = jnp.stack([att_keep, att_send.astype(F32)]), jnp.stack([mlp_keep, mlp_send.astype(F32)])
         every_pair = [(h, g) for h in range(2) for g in range(rows)]
@@ -764,42 +932,20 @@
         )
         down_done = deliver_rows(regroup([mlp_grads[h, g][256:] for h, g in every_pair]))
 
-    everywhere = jnp.concatenate([small_join[:2], mlp_small[1:4]])
-    everywhere = everywhere.reshape(5, rows * cols, part).transpose(1, 0, 2).reshape(rows * cols, -1)
-
-    def by_half(own, other):
-        first = jnp.where(y == 0, own, other)
-        second = jnp.where(y == 0, other, own)
-        return jnp.concatenate([first, second]).reshape(cols, -1)
-
-    local = jnp.concatenate([by_half(pb_own, pb_oth), by_half(ub_own, ub_oth)], axis=1)
-    local = lax.dynamic_update_slice(
-        jnp.zeros((rows * cols, local.shape[1]), F32), local, (group * cols, 0)
-    )
-    small = jnp.concatenate([everywhere, local], axis=1)
-    if paired:
-        small, blocks = lax.optimization_barrier((small, blocks))
-    sums = lax.all_to_all(small, both, 0, 0, tiled=True).sum(axis=0)
-    if paired:
-        project_done, mix_done, up_done, down_done = call(
-            collect_kernel,
-            "collect",
-            1 << 26,
-            (where, *bring(blocks)),
-            (
-                SHAPE(project_weight.shape[::-1], F32),
-                SHAPE(output_weight.shape, F32),
-                SHAPE(up_weight.shape, F32),
-                SHAPE(down_weight.shape, F32),
-            ),
+    *pieces, project_shift_grad, up_shift_grad = [
+        v[0]
+        for v in call(
+            small_kernel,
+            "small_sums",
+            1 << 24,
+            (where, shares),
+            (SHAPE((1, part), F32),) * 5
+            + (SHAPE((1, project_len), F32), SHAPE((1, up_len), F32)),
             (),
         )
-        project_done = project_done.T
-    pieces = [sums[i * part : (i + 1) * part] for i in range(5)]
-    project_shift_grad = sums[5 * part : 5 * part + project_len]
-    up_shift_grad = sums[5 * part + project_len :]
+    ]
     return (
-        output,
+        output[None],
         input_grad[None],
         project_done,
         project_shift_grad,

time: 134 us -> 112 us (0.84)
  the two profiles are of different devices: /device:TPU:25 before, /device:TPU:0 now
where the time goes in v4:
time: 112 us
  starting transfers between devices  38.1 us (34%)
  Pallas kernels  35.5 us (32%)
  waiting for transfers between devices  31.8 us (28%)
  other arithmetic  3.69 us (3%)
  local copies, waits for them, and re-layouts  1.65 us (1%)
    pallas_call x7, Pallas kernels, call(): pl.pallas_call(kernel, out_shape=results, in_specs=[SMEM] + places, out_s...  27.5 us
    ppermute x4, starting transfers between devices, spread(): lax.ppermute(block, both, [(i, home(i, k)) for i in everyone])  10.6 us
    ppermute x4, waiting for transfers between devices, bring(): lax.ppermute(b, both, [(home(i, k), i) for i in everyone])  9.9 us
    ppermute x4, starting transfers between devices, bring(): lax.ppermute(b, both, [(home(i, k), i) for i in everyone])  9.79 us
    all_to_all x1, waiting for transfers between devices, on_device(): every = lax.all_to_all(small, both, 0, 0, tiled=True)  8.05 us
    ppermute x4, waiting for transfers between devices, beside(): return lax.ppermute(value, 'col', [(i, i ^ 1) for i in range(cols)])  5.97 us
    pallas_call x4, Pallas kernels, call_streamed(): pl.pallas_call(body, out_shape=results, in_specs=[HBM] * len(operands), o...  5.83 us
    all_to_all x1, starting transfers between devices, on_device(): shares = lax.all_to_all(small, both, 0, 0, tiled=True)  5.09 us
  transfers between devices with their start and end apart: 19, of which 6 were waited for; matrix products, arithmetic and copies ran while one was open for 3% of the time, Pallas kernels for 27%

profile of v4, /device:TPU:0, one launch (start us, length us, event | category | flops | bytes accessed | tf_op | source)
XLA Modules:
  0.0 111.8 jit_solution(8555372036716983944)
XLA Ops:
  0.7 2.2 %prepare.1 = (bf16[32,8,128]{2,1,0:T(8,128)(2,1)}, bf16[2,256,512]{2,1,0:T(8,128)(2,1)}, bf16[768,128]{1,0:T(8,128)(2,1)}) custom-call(bf16[256,512]{1,0:T(8,128)(2,1)} %bitcast.42, bf16[256,512]{1,0:T(8,128)(2,1)} %bitcast.44, s32[1,256]{1,0:T(1,128)} %refs_2_.1, bf16[192,128]{1,0:T(8,128)(2,1)} %bitcast.46, bf16[64,128]{1,0:T(8,128)(2,1)} %refs_4_.1, ...), custom_call_target="tpu_custom_call" | custom-call | flops 1048576 | bytes 1048576 | tf_op jit(solution)/shard_map/prepare/pallas_call | solution.py:155
  2.9 7.0 %collective-permute-start.6 = (bf16[768,128]{1,0:T(8,128)(2,1)}, bf16[768,128]{1,0:T(8,128)(2,1)S(1)}, u32[]{:S(2)}, u32[]{:S(2)}) collective-permute-start(bf16[768,128]{1,0:T(8,128)(2,1)} %get-tuple-element.79), channel_id=1, source_target_pairs={{0,6},{1,7},{2,22},{3,23},{4,14},{5,15},{6,30},{7,31},{8,4},{9,5},... | collective-permute-start | bytes 589832 | tf_op jit(solution)/shard_map/ppermute | solution.py:738
  9.9 1.6 %collective-permute-start.3 = (bf16[768,128]{1,0:T(8,128)(2,1)}, bf16[768,128]{1,0:T(8,128)(2,1)S(1)}, u32[]{:S(2)}, u32[]{:S(2)}) collective-permute-start(bf16[768,128]{1,0:T(8,128)(2,1)} %get-tuple-element.79), channel_id=1, source_target_pairs={{0,0},{1,1},{2,16},{3,17},{4,8},{5,9},{6,24},{7,25},{8,2},{9,3},{1... | collective-permute-start | bytes 589832 | tf_op jit(solution)/shard_map/ppermute | solution.py:738
  11.4 1.9 %collective-permute-start.4 = (bf16[768,128]{1,0:T(8,128)(2,1)}, bf16[768,128]{1,0:T(8,128)(2,1)S(1)}, u32[]{:S(2)}, u32[]{:S(2)}) collective-permute-start(bf16[768,128]{1,0:T(8,128)(2,1)} %get-tuple-element.79), channel_id=1, source_target_pairs={{0,2},{1,3},{2,18},{3,19},{4,10},{5,11},{6,26},{7,27},{8,0},{9,1},... | collective-permute-start | bytes 589832 | tf_op jit(solution)/shard_map/ppermute | solution.py:738
  13.5 1.8 %collective-permute-start = (bf16[2,256,512]{2,1,0:T(8,128)(2,1)}, bf16[2,256,512]{2,1,0:T(8,128)(2,1)S(1)}, u32[]{:S(2)}, u32[]{:S(2)}) collective-permute-start(bf16[2,256,512]{2,1,0:T(8,128)(2,1)} %get-tuple-element.75.act0_ref), channel_id=1, source_target_pairs={{0,16},{8,24},{16,0},{24,8},{1,17},{9,25},{17,1},{25,9},{2,18},{10... | collective-permute-start | bytes 1572872 | tf_op jit(solution)/shard_map/ppermute | solution.py:722
  15.4 4.4 %all-to-all-start = ((bf16[32,8,128]{2,1,0:T(8,128)(2,1)}), bf16[32,8,128]{2,1,0:T(8,128)(2,1)S(1)}, u32[]{:S(2)}, u32[]{:S(2)}) async-start(bf16[32,8,128]{2,1,0:T(8,128)(2,1)} %get-tuple-element.74), calls=%async_computation | async-start | bytes 131072 | tf_op jit(solution)/shard_map/all_to_all | solution.py:807
  20.2 2.9 %collective-permute-done.5.slot2_ref.own2_ref = bf16[768,128]{1,0:T(8,128)(2,1)S(1)} collective-permute-done((bf16[768,128]{1,0:T(8,128)(2,1)}, bf16[768,128]{1,0:T(8,128)(2,1)S(1)}, u32[]{:S(2)}, u32[]{:S(2)}) %collective-permute-start.5) | collective-permute-done | bytes 196640 | tf_op jit(solution)/shard_map/ppermute | solution.py:738
  24.0 1.5 %collective-permute-start.7 = (bf16[4,512,128]{2,1,0:T(8,128)(2,1)}, bf16[4,512,128]{2,1,0:T(8,128)(2,1)S(1)}, u32[]{:S(2)}, u32[]{:S(2)}) collective-permute-start(bf16[4,512,128]{2,1,0:T(8,128)(2,1)} %pad_maximum_fusion), channel_id=1, source_target_pairs={{0,1},{1,0},{2,3},{3,2},{4,5},{5,4},{6,7},{7,6},{8,9},{9,8},{10,11... | collective-permute-start | bytes 1572872 | tf_op jit(solution)/shard_map/ppermute | solution.py:735
  26.8 8.0 %all-to-all-done.every_ref = bf16[32,8,128]{2,1,0:T(8,128)(2,1)S(1)} async-done(((bf16[32,8,128]{2,1,0:T(8,128)(2,1)}), bf16[32,8,128]{2,1,0:T(8,128)(2,1)S(1)}, u32[]{:S(2)}, u32[]{:S(2)}) %all-to-all-start) | async-done | bytes 65568 | tf_op jit(solution)/shard_map/all_to_all | solution.py:807
  36.1 1.9 %multiply_sine_fusion = (f32[1024,128]{1,0:T(8,128)S(1)}, f32[1024,128]{1,0:T(8,128)S(1)}) fusion(f32[128]{0:T(128)S(1)} %copy-done.5, f32[1024]{0:T(1024)S(1)} %convert_reduce_fusion), kind=kLoop, calls=%fused_computation | loop fusion | flops 131072 | bytes 1053184 | tf_op jit(solution)/shard_map/sin | solution.py:48
  38.0 8.1 %attention_first.1 = (bf16[1024,512]{1,0:T(8,128)(2,1)S(1)}, bf16[1024,512]{1,0:T(8,128)(2,1)S(1)}, bf16[1024,512]{1,0:T(8,128)(2,1)S(1)}, bf16[1024,512]{1,0:T(...) custom-call(s32[5]{0:T(128)S(1)} %stack.53.where_ref.unused, ...), custom_call_target="tpu_custom_call" | custom-call | flops 34359738368 | bytes 85899344 | tf_op jit(solution)/shard_map/attention_first/pallas_call | solution.py:94
  46.1 5.6 %feed_forward.1 = (bf16[1024,512]{1,0:T(8,128)(2,1)S(1)}, bf16[1024,512]{1,0:T(8,128)(2,1)S(1)}, bf16[4,512,128]{2,1,0:T(8,128)(2,1)S(1)}, f32[4,512,128]{2,1,0:T(8,128)S(1)}, f32[8,512]{1,0:T(8,128)S(1)}) custom-call(s32[5]{0:T(128)S(1)} %stack.53.where_ref.unused, bf16[1024,512]{1,0:T(8,128)(2,1)S(1)} %get-tuple-element.87.n2_ref, ...), custom_call_target="tpu_custom_call" | custom-call | flops 34359738368 | bytes 85899344 | tf_op jit(solution)/shard_map/feed_forward/pallas_call | solution.py:94
  51.7 1.7 %collective-permute-start.9 = (bf16[4,512,128]{2,1,0:T(8,128)(2,1)S(1)}, bf16[4,512,128]{2,1,0:T(8,128)(2,1)S(1)}, u32[]{:S(2)}, u32[]{:S(2)}) collective-permute-start(bf16[4,512,128]{2,1,0:T(8,128)(2,1)S(1)} %get-tuple-element.104), channel_id=1, source_target_pairs={{0,1},{1,0},{2,3},{3,2},{4,5},{5,4},{6,7},{7,6},{8,9},{9,8},{10,11... | collective-permute-start | bytes 1572872 | tf_op jit(solution)/shard_map/ppermute | solution.py:735
  53.5 6.7 %attention_second.1 = (bf16[256,512]{1,0:T(8,128)(2,1)S(1)}, bf16[128,512]{1,0:T(8,128)(2,1)S(1)}, bf16[1024,128]{1,0:T(8,128)(2,1)S(1)}, bf16[1024,256]{1,0:T(8...) custom-call(s32[5]{0:T(128)S(1)} %stack.53.where_ref.unused, ...), custom_call_target="tpu_custom_call" | custom-call | flops 34359738368 | bytes 85899344 | tf_op jit(solution)/shard_map/attention_second/pallas_call | solution.py:94
  60.6 2.2 %share_small.1 = f32[32,8,128]{2,1,0:T(8,128)} custom-call(s32[5]{0:T(128)S(1)} %stack.53.where_ref.unused, f32[8,512]{1,0:T(8,128)S(1)} %get-tuple-element.101.mlp_ref, f32[8,512]{1,0:T(8,128)S(1)} %get-tuple-element.102.own_ref, f32[8,512]{1,0:T(8,128)S(1)} %get-tuple-element.103.oth_ref), custom_call_target="tpu_custom_call" | custom-call | flops 16777216 | bytes 41943 | tf_op jit(solution)/shard_map/share_small/pallas_call | solution.py:94
  62.9 2.8 %join.1 = (bf16[2,2,256,512]{3,2,1,0:T(8,128)(2,1)}, f32[2,2,256,512]{3,2,1,0:T(8,128)S(1)}) custom-call(s32[5]{0:T(128)S(1)} %stack.53.where_ref.unused, f32[8,512]{1,0:T(8,128)S(1)} %get-tuple-element.77.norms_ref.refs_4_, bf16[256,512]{1,0:T(8,128)(2,1)S(1)} %get-tuple-element.82.w_a, bf16[128,512]{1,0:T(8,128)(2,1)S(1)} %get-tuple-element.83.mix_a, ...), custom_call_target="tpu_custom_call" | custom-call | flops 16777216 | bytes 41943 | tf_op jit(solution)/shard_map/join/pallas_call | solution.py:94
  65.7 6.0 %collective-permute-done.10.refs_1_ = bf16[4,256,128]{2,1,0:T(8,128)(2,1)S(1)} collective-permute-done((bf16[4,256,128]{2,1,0:T(8,128)(2,1)S(1)}, bf16[4,256,128]{2,1,0:T(8,128)(2,1)S(1)}, u32[]{:S(2)}, u32[]{:S(2)}) %collective-permute-start.10) | collective-permute-done | bytes 262176 | tf_op jit(solution)/shard_map/ppermute | solution.py:735
  71.6 1.1 %merge.1 = (bf16[768,128]{1,0:T(8,128)(2,1)}, bf16[768,128]{1,0:T(8,128)(2,1)}, bf16[768,128]{1,0:T(8,128)(2,1)}, bf16[768,128]{1,0:T(8,128)(2,1)}) custom-call(f32[4,256,128]{2,1,0:T(8,128)S(1)} %get-tuple-element.108.refs_0_, bf16[4,256,128]{2,1,0:T(8,128)(2,1)S(1)} %collective-permute-done.10.refs_1_, f32[4,512,128]{2,1,0:T(8,128)S(1)} %get-tuple-element.110.refs_2_, ...), custom_call_target="tpu_custom_call" | custom-call | flops 67108864 | bytes 167772 | tf_op jit(solution)/shard_map/merge/pallas_call | solution.py:79
  72.8 1.6 %collective-permute-start.12 = (bf16[768,128]{1,0:T(8,128)(2,1)}, bf16[768,128]{1,0:T(8,128)(2,1)S(1)}, u32[]{:S(2)}, u32[]{:S(2)}) collective-permute-start(bf16[768,128]{1,0:T(8,128)(2,1)} %get-tuple-element.112), channel_id=1, source_target_pairs={{0,0},{1,1},{16,2},{17,3},{8,4},{9,5},{24,6},{25,7},{2,8},{3,9},{1... | collective-permute-start | bytes 589832 | tf_op jit(solution)/shard_map/ppermute | solution.py:742
  74.4 1.3 %collective-permute-start.13 = (bf16[768,128]{1,0:T(8,128)(2,1)}, bf16[768,128]{1,0:T(8,128)(2,1)}, u32[]{:S(2)}, u32[]{:S(2)}) collective-permute-start(bf16[768,128]{1,0:T(8,128)(2,1)} %get-tuple-element.113), channel_id=1, source_target_pairs={{2,0},{3,1},{18,2},{19,3},{10,4},{11,5},{26,6},{27,7},{0,8},{1,9},... | collective-permute-start | bytes 589832 | tf_op jit(solution)/shard_map/ppermute | solution.py:742
  75.7 2.1 %collective-permute-start.14 = (bf16[768,128]{1,0:T(8,128)(2,1)}, bf16[768,128]{1,0:T(8,128)(2,1)}, u32[]{:S(2)}, u32[]{:S(2)}) collective-permute-start(bf16[768,128]{1,0:T(8,128)(2,1)} %get-tuple-element.114), channel_id=1, source_target_pairs={{4,0},{5,1},{20,2},{21,3},{12,4},{13,5},{28,6},{29,7},{6,8},{7,9},... | collective-permute-start | bytes 589832 | tf_op jit(solution)/shard_map/ppermute | solution.py:742
  77.7 4.8 %collective-permute-start.15 = (bf16[768,128]{1,0:T(8,128)(2,1)}, bf16[768,128]{1,0:T(8,128)(2,1)}, u32[]{:S(2)}, u32[]{:S(2)}) collective-permute-start(bf16[768,128]{1,0:T(8,128)(2,1)} %get-tuple-element.115), channel_id=1, source_target_pairs={{6,0},{7,1},{22,2},{23,3},{14,4},{15,5},{30,6},{31,7},{4,8},{5,9},... | collective-permute-start | bytes 589832 | tf_op jit(solution)/shard_map/ppermute | solution.py:742
  82.6 5.1 %all-to-all-start.1 = ((f32[32,8,128]{2,1,0:T(8,128)}), f32[32,8,128]{2,1,0:T(8,128)S(1)}, u32[]{:S(2)}, u32[]{:S(2)}) async-start(f32[32,8,128]{2,1,0:T(8,128)} %share_small.1), calls=%async_computation.1 | async-start | bytes 262144 | tf_op jit(solution)/shard_map/all_to_all | solution.py:884
  87.7 1.1 add_near.1
  88.8 1.0 copy-done
  89.8 1.8 %collective-permute-start.16 = (bf16[2,256,512]{2,1,0:T(8,128)(2,1)}, bf16[2,256,512]{2,1,0:T(8,128)(2,1)S(1)}, u32[]{:S(2)}, u32[]{:S(2)}) collective-permute-start(bf16[2,256,512]{2,1,0:T(8,128)(2,1)} %get-tuple-element.117), channel_id=1, source_target_pairs={{0,16},{8,24},{16,0},{24,8},{1,17},{9,25},{17,1},{25,9},{2,18},{10... | collective-permute-start | bytes 1572872 | tf_op jit(solution)/shard_map/ppermute | solution.py:722
  91.5 9.9 %collective-permute-done.13.refs_1_ = bf16[768,128]{1,0:T(8,128)(2,1)} collective-permute-done((bf16[768,128]{1,0:T(8,128)(2,1)}, bf16[768,128]{1,0:T(8,128)(2,1)}, u32[]{:S(2)}, u32[]{:S(2)}) %collective-permute-start.13) | collective-permute-done | bytes 196640 | tf_op jit(solution)/shard_map/ppermute | solution.py:742
  101.4 2.2 %collect.1 = (f32[192,128]{1,0:T(8,128)}, f32[64,128]{1,0:T(8,128)}, f32[128,256]{1,0:T(8,128)}, f32[256,128]{1,0:T(8,128)}) custom-call(bf16[768,128]{1,0:T(8,128)(2,1)S(1)} %collective-permute-done.12.refs_0_, bf16[768,128]{1,0:T(8,128)(2,1)} %collective-permute-done.13.refs_1_, bf16[768,128]{1,0:T(8,128)(2,1)} %collective-permute-done.14.refs_2_, ...), custom_call_target="tpu_custom_call" | custom-call | flops 34359738368 | bytes 85899344 | tf_op jit(solution)/shard_map/collect/pallas_call | solution.py:79
  103.6 2.8 %all-to-all-done.1.sums_ref = f32[32,8,128]{2,1,0:T(8,128)S(1)} async-done(((f32[32,8,128]{2,1,0:T(8,128)}), f32[32,8,128]{2,1,0:T(8,128)S(1)}, u32[]{:S(2)}, u32[]{:S(2)}) %all-to-all-start.1) | async-done | bytes 131104 | tf_op jit(solution)/shard_map/all_to_all | solution.py:884
  106.4 2.2 %collective-permute-done.16.refs_3_ = bf16[2,256,512]{2,1,0:T(8,128)(2,1)S(1)} collective-permute-done((bf16[2,256,512]{2,1,0:T(8,128)(2,1)}, bf16[2,256,512]{2,1,0:T(8,128)(2,1)S(1)}, u32[]{:S(2)}, u32[]{:S(2)}) %collective-permute-start.16) | collective-permute-done | bytes 524320 | tf_op jit(solution)/shard_map/ppermute | solution.py:722
  108.6 1.2 %small_sums.1 = (f32[1,16]{1,0:T(1,128)}, f32[1,16]{1,0:T(1,128)}, f32[1,16]{1,0:T(1,128)}, f32[1,16]{1,0:T(1,128)}, f32[1,16]{1,0:T(1,128)}, /*index=5*/f32[1,48]{1,0:T(1,128)}, f32[1,64]{1,0:T(1,128)}) custom-call(s32[5]{0:T(128)S(1)} %stack.53.where_ref.unused, f32[32,8,128]{2,1,0:T(8,128)S(1)} %all-to-all-done.1.sums_ref), custom_call_target="tpu_custom_call" | custom-call | flops 16777216 | bytes 41943 | tf_op jit(solution)/shard_map/small_sums/pallas_call | solution.py:94
  109.8 1.4 %finish.1 = (bf16[256,512]{1,0:T(8,128)(2,1)}, f32[256,512]{1,0:T(8,128)}) custom-call(bf16[256,512]{1,0:T(8,128)(2,1)S(1)} %bitcast.43, bf16[256,512]{1,0:T(8,128)(2,1)S(1)} %bitcast.45, f32[2,256,512]{2,1,0:T(8,128)S(1)} %copy-done.1, bf16[2,256,512]{2,1,0:T(8,128)(2,1)S(1)} %collective-permute-done.16.refs_3_, ...), custom_call_target="tpu_custom_call" | custom-call | flops 16777216 | bytes 41943 | tf_op jit(solution)/shard_map/finish/pallas_call | solution.py:79
  (46 shorter events, 5.0 us)
Async XLA Ops:
  2.9 17.0 %collective-permute-start.6 = (bf16[768,128]{1,0:T(8,128)(2,1)}, bf16[768,128]{1,0:T(8,128)(2,1)S(1)}, u32[]{:S(2)}, u32[]{:S(2)}) collective-permute-start(bf16[768,128]{1,0:T(8,128)(2,1)} %get-tuple-element.79), channel_id=1, source_target_pairs={{0,6},{1,7},{2,22},{3,23},{4,14},{5,15},{6,30},{7,31},{8,4},{9,5},... | collective-permute-start | bytes 589832 | tf_op jit(solution)/shard_map/ppermute | solution.py:738
  9.9 13.3 %collective-permute-start.3 = (bf16[768,128]{1,0:T(8,128)(2,1)}, bf16[768,128]{1,0:T(8,128)(2,1)S(1)}, u32[]{:S(2)}, u32[]{:S(2)}) collective-permute-start(bf16[768,128]{1,0:T(8,128)(2,1)} %get-tuple-element.79), channel_id=1, source_target_pairs={{0,0},{1,1},{2,16},{3,17},{4,8},{5,9},{6,24},{7,25},{8,2},{9,3},{1... | collective-permute-start | bytes 589832 | tf_op jit(solution)/shard_map/ppermute | solution.py:738
  11.4 11.6 %collective-permute-start.4 = (bf16[768,128]{1,0:T(8,128)(2,1)}, bf16[768,128]{1,0:T(8,128)(2,1)S(1)}, u32[]{:S(2)}, u32[]{:S(2)}) collective-permute-start(bf16[768,128]{1,0:T(8,128)(2,1)} %get-tuple-element.79), channel_id=1, source_target_pairs={{0,2},{1,3},{2,18},{3,19},{4,10},{5,11},{6,26},{7,27},{8,0},{9,1},... | collective-permute-start | bytes 589832 | tf_op jit(solution)/shard_map/ppermute | solution.py:738
  13.3 9.7 %collective-permute-start.5 = (bf16[768,128]{1,0:T(8,128)(2,1)}, bf16[768,128]{1,0:T(8,128)(2,1)S(1)}, u32[]{:S(2)}, u32[]{:S(2)}) collective-permute-start(bf16[768,128]{1,0:T(8,128)(2,1)} %get-tuple-element.79), channel_id=1, source_target_pairs={{0,4},{1,5},{2,20},{3,21},{4,12},{5,13},{6,28},{7,29},{8,6},{9,7},... | collective-permute-start | bytes 589832 | tf_op jit(solution)/shard_map/ppermute | solution.py:738
  13.5 21.3 %collective-permute-start = (bf16[2,256,512]{2,1,0:T(8,128)(2,1)}, bf16[2,256,512]{2,1,0:T(8,128)(2,1)S(1)}, u32[]{:S(2)}, u32[]{:S(2)}) collective-permute-start(bf16[2,256,512]{2,1,0:T(8,128)(2,1)} %get-tuple-element.75.act0_ref), channel_id=1, source_target_pairs={{0,16},{8,24},{16,0},{24,8},{1,17},{9,25},{17,1},{25,9},{2,18},{10... | collective-permute-start | bytes 1572872 | tf_op jit(solution)/shard_map/ppermute | solution.py:722
  15.4 19.5 %all-to-all-start = ((bf16[32,8,128]{2,1,0:T(8,128)(2,1)}), bf16[32,8,128]{2,1,0:T(8,128)(2,1)S(1)}, u32[]{:S(2)}, u32[]{:S(2)}) async-start(bf16[32,8,128]{2,1,0:T(8,128)(2,1)} %get-tuple-element.74), calls=%async_computation | async-start | bytes 131072 | tf_op jit(solution)/shard_map/all_to_all | solution.py:807
  19.9 18.1 %collective-permute-start.1 = (bf16[2,256,512]{2,1,0:T(8,128)(2,1)}, bf16[2,256,512]{2,1,0:T(8,128)(2,1)S(1)}, u32[]{:S(2)}, u32[]{:S(2)}) collective-permute-start(bf16[2,256,512]{2,1,0:T(8,128)(2,1)} %get-tuple-element.75.act0_ref), channel_id=1, source_target_pairs={{0,8},{8,0},{16,24},{24,16},{1,9},{9,1},{17,25},{25,17},{2,10},{10... | collective-permute-start | bytes 1572872 | tf_op jit(solution)/shard_map/ppermute | solution.py:722
  24.0 22.1 %collective-permute-start.7 = (bf16[4,512,128]{2,1,0:T(8,128)(2,1)}, bf16[4,512,128]{2,1,0:T(8,128)(2,1)S(1)}, u32[]{:S(2)}, u32[]{:S(2)}) collective-permute-start(bf16[4,512,128]{2,1,0:T(8,128)(2,1)} %pad_maximum_fusion), channel_id=1, source_target_pairs={{0,1},{1,0},{2,3},{3,2},{4,5},{5,4},{6,7},{7,6},{8,9},{9,8},{10,11... | collective-permute-start | bytes 1572872 | tf_op jit(solution)/shard_map/ppermute | solution.py:735
  26.3 9.8 %copy-start.5 = (f32[128]{0:T(128)S(1)}, f32[128]{0:T(128)}, u32[]{:S(2)}) copy-start(f32[128]{0:T(128)} %constant.45.clone) | copy-start | bytes 1540
  26.3 11.7 %copy-start.4 = (bf16[2,256,512]{2,1,0:T(8,128)(2,1)S(1)}, bf16[2,256,512]{2,1,0:T(8,128)(2,1)}, u32[]{:S(2)}) copy-start(bf16[2,256,512]{2,1,0:T(8,128)(2,1)} %get-tuple-element.75.act0_ref) | copy-start | bytes 1572868
  26.3 27.2 %collective-permute-start.8 = (bf16[4,256,128]{2,1,0:T(8,128)(2,1)}, bf16[4,256,128]{2,1,0:T(8,128)(2,1)S(1)}, u32[]{:S(2)}, u32[]{:S(2)}) collective-permute-start(bf16[4,256,128]{2,1,0:T(8,128)(2,1)} %pad_maximum_fusion.1), channel_id=1, source_target_pairs={{0,1},{1,0},{2,3},{3,2},{4,5},{5,4},{6,7},{7,6},{8,9},{9,8},{10,11... | collective-permute-start | bytes 786440 | tf_op jit(solution)/shard_map/ppermute | solution.py:735
  34.9 3.2 %collective-permute-start.2 = (bf16[2,256,512]{2,1,0:T(8,128)(2,1)S(1)}, bf16[2,256,512]{2,1,0:T(8,128)(2,1)S(1)}, u32[]{:S(2)}, u32[]{:S(2)}) collective-permute-start(bf16[2,256,512]{2,1,0:T(8,128)(2,1)S(1)} %collective-permute-done.act2_ref), channel_id=1, source_target_pairs={{0,8},{8,0},{16,24},{24,16},{1,9},{9,1},{17,25},{25,17},{2,10},{10... | collective-permute-start | bytes 1572872 | tf_op jit(solution)/shard_map/ppermute | solution.py:722
  51.7 19.9 %collective-permute-start.9 = (bf16[4,512,128]{2,1,0:T(8,128)(2,1)S(1)}, bf16[4,512,128]{2,1,0:T(8,128)(2,1)S(1)}, u32[]{:S(2)}, u32[]{:S(2)}) collective-permute-start(bf16[4,512,128]{2,1,0:T(8,128)(2,1)S(1)} %get-tuple-element.104), channel_id=1, source_target_pairs={{0,1},{1,0},{2,3},{3,2},{4,5},{5,4},{6,7},{7,6},{8,9},{9,8},{10,11... | collective-permute-start | bytes 1572872 | tf_op jit(solution)/shard_map/ppermute | solution.py:735
  60.2 11.5 %collective-permute-start.10 = (bf16[4,256,128]{2,1,0:T(8,128)(2,1)S(1)}, bf16[4,256,128]{2,1,0:T(8,128)(2,1)S(1)}, u32[]{:S(2)}, u32[]{:S(2)}) collective-permute-start(bf16[4,256,128]{2,1,0:T(8,128)(2,1)S(1)} %get-tuple-element.105), channel_id=1, source_target_pairs={{0,1},{1,0},{2,3},{3,2},{4,5},{5,4},{6,7},{7,6},{8,9},{9,8},{10,11... | collective-permute-start | bytes 786440 | tf_op jit(solution)/shard_map/ppermute | solution.py:735
  71.6 16.0 %collective-permute-start.11 = (bf16[2,2,256,512]{3,2,1,0:T(8,128)(2,1)}, bf16[2,2,256,512]{3,2,1,0:T(8,128)(2,1)S(1)}, u32[]{:S(2)}, u32[]{:S(2)}) collective-permute-start(bf16[2,2,256,512]{3,2,1,0:T(8,128)(2,1)} %get-tuple-element.106), channel_id=1, source_target_pairs={{0,8},{8,0},{16,24},{24,16},{1,9},{9,1},{17,25},{25,17},{2,10},{10... | collective-permute-start | bytes 3145736 | tf_op jit(solution)/shard_map/ppermute | solution.py:722
  72.8 18.8 %collective-permute-start.12 = (bf16[768,128]{1,0:T(8,128)(2,1)}, bf16[768,128]{1,0:T(8,128)(2,1)S(1)}, u32[]{:S(2)}, u32[]{:S(2)}) collective-permute-start(bf16[768,128]{1,0:T(8,128)(2,1)} %get-tuple-element.112), channel_id=1, source_target_pairs={{0,0},{1,1},{16,2},{17,3},{8,4},{9,5},{24,6},{25,7},{2,8},{3,9},{1... | collective-permute-start | bytes 589832 | tf_op jit(solution)/shard_map/ppermute | solution.py:742
  74.4 27.1 %collective-permute-start.13 = (bf16[768,128]{1,0:T(8,128)(2,1)}, bf16[768,128]{1,0:T(8,128)(2,1)}, u32[]{:S(2)}, u32[]{:S(2)}) collective-permute-start(bf16[768,128]{1,0:T(8,128)(2,1)} %get-tuple-element.113), channel_id=1, source_target_pairs={{2,0},{3,1},{18,2},{19,3},{10,4},{11,5},{26,6},{27,7},{0,8},{1,9},... | collective-permute-start | bytes 589832 | tf_op jit(solution)/shard_map/ppermute | solution.py:742
  75.7 25.8 %collective-permute-start.14 = (bf16[768,128]{1,0:T(8,128)(2,1)}, bf16[768,128]{1,0:T(8,128)(2,1)}, u32[]{:S(2)}, u32[]{:S(2)}) collective-permute-start(bf16[768,128]{1,0:T(8,128)(2,1)} %get-tuple-element.114), channel_id=1, source_target_pairs={{4,0},{5,1},{20,2},{21,3},{12,4},{13,5},{28,6},{29,7},{6,8},{7,9},... | collective-permute-start | bytes 589832 | tf_op jit(solution)/shard_map/ppermute | solution.py:742
  77.7 23.7 %collective-permute-start.15 = (bf16[768,128]{1,0:T(8,128)(2,1)}, bf16[768,128]{1,0:T(8,128)(2,1)}, u32[]{:S(2)}, u32[]{:S(2)}) collective-permute-start(bf16[768,128]{1,0:T(8,128)(2,1)} %get-tuple-element.115), channel_id=1, source_target_pairs={{6,0},{7,1},{22,2},{23,3},{14,4},{15,5},{30,6},{31,7},{4,8},{5,9},... | collective-permute-start | bytes 589832 | tf_op jit(solution)/shard_map/ppermute | solution.py:742
  82.6 23.8 %all-to-all-start.1 = ((f32[32,8,128]{2,1,0:T(8,128)}), f32[32,8,128]{2,1,0:T(8,128)S(1)}, u32[]{:S(2)}, u32[]{:S(2)}) async-start(f32[32,8,128]{2,1,0:T(8,128)} %share_small.1), calls=%async_computation.1 | async-start | bytes 262144 | tf_op jit(solution)/shard_map/all_to_all | solution.py:884
  88.8 1.0 copy-start
  89.8 20.0 %copy-start.1 = (f32[2,256,512]{2,1,0:T(8,128)S(1)}, f32[2,256,512]{2,1,0:T(8,128)}, u32[]{:S(2)}) copy-start(f32[2,256,512]{2,1,0:T(8,128)} %copy-done) | copy-start | bytes 3145732
  89.8 20.0 %copy-start.2 = (bf16[1,256,512]{2,1,0:T(8,128)(2,1)S(1)}, bf16[1,256,512]{2,1,0:T(8,128)(2,1)}, u32[]{:S(2)}) copy-start(bf16[1,256,512]{2,1,0:T(8,128)(2,1)} %param.16) | copy-start | bytes 786436
  89.8 20.0 %copy-start.3 = (bf16[1,256,512]{2,1,0:T(8,128)(2,1)S(1)}, bf16[1,256,512]{2,1,0:T(8,128)(2,1)}, u32[]{:S(2)}) copy-start(bf16[1,256,512]{2,1,0:T(8,128)(2,1)} %param.18) | copy-start | bytes 786436
  89.8 18.8 %collective-permute-start.16 = (bf16[2,256,512]{2,1,0:T(8,128)(2,1)}, bf16[2,256,512]{2,1,0:T(8,128)(2,1)S(1)}, u32[]{:S(2)}, u32[]{:S(2)}) collective-permute-start(bf16[2,256,512]{2,1,0:T(8,128)(2,1)} %get-tuple-element.117), channel_id=1, source_target_pairs={{0,16},{8,24},{16,0},{24,8},{1,17},{9,25},{17,1},{25,9},{2,18},{10... | collective-permute-start | bytes 1572872 | tf_op jit(solution)/shard_map/ppermute | solution.py:722
  109.8 1.5 %copy-start.6 = (f32[1,16]{1,0:T(1,128)S(1)}, f32[1,16]{1,0:T(1,128)}, u32[]{:S(2)}) copy-start(f32[1,16]{1,0:T(1,128)} %get-tuple-element.126) | copy-start | bytes 196

commit v5 on v4

--- a/solution.py
+++ b/solution.py
@@ -227,8 +227,16 @@
     oth_ref,
     norms_ref,
     shift_ref,
-    out_ref,
-    e_ref,
+    w_a,
+    mix_a,
+    ctx_a,
+    dp_a,
+    w_b,
+    mix_b,
+    ctx_b,
+    dp_b,
+    near_ref,
+    rest_ref,
     send_ref,
     keep_ref,
     small_ref,
@@ -242,7 +250,7 @@
 ):
     r, key = where_ref[0], where_ref[1]
     count = n2_ref.shape[0] // 4
-    gain = norms_ref[2:3, :]
+    gain, first_gain = norms_ref[2:3, :], norms_ref[0:1, :]
     owns, others = (own0_ref, own1_ref, own2_ref, own3_ref), [oth_ref.at[k] for k in range(4)]
     moves = []
     for k in range(4):
@@ -259,17 +267,21 @@
     up, down = up_s[...], down_s[...]
     shift = shift_ref[...]
     shift_sum = jnp.zeros((1, up.shape[1]), F32)
-    for t in range(4):
-        at = slice(t * count, t * count + count)
+    for j in range(4):
+        at = pl.ds(pl.multiple_of((r ^ j) * count, count), count)
+        target = near_ref if j % 2 else rest_ref
         hidden = dot(n2_ref[at, :], up) + shift
         cdf = 0.5 + 0.5 * lax.erf(hidden * math.sqrt(0.5))
         active = (hidden * cdf).astype(BF)
         slope = cdf + hidden * jnp.exp(-0.5 * hidden * hidden) * (1.0 / math.sqrt(2 * math.pi))
         act_s[at, :] = active
-        out_ref[at, :] = dot(active, down).astype(BF)
+        out = dot(active, down) + dot(ctx_a[at, :], mix_a[...]) + dot(ctx_b[at, :], mix_b[...])
+        target[j // 2, 0] = out.astype(target.dtype)
         d_hidden = (dot(cot_ref[at, :], down, ((1,), (1,))) * slope).astype(BF)
         dh_s[at, :] = d_hidden
-        e_ref[at, :] = (dot(d_hidden, up, ((1,), (1,))) * gain).astype(BF)
+        d_first = dot(dp_a[at, :], w_a[...]) + dot(dp_b[at, :], w_b[...])
+        e = dot(d_hidden, up, ((1,), (1,))) * gain + d_first * first_gain
+        target[j // 2, 1] = e.astype(target.dtype)
         shift_sum += jnp.sum(d_hidden.astype(F32), axis=0, keepdims=True)
     mine = cot_ref[pl.ds(pl.multiple_of(r * count, count), count), :]
     product = dot(dh_s[...], xhat_ref[...], ((0,), (0,)))
@@ -290,17 +302,18 @@
             ref[k, 256:512] = dg_s[h * 256 : h * 256 + 256, pl.ds(g, 128)].astype(ref.dtype)
 
 
-def run_mlp(where, n2, xhat, cot, own, oth, norms, shift):
+def run_mlp(where, n2, xhat, cot, own, oth, norms, shift, first, second):
     tall, width = n2.shape
+    count = tall // 4
     wide = shift.shape[1]
     return call(
         mlp_kernel,
         "feed_forward",
         1 << 35,
-        (where, n2, xhat, cot, *own, *oth, norms, shift),
+        (where, n2, xhat, cot, *own, *oth, norms, shift, *first, *second),
         (
-            SHAPE((tall, width), BF),
-            SHAPE((tall, width), BF),
+            SHAPE((2, 2, count, width), BF),
+            SHAPE((2, 2, count, width), F32),
             SHAPE((4, 512, 128), BF),
             SHAPE((4, 512, 128), F32),
             SHAPE((8, wide), F32),
@@ -318,6 +331,12 @@
     )
 
 
+def cut_kernel(a_ref, b_ref, c_ref, d_ref, att_ref, mlp_ref):
+    for k, ref in enumerate((a_ref, b_ref, c_ref, d_ref)):
+        att_ref[k] = ref[0:256, :]
+        mlp_ref[k] = ref[256:768, :]
+
+
 def head(key, n1_ref, xhat_ref, cot_ref, norms_ref, shift, cos_ref, sin_ref, starts_ref, w, mix, ctx, dp, grads_ref, scratch):
     q_s, qh_s, k_s, v_s, dctx_s, dq_s, dt_s, pg_s, mg_s, unused = scratch
     tall = n1_ref.shape[0]
@@ -338,7 +357,7 @@
         projected = dot(n1_ref[at, :], w[...], ((1,), (1,))) + shift
         qk = turn(projected[:, :128], at, 1.0)
         turned = roll(qk, 64)
-        q_s[at, :] = jnp.where(left, qk, 0.0).astype(BF)
+        q_s[at, :] = jnp.where(left, qk * scaling, 0.0).astype(BF)
         k_s[at, :] = jnp.where(left, turned, 0.0).astype(BF)
         qh_s[at, :] = jnp.where(left, 0.0, turned).astype(BF)
         v_s[at, :] = projected[:, 128:].astype(BF)
@@ -349,7 +368,7 @@
         keys = (t + 1) * count
         q, d_context = q_s[at, :], dctx_s[at, :]
         kk, vv = k_s[0:keys, :], v_s[0:keys, :]
-        scores = dot(q, kk, ((1,), (1,))) * scaling
+        scores = dot(q, kk, ((1,), (1,)))
         place = lax.broadcasted_iota(jnp.int32, (count, keys), 1)
         row = lax.broadcasted_iota(jnp.int32, (count, 1), 0) + t * count
         allowed = (place >= starts_ref[at, :]) & (place <= row)
@@ -568,50 +587,6 @@
     )
 
 
-def join_kernel(
-    where_ref,
-    norms_ref,
-    w_a,
-    mix_a,
-    ctx_a,
-    dp_a,
-    w_b,
-    mix_b,
-    ctx_b,
-    dp_b,
-    out_in,
-    e_in,
-    near_ref,
-    rest_ref,
-):
-    r = where_ref[0]
-    count = ctx_a.shape[0] // 4
-    gain = norms_ref[0:1, :]
-    for j in range(4):
-        at = pl.ds(pl.multiple_of((r ^ j) * count, count), count)
-        d_first = dot(dp_a[at, :], w_a[...]) + dot(dp_b[at, :], w_b[...])
-        out = dot(ctx_a[at, :], mix_a[...]) + dot(ctx_b[at, :], mix_b[...])
-        target = near_ref if j % 2 else rest_ref
-        target[j // 2, 0] = (out_in[at, :].astype(F32) + out).astype(target.dtype)
-        target[j // 2, 1] = (e_in[at, :].astype(F32) + d_first * gain).astype(target.dtype)
-
-
-def run_join(where, norms, first, second, out, e):
-    tall, width = out.shape
-    count = tall // 4
-    return call(
-        join_kernel,
-        "join",
-        1 << 24,
-        (where, norms, *first, *second, out, e),
-        (
-            SHAPE((2, 2, count, width), BF),
-            SHAPE((2, 2, count, width), F32),
-        ),
-        (),
-    )
-
-
 def add_kernel(rest_ref, come_ref, mine_ref, onward_ref):
     for i in range(2):
         mine_ref[i] = rest_ref[0, i] + come_ref[0, i].astype(F32)
@@ -641,8 +616,10 @@
         kept = jnp.where(device == device_of(place), row, 0.0)
         place = lax.broadcasted_iota(jnp.int32, (wide, 128), 0)
         lane = lax.broadcasted_iota(jnp.int32, (wide, 128), 1)
-        chosen = jnp.where(lane == lane_of(place), 1.0, 0.0)
-        return jnp.dot(kept, chosen, precision=lax.Precision.HIGHEST, preferred_element_type=F32)
+        chosen = jnp.where(lane == lane_of(place), 1.0, 0.0).astype(BF)
+        high = kept.astype(BF)
+        low = (kept - high.astype(F32)).astype(BF)
+        return dot(high, chosen) + dot(low, chosen)
 
     rows = [own_ref[i : i + 1, :] + oth_ref[i : i + 1, :] for i in (1, 2)]
     rows += [mlp_ref[i : i + 1, :] for i in (1, 2, 3)]
@@ -672,26 +649,33 @@
     part = outs[0].shape[1]
     for i in range(5):
         outs[i][...] = total[0:1, i * part : (i + 1) * part]
-    outs[5][...] = total[1:2, 0 : outs[5].shape[1]]
-    outs[6][...] = total[2:3, 0 : outs[6].shape[1]]
-
-
-def merge_kernel(att_keep, att_come, mlp_keep, mlp_come, *outs):
+    outs[5][...] = outs[4][...]
+    outs[6][...] = total[1:2, 0 : outs[6].shape[1]]
+    outs[7][...] = total[2:3, 0 : outs[7].shape[1]]
+
+
+def merge_kernel(keep, come, *outs):
     for k in range(4):
-        outs[k][0:256, :] = (att_keep[k] + att_come[k].astype(F32)).astype(BF)
-        outs[k][256:768, :] = (mlp_keep[k] + mlp_come[k].astype(F32)).astype(BF)
-
-
-def collect_kernel(a_ref, b_ref, c_ref, d_ref, project_ref, mix_ref, up_ref, down_ref):
-    def total(begin, end):
-        refs = (a_ref, b_ref, c_ref, d_ref)
-        return sum(ref[begin:end, :].astype(F32) for ref in refs)
-
-    project_ref[...] = total(0, 192)
-    mix_ref[...] = total(192, 256)
-    up_ref[:, 0:128] = total(256, 384)
-    up_ref[:, 128:256] = total(384, 512)
-    down_ref[...] = total(512, 768)
+        outs[k][...] = (keep[k] + come[k].astype(F32)).astype(BF)
+
+
+def collect_kernel(unused, *refs):
+    att, mlp, (project_ref, mix_ref, up_ref, down_ref) = refs[:4], refs[4:8], refs[8:]
+
+    def total(blocks, begin, end):
+        return sum(ref[begin:end, :].astype(F32) for ref in blocks)
+
+    project_ref[...] = total(att, 0, 192)
+    mix_ref[...] = total(att, 192, 256)
+    up_ref[:, 0:128] = total(mlp, 0, 128)
+    up_ref[:, 128:256] = total(mlp, 128, 256)
+    down_ref[...] = total(mlp, 256, 512)
+
+
+def merge(name, keep, come):
+    return call_streamed(
+        merge_kernel, name, 1 << 26, (keep, come), (SHAPE(keep.shape[1:], BF),) * 4
+    )
 
 
 def on_device(
@@ -807,8 +791,15 @@
     every = lax.all_to_all(small, both, 0, 0, tiled=True)
     if paired:
         own = spread(packs[0])
-        mlp_slots = own, (beside(jnp.stack([v[256:] for v in own])),)
-        att_slots = own, (beside(jnp.stack([v[:256] for v in own])),)
+        own, across, every = lax.optimization_barrier((own, across, every))
+        att_cut, mlp_cut = call_streamed(
+            cut_kernel,
+            "cut",
+            1 << 31,
+            tuple(own),
+            (SHAPE((4, 256, 128), BF), SHAPE((4, 512, 128), BF)),
+        )
+        att_slots, mlp_slots = (own, (beside(att_cut),)), (own, (beside(mlp_cut),))
         every, across = lax.optimization_barrier((every, across))
     else:
         ups, downs = fetch_columns(up_weight), fetch_rows(down_weight)
@@ -850,14 +841,12 @@
     n1, n2, xhat, cot_all, *first, att_keep, small_own = run_first(
         where, chunks, att_slots[0], project_shift, cosine, sine, starts, norms
     )
-    out, e, mlp_send, mlp_keep, mlp_small = run_mlp(
-        where, n2, xhat, cot_all, mlp_slots[0], mlp_slots[1], norms, up_shift
-    )
-    n1, out = lax.optimization_barrier((n1, out))
     *second, att_send, small_oth = run_second(
         where, n1, xhat, cot_all, att_slots[1], project_shift, cosine, sine, starts, norms
     )
-    near, rest = run_join(where, norms, first, second, out, e)
+    near, rest, mlp_send, mlp_keep, mlp_small = run_mlp(
+        where, n2, xhat, cot_all, mlp_slots[0], mlp_slots[1], norms, up_shift, first, second
+    )
 
     (small,) = call(
         functools.partial(share_kernel, cols, (part, project_len, up_len)),
@@ -868,19 +857,13 @@
         (),
     )
     if paired:
-        near, small, mlp_come, att_come = lax.optimization_barrier(
-            (near, small, beside(mlp_send), beside(att_send))
-        )
-
-    if paired:
-        blocks = call_streamed(
-            merge_kernel,
-            "merge",
-            1 << 26,
-            (att_keep, att_come, mlp_keep, mlp_come),
-            (SHAPE((768, 128), BF),) * 4,
-        )
-        blocks = bring(blocks)
+        near, att_come = lax.optimization_barrier((near, beside(att_send)))
+        mlp_come = beside(mlp_send)
+        att_blocks = bring(merge("merge_att", att_keep, att_come))
+        mlp_come, att_blocks = lax.optimization_barrier((mlp_come, att_blocks))
+        small, att_blocks = lax.optimization_barrier((small, att_blocks))
+        blocks = att_blocks + bring(merge("merge_mlp", mlp_keep, mlp_come))
+
     shares = lax.all_to_all(small, both, 0, 0, tiled=True)
 
     mine, onward = call_streamed(
@@ -890,22 +873,10 @@
         (rest, flip(near, 1)),
         (SHAPE((2, count, width), F32), SHAPE((2, count, width), BF)),
     )
+    if paired:
+        onward, att_blocks = lax.optimization_barrier((onward, att_blocks))
+        blocks[:4] = att_blocks
     onward = flip(onward, 2)
-    if paired:
-        project_done, mix_done, up_done, down_done = call_streamed(
-            collect_kernel,
-            "collect",
-            1 << 35,
-            tuple(blocks),
-            (
-                SHAPE(project_weight.shape[::-1], F32),
-                SHAPE(output_weight.shape, F32),
-                SHAPE(up_weight.shape, F32),
-                SHAPE(down_weight.shape, F32),
-            ),
-        )
-        project_done, onward, shares = lax.optimization_barrier((project_done, onward, shares))
-        project_done = project_done.T
     output, input_grad = call_streamed(
         finish_kernel,
         "finish",
@@ -939,11 +910,27 @@
             "small_sums",
             1 << 24,
             (where, shares),
-            (SHAPE((1, part), F32),) * 5
+            (SHAPE((1, part), F32),) * 6
             + (SHAPE((1, project_len), F32), SHAPE((1, up_len), F32)),
             (),
         )
     ]
+    if paired:
+        output, pieces, blocks = lax.optimization_barrier((output, pieces, blocks))
+        project_done, mix_done, up_done, down_done = call(
+            collect_kernel,
+            "collect",
+            1 << 26,
+            (where, *blocks),
+            (
+                SHAPE(project_weight.shape[::-1], F32),
+                SHAPE(output_weight.shape, F32),
+                SHAPE(up_weight.shape, F32),
+                SHAPE(down_weight.shape, F32),
+            ),
+            (),
+        )
+        project_done = project_done.T
     return (
         output[None],
         input_grad[None],
@@ -954,7 +941,7 @@
         up_done,
         up_shift_grad,
         down_done,
-        pieces[4],
+        pieces[5],
         pieces[0],
         pieces[1],
         pieces[2],

time: 112 us -> 109 us (0.973); the launches traced: 112 us -> 107 us
  waiting for transfers between devices: 31.8 us -> 20 us
  starting transfers between devices: 38.1 us -> 48.9 us
  Pallas kernels: 35.5 us -> 33.9 us
  other arithmetic: 3.69 us -> 2.09 us
    ppermute x4 -> x8, starting transfers between devices: 9.79 us -> 21.7 us  [bring(): lax.ppermute(b, both, [(home(i, k), i) for i in everyone])]
    ppermute x4 -> x8, waiting for transfers between devices: 9.9 us -> 2.5 us  [bring(): lax.ppermute(b, both, [(home(i, k), i) for i in everyone])]
    ppermute x4, waiting for transfers between devices: 5.97 us -> 0.83 us  [beside(): return lax.ppermute(value, 'col', [(i, i ^ 1) for i in range(cols)])]
    ppermute x4, starting transfers between devices: 10.6 us -> 7.73 us  [spread(): lax.ppermute(block, both, [(i, home(i, k)) for i in everyone])]
    all_to_all x1, waiting for transfers between devices: 2.79 us -> 5.31 us  [on_device(): shares = lax.all_to_all(small, both, 0, 0, tiled=True)]
    all_to_all x1, starting transfers between devices: 4.43 us -> 6.93 us  [on_device(): every = lax.all_to_all(small, both, 0, 0, tiled=True)]
    ppermute x5, waiting for transfers between devices: 2.21 us -> 0.01 us  [flip(): return lax.ppermute(value, 'row', [(i, i ^ bit) for i in range(rows)])]
    all_to_all x1, starting transfers between devices: 5.09 us -> 2.93 us  [on_device(): shares = lax.all_to_all(small, both, 0, 0, tiled=True)]
  transfers between devices with their start and end apart: 19 -> 23, of which waited for: 6 -> 6; matrix products, arithmetic and copies ran while one was open for 3% -> 2% of each run, Pallas kernels for 27% -> 27%
where the time goes in v5:
time: 109 us; the launch traced here: 107 us
  starting transfers between devices  48.9 us (45%)
  Pallas kernels  33.9 us (31%)
  waiting for transfers between devices  20 us (18%)
  other arithmetic  2.09 us (2%)
    pallas_call x7, Pallas kernels, call(): pl.pallas_call(kernel, out_shape=results, in_specs=[SMEM] + places, out_s...  26 us
    ppermute x8, starting transfers between devices, bring(): lax.ppermute(b, both, [(home(i, k), i) for i in everyone])  21.7 us
    all_to_all x1, waiting for transfers between devices, on_device(): every = lax.all_to_all(small, both, 0, 0, tiled=True)  9.51 us
    ppermute x4, starting transfers between devices, spread(): lax.ppermute(block, both, [(i, home(i, k)) for i in everyone])  7.73 us
    all_to_all x1, starting transfers between devices, on_device(): every = lax.all_to_all(small, both, 0, 0, tiled=True)  6.93 us
    ppermute x5, starting transfers between devices, flip(): return lax.ppermute(value, 'row', [(i, i ^ bit) for i in range(rows)])  5.94 us
    pallas_call x5, Pallas kernels, call_streamed(): pl.pallas_call(body, out_shape=results, in_specs=[HBM] * len(operands), o...  5.66 us
    all_to_all x1, waiting for transfers between devices, on_device(): shares = lax.all_to_all(small, both, 0, 0, tiled=True)  5.31 us
  transfers between devices with their start and end apart: 23, of which 6 were waited for; matrix products, arithmetic and copies ran while one was open for 2% of the time, Pallas kernels for 27%

profile of v5, /device:TPU:0, one launch (start us, length us, event | category | flops | bytes accessed | tf_op | source)
XLA Modules:
  0.0 106.6 jit_solution(17714960835231742498)
XLA Ops:
  0.7 2.2 %prepare.1 = (bf16[32,8,128]{2,1,0:T(8,128)(2,1)}, bf16[2,256,512]{2,1,0:T(8,128)(2,1)}, bf16[768,128]{1,0:T(8,128)(2,1)}) custom-call(bf16[256,512]{1,0:T(8,128)(2,1)} %bitcast.27, bf16[256,512]{1,0:T(8,128)(2,1)} %bitcast.29, s32[1,256]{1,0:T(1,128)} %refs_2_.1, bf16[192,128]{1,0:T(8,128)(2,1)} %bitcast.31, bf16[64,128]{1,0:T(8,128)(2,1)} %refs_4_.1, ...), custom_call_target="tpu_custom_call" | custom-call | flops 1048576 | bytes 1048576 | tf_op jit(solution)/shard_map/prepare/pallas_call | solution.py:155
  2.9 3.0 %collective-permute-start.5 = (bf16[2,256,512]{2,1,0:T(8,128)(2,1)}, bf16[2,256,512]{2,1,0:T(8,128)(2,1)S(1)}, u32[]{:S(2)}, u32[]{:S(2)}) collective-permute-start(bf16[2,256,512]{2,1,0:T(8,128)(2,1)} %get-tuple-element.108.act0_ref), channel_id=1, source_target_pairs={{0,16},{8,24},{16,0},{24,8},{1,17},{9,25},{17,1},{25,9},{2,18},{10... | collective-permute-start | bytes 1572872 | tf_op jit(solution)/shard_map/ppermute | solution.py:706
  5.9 5.5 %collective-permute-start.4 = (bf16[768,128]{1,0:T(8,128)(2,1)}, bf16[768,128]{1,0:T(8,128)(2,1)S(1)}, u32[]{:S(2)}, u32[]{:S(2)}) collective-permute-start(bf16[768,128]{1,0:T(8,128)(2,1)} %get-tuple-element.109), channel_id=1, source_target_pairs={{0,6},{1,7},{2,22},{3,23},{4,14},{5,15},{6,30},{7,31},{8,4},{9,5},... | collective-permute-start | bytes 589832 | tf_op jit(solution)/shard_map/ppermute | solution.py:722
  12.1 1.6 %collective-permute-start.1 = (bf16[768,128]{1,0:T(8,128)(2,1)}, bf16[768,128]{1,0:T(8,128)(2,1)S(1)}, u32[]{:S(2)}, u32[]{:S(2)}) collective-permute-start(bf16[768,128]{1,0:T(8,128)(2,1)} %get-tuple-element.109), channel_id=1, source_target_pairs={{0,0},{1,1},{2,16},{3,17},{4,8},{5,9},{6,24},{7,25},{8,2},{9,3},{1... | collective-permute-start | bytes 589832 | tf_op jit(solution)/shard_map/ppermute | solution.py:722
  13.6 6.9 %all-to-all-start = ((bf16[32,8,128]{2,1,0:T(8,128)(2,1)}), bf16[32,8,128]{2,1,0:T(8,128)(2,1)S(1)}, u32[]{:S(2)}, u32[]{:S(2)}) async-start(bf16[32,8,128]{2,1,0:T(8,128)(2,1)} %get-tuple-element.110), calls=%async_computation | async-start | bytes 131072 | tf_op jit(solution)/shard_map/all_to_all | solution.py:791
  20.7 1.9 %collective-permute-done.4.slot3_ref.refs_3_.own3_ref = bf16[768,128]{1,0:T(8,128)(2,1)S(1)} collective-permute-done((bf16[768,128]{1,0:T(8,128)(2,1)}, bf16[768,128]{1,0:T(8,128)(2,1)S(1)}, u32[]{:S(2)}, u32[]{:S(2)}) %collective-permute-start.4) | collective-permute-done | bytes 196640 | tf_op jit(solution)/shard_map/ppermute | solution.py:722
  22.6 1.8 %collective-permute-start = (bf16[2,256,512]{2,1,0:T(8,128)(2,1)}, bf16[2,256,512]{2,1,0:T(8,128)(2,1)S(1)}, u32[]{:S(2)}, u32[]{:S(2)}) collective-permute-start(bf16[2,256,512]{2,1,0:T(8,128)(2,1)} %get-tuple-element.108.act0_ref), channel_id=1, source_target_pairs={{0,8},{8,0},{16,24},{24,16},{1,9},{9,1},{17,25},{25,17},{2,10},{10... | collective-permute-start | bytes 1572872 | tf_op jit(solution)/shard_map/ppermute | solution.py:706
  24.4 9.5 %all-to-all-done.every_ref = bf16[32,8,128]{2,1,0:T(8,128)(2,1)S(1)} async-done(((bf16[32,8,128]{2,1,0:T(8,128)(2,1)}), bf16[32,8,128]{2,1,0:T(8,128)(2,1)S(1)}, u32[]{:S(2)}, u32[]{:S(2)}) %all-to-all-start) | async-done | bytes 65568 | tf_op jit(solution)/shard_map/all_to_all | solution.py:791
  34.1 1.1 %cut.1 = (bf16[4,256,128]{2,1,0:T(8,128)(2,1)S(1)}, bf16[4,512,128]{2,1,0:T(8,128)(2,1)S(1)}) custom-call(bf16[768,128]{1,0:T(8,128)(2,1)S(1)} %collective-permute-done.1.slot0_ref.refs_0_.own0_ref, bf16[768,128]{1,0:T(8,128)(2,1)S(1)} %collective-permute-done.2.slot1_ref.refs_1_.own1_ref, ...), custom_call_target="tpu_custom_call" | custom-call | flops 2147483648 | bytes 5368709 | tf_op jit(solution)/shard_map/cut/pallas_call | solution.py:79
  36.0 1.3 %collective-permute-start.7 = (bf16[4,512,128]{2,1,0:T(8,128)(2,1)S(1)}, bf16[4,512,128]{2,1,0:T(8,128)(2,1)S(1)}, u32[]{:S(2)}, u32[]{:S(2)}) collective-permute-start(bf16[4,512,128]{2,1,0:T(8,128)(2,1)S(1)} %get-tuple-element.125), channel_id=1, source_target_pairs={{0,1},{1,0},{2,3},{3,2},{4,5},{5,4},{6,7},{7,6},{8,9},{9,8},{10,11... | collective-permute-start | bytes 1572872 | tf_op jit(solution)/shard_map/ppermute | solution.py:719
  37.3 0.9 layout.1
  38.4 1.9 %multiply_sine_fusion = (f32[1024,128]{1,0:T(8,128)S(1)}, f32[1024,128]{1,0:T(8,128)S(1)}) fusion(f32[128]{0:T(128)S(1)} %copy-done.6, f32[1024]{0:T(1024)S(1)} %convert_reduce_fusion), kind=kLoop, calls=%fused_computation | loop fusion | flops 131072 | bytes 1053184 | tf_op jit(solution)/shard_map/sin | solution.py:48
  40.4 8.1 %attention_first.1 = (bf16[1024,512]{1,0:T(8,128)(2,1)S(1)}, bf16[1024,512]{1,0:T(8,128)(2,1)S(1)}, bf16[1024,512]{1,0:T(8,128)(2,1)S(1)}, bf16[1024,512]{1,0:T(...) custom-call(s32[5]{0:T(128)S(1)} %stack.23.where_ref.unused, ...), custom_call_target="tpu_custom_call" | custom-call | flops 34359738368 | bytes 85899344 | tf_op jit(solution)/shard_map/attention_first/pallas_call | solution.py:94
  48.4 6.4 %attention_second.1 = (bf16[256,512]{1,0:T(8,128)(2,1)S(1)}, bf16[128,512]{1,0:T(8,128)(2,1)S(1)}, bf16[1024,128]{1,0:T(8,128)(2,1)S(1)}, bf16[1024,256]{1,0:T(8...) custom-call(s32[5]{0:T(128)S(1)} %stack.23.where_ref.unused, ...), custom_call_target="tpu_custom_call" | custom-call | flops 34359738368 | bytes 85899344 | tf_op jit(solution)/shard_map/attention_second/pallas_call | solution.py:94
  55.6 6.5 %feed_forward.1 = (bf16[2,2,256,512]{3,2,1,0:T(8,128)(2,1)S(1)}, f32[2,2,256,512]{3,2,1,0:T(8,128)S(1)}, bf16[4,512,128]{2,1,0:T(8,128)(2,1)S(1)}, f32[4,512,128]{2,1,0:T(8,128)S(1)}, f32[8,512]{1,0:T(8,128)S(1)}) custom-call(s32[5]{0:T(128)S(1)} %stack.23.where_ref.unused, bf16[1024,512]{1,0:T(8,128)(2,1)S(1)} %get-tuple-element.122.n2_ref, ...), custom_call_target="tpu_custom_call" | custom-call | flops 34359738368 | bytes 85899344 | tf_op jit(solution)/shard_map/feed_forward/pallas_call | solution.py:94
  64.5 3.1 %collective-permute-start.13 = (bf16[256,128]{1,0:T(8,128)(2,1)S(1)}, bf16[256,128]{1,0:T(8,128)(2,1)S(1)}, u32[]{:S(2)}, u32[]{:S(2)}) collective-permute-start(bf16[256,128]{1,0:T(8,128)(2,1)S(1)} %get-tuple-element.150), channel_id=1, source_target_pairs={{2,0},{3,1},{18,2},{19,3},{10,4},{11,5},{26,6},{27,7},{0,8},{1,9},... | collective-permute-start | bytes 196616 | tf_op jit(solution)/shard_map/ppermute | solution.py:726
  67.6 1.5 %collective-permute-start.14 = (bf16[256,128]{1,0:T(8,128)(2,1)S(1)}, bf16[256,128]{1,0:T(8,128)(2,1)S(1)}, u32[]{:S(2)}, u32[]{:S(2)}) collective-permute-start(bf16[256,128]{1,0:T(8,128)(2,1)S(1)} %get-tuple-element.151), channel_id=1, source_target_pairs={{4,0},{5,1},{20,2},{21,3},{12,4},{13,5},{28,6},{29,7},{6,8},{7,9},... | collective-permute-start | bytes 196616 | tf_op jit(solution)/shard_map/ppermute | solution.py:726
  69.1 6.9 %collective-permute-start.15 = (bf16[256,128]{1,0:T(8,128)(2,1)S(1)}, bf16[256,128]{1,0:T(8,128)(2,1)S(1)}, u32[]{:S(2)}, u32[]{:S(2)}) collective-permute-start(bf16[256,128]{1,0:T(8,128)(2,1)S(1)} %get-tuple-element.152), channel_id=1, source_target_pairs={{6,0},{7,1},{22,2},{23,3},{14,4},{15,5},{30,6},{31,7},{4,8},{5,9},... | collective-permute-start | bytes 196616 | tf_op jit(solution)/shard_map/ppermute | solution.py:726
  75.9 1.7 %share_small.1 = f32[32,8,128]{2,1,0:T(8,128)} custom-call(s32[5]{0:T(128)S(1)} %stack.23.where_ref.unused, f32[8,512]{1,0:T(8,128)S(1)} %get-tuple-element.143.mlp_ref, f32[8,512]{1,0:T(8,128)S(1)} %get-tuple-element.144.own_ref, f32[8,512]{1,0:T(8,128)S(1)} %get-tuple-element.145.oth_ref), custom_call_target="tpu_custom_call" | custom-call | flops 16777216 | bytes 41943 | tf_op jit(solution)/shard_map/share_small/pallas_call | solution.py:94
  77.7 1.9 %collective-permute-done.15.refs_3_ = bf16[256,128]{1,0:T(8,128)(2,1)S(1)} collective-permute-done((bf16[256,128]{1,0:T(8,128)(2,1)S(1)}, bf16[256,128]{1,0:T(8,128)(2,1)S(1)}, u32[]{:S(2)}, u32[]{:S(2)}) %collective-permute-start.15) | collective-permute-done | bytes 65568 | tf_op jit(solution)/shard_map/ppermute | solution.py:726
  79.7 1.1 %add_near.1 = (f32[2,256,512]{2,1,0:T(8,128)S(1)}, bf16[2,256,512]{2,1,0:T(8,128)(2,1)}) custom-call(f32[2,2,256,512]{3,2,1,0:T(8,128)S(1)} %get-tuple-element.137.refs_0_, bf16[2,2,256,512]{3,2,1,0:T(8,128)(2,1)S(1)} %collective-permute-done.10.refs_1_), custom_call_target="tpu_custom_call" | custom-call | flops 16777216 | bytes 41943 | tf_op jit(solution)/shard_map/add_near/pallas_call | solution.py:79
  80.8 0.9 collective-permute-start.16
  81.7 2.9 %all-to-all-start.1 = ((f32[32,8,128]{2,1,0:T(8,128)}), f32[32,8,128]{2,1,0:T(8,128)S(1)}, u32[]{:S(2)}, u32[]{:S(2)}) async-start(f32[32,8,128]{2,1,0:T(8,128)} %share_small.1), calls=%async_computation.1 | async-start | bytes 262144 | tf_op jit(solution)/shard_map/all_to_all | solution.py:867
  84.6 0.9 merge_mlp.1
  85.6 1.6 %collective-permute-start.17 = (bf16[512,128]{1,0:T(8,128)(2,1)}, bf16[512,128]{1,0:T(8,128)(2,1)S(1)}, u32[]{:S(2)}, u32[]{:S(2)}) collective-permute-start(bf16[512,128]{1,0:T(8,128)(2,1)} %get-tuple-element.176), channel_id=1, source_target_pairs={{0,0},{1,1},{16,2},{17,3},{8,4},{9,5},{24,6},{25,7},{2,8},{3,9},{1... | collective-permute-start | bytes 393224 | tf_op jit(solution)/shard_map/ppermute | solution.py:726
  87.2 3.2 %collective-permute-start.18 = (bf16[512,128]{1,0:T(8,128)(2,1)}, bf16[512,128]{1,0:T(8,128)(2,1)S(1)}, u32[]{:S(2)}, u32[]{:S(2)}) collective-permute-start(bf16[512,128]{1,0:T(8,128)(2,1)} %get-tuple-element.177), channel_id=1, source_target_pairs={{2,0},{3,1},{18,2},{19,3},{10,4},{11,5},{26,6},{27,7},{0,8},{1,9},... | collective-permute-start | bytes 393224 | tf_op jit(solution)/shard_map/ppermute | solution.py:726
  90.4 1.4 %collective-permute-start.19 = (bf16[512,128]{1,0:T(8,128)(2,1)}, bf16[512,128]{1,0:T(8,128)(2,1)S(1)}, u32[]{:S(2)}, u32[]{:S(2)}) collective-permute-start(bf16[512,128]{1,0:T(8,128)(2,1)} %get-tuple-element.178), channel_id=1, source_target_pairs={{4,0},{5,1},{20,2},{21,3},{12,4},{13,5},{28,6},{29,7},{6,8},{7,9},... | collective-permute-start | bytes 393224 | tf_op jit(solution)/shard_map/ppermute | solution.py:726
  91.8 3.4 %collective-permute-start.20 = (bf16[512,128]{1,0:T(8,128)(2,1)}, bf16[512,128]{1,0:T(8,128)(2,1)S(1)}, u32[]{:S(2)}, u32[]{:S(2)}) collective-permute-start(bf16[512,128]{1,0:T(8,128)(2,1)} %get-tuple-element.179), channel_id=1, source_target_pairs={{6,0},{7,1},{22,2},{23,3},{14,4},{15,5},{30,6},{31,7},{4,8},{5,9},... | collective-permute-start | bytes 393224 | tf_op jit(solution)/shard_map/ppermute | solution.py:726
  95.2 5.3 %all-to-all-done.1.sums_ref = f32[32,8,128]{2,1,0:T(8,128)S(1)} async-done(((f32[32,8,128]{2,1,0:T(8,128)}), f32[32,8,128]{2,1,0:T(8,128)S(1)}, u32[]{:S(2)}, u32[]{:S(2)}) %all-to-all-start.1) | async-done | bytes 131104 | tf_op jit(solution)/shard_map/all_to_all | solution.py:867
  101.2 1.2 %small_sums.1 = (f32[1,16]{1,0:T(1,128)}, f32[1,16]{1,0:T(1,128)}, f32[1,16]{1,0:T(1,128)}, f32[1,16]{1,0:T(1,128)}, f32[1,16]{1,0:T(1,128)}, /*index=5*/f32[1,16]{1,0:T(1,128)}, f32[1,48]{1,0:T(1,128)}, f32[1,64]{1,0:T(1,128)}) custom-call(s32[5]{0:T(128)S(1)} %copy-done.3, f32[32,8,128]{2,1,0:T(8,128)S(1)} %all-to-all-done.1.sums_ref), custom_call_target="tpu_custom_call" | custom-call | flops 16777216 | bytes 41943 | tf_op jit(solution)/shard_map/small_sums/pallas_call | solution.py:94
  102.3 2.4 %finish.1 = (bf16[256,512]{1,0:T(8,128)(2,1)}, f32[256,512]{1,0:T(8,128)}) custom-call(bf16[256,512]{1,0:T(8,128)(2,1)S(1)} %bitcast.28, bf16[256,512]{1,0:T(8,128)(2,1)S(1)} %bitcast.30, f32[2,256,512]{2,1,0:T(8,128)S(1)} %get-tuple-element.141.refs_2_, bf16[2,256,512]{2,1,0:T(8,128)(2,1)} %collective-permute-done.16.refs_3_, ...), custom_call_target="tpu_custom_call" | custom-call | flops 16777216 | bytes 41943 | tf_op jit(solution)/shard_map/finish/pallas_call | solution.py:79
  105.3 1.3 %collect.1 = (f32[192,128]{1,0:T(8,128)}, f32[64,128]{1,0:T(8,128)}, f32[128,256]{1,0:T(8,128)}, f32[256,128]{1,0:T(8,128)}) custom-call(s32[5]{0:T(128)S(1)} %copy-done.4, bf16[256,128]{1,0:T(8,128)(2,1)S(1)} %collective-permute-done.12.refs_0_, bf16[256,128]{1,0:T(8,128)(2,1)S(1)} %collective-permute-done.13.refs_1_, ...), custom_call_target="tpu_custom_call" | custom-call | flops 67108864 | bytes 167772 | tf_op jit(solution)/shard_map/collect/pallas_call | solution.py:94
  (44 shorter events, 6.4 us)
Async XLA Ops:
  2.9 31.0 %collective-permute-start.5 = (bf16[2,256,512]{2,1,0:T(8,128)(2,1)}, bf16[2,256,512]{2,1,0:T(8,128)(2,1)S(1)}, u32[]{:S(2)}, u32[]{:S(2)}) collective-permute-start(bf16[2,256,512]{2,1,0:T(8,128)(2,1)} %get-tuple-element.108.act0_ref), channel_id=1, source_target_pairs={{0,16},{8,24},{16,0},{24,8},{1,17},{9,25},{17,1},{25,9},{2,18},{10... | collective-permute-start | bytes 1572872 | tf_op jit(solution)/shard_map/ppermute | solution.py:706
  5.9 16.7 %collective-permute-start.4 = (bf16[768,128]{1,0:T(8,128)(2,1)}, bf16[768,128]{1,0:T(8,128)(2,1)S(1)}, u32[]{:S(2)}, u32[]{:S(2)}) collective-permute-start(bf16[768,128]{1,0:T(8,128)(2,1)} %get-tuple-element.109), channel_id=1, source_target_pairs={{0,6},{1,7},{2,22},{3,23},{4,14},{5,15},{6,30},{7,31},{8,4},{9,5},... | collective-permute-start | bytes 589832 | tf_op jit(solution)/shard_map/ppermute | solution.py:722
  11.4 22.5 %collective-permute-start.3 = (bf16[768,128]{1,0:T(8,128)(2,1)}, bf16[768,128]{1,0:T(8,128)(2,1)S(1)}, u32[]{:S(2)}, u32[]{:S(2)}) collective-permute-start(bf16[768,128]{1,0:T(8,128)(2,1)} %get-tuple-element.109), channel_id=1, source_target_pairs={{0,4},{1,5},{2,20},{3,21},{4,12},{5,13},{6,28},{7,29},{8,6},{9,7},... | collective-permute-start | bytes 589832 | tf_op jit(solution)/shard_map/ppermute | solution.py:722
  11.5 22.4 %collective-permute-start.2 = (bf16[768,128]{1,0:T(8,128)(2,1)}, bf16[768,128]{1,0:T(8,128)(2,1)S(1)}, u32[]{:S(2)}, u32[]{:S(2)}) collective-permute-start(bf16[768,128]{1,0:T(8,128)(2,1)} %get-tuple-element.109), channel_id=1, source_target_pairs={{0,2},{1,3},{2,18},{3,19},{4,10},{5,11},{6,26},{7,27},{8,0},{9,1},... | collective-permute-start | bytes 589832 | tf_op jit(solution)/shard_map/ppermute | solution.py:722
  12.1 21.8 %collective-permute-start.1 = (bf16[768,128]{1,0:T(8,128)(2,1)}, bf16[768,128]{1,0:T(8,128)(2,1)S(1)}, u32[]{:S(2)}, u32[]{:S(2)}) collective-permute-start(bf16[768,128]{1,0:T(8,128)(2,1)} %get-tuple-element.109), channel_id=1, source_target_pairs={{0,0},{1,1},{2,16},{3,17},{4,8},{5,9},{6,24},{7,25},{8,2},{9,3},{1... | collective-permute-start | bytes 589832 | tf_op jit(solution)/shard_map/ppermute | solution.py:722
  13.6 20.2 %all-to-all-start = ((bf16[32,8,128]{2,1,0:T(8,128)(2,1)}), bf16[32,8,128]{2,1,0:T(8,128)(2,1)S(1)}, u32[]{:S(2)}, u32[]{:S(2)}) async-start(bf16[32,8,128]{2,1,0:T(8,128)(2,1)} %get-tuple-element.110), calls=%async_computation | async-start | bytes 131072 | tf_op jit(solution)/shard_map/all_to_all | solution.py:791
  20.7 55.2 %copy-start.2 = (s32[5]{0:T(128)}, s32[5]{0:T(128)S(1)}, u32[]{:S(2)}) copy-start(s32[5]{0:T(128)S(1)} %stack.23.where_ref.unused) | copy-start | bytes 64
  22.6 17.8 %collective-permute-start = (bf16[2,256,512]{2,1,0:T(8,128)(2,1)}, bf16[2,256,512]{2,1,0:T(8,128)(2,1)S(1)}, u32[]{:S(2)}, u32[]{:S(2)}) collective-permute-start(bf16[2,256,512]{2,1,0:T(8,128)(2,1)} %get-tuple-element.108.act0_ref), channel_id=1, source_target_pairs={{0,8},{8,0},{16,24},{24,16},{1,9},{9,1},{17,25},{25,17},{2,10},{10... | collective-permute-start | bytes 1572872 | tf_op jit(solution)/shard_map/ppermute | solution.py:706
  33.9 6.4 %collective-permute-start.6 = (bf16[2,256,512]{2,1,0:T(8,128)(2,1)S(1)}, bf16[2,256,512]{2,1,0:T(8,128)(2,1)S(1)}, u32[]{:S(2)}, u32[]{:S(2)}) collective-permute-start(bf16[2,256,512]{2,1,0:T(8,128)(2,1)S(1)} %collective-permute-done.5.act2_ref), channel_id=1, source_target_pairs={{0,8},{8,0},{16,24},{24,16},{1,9},{9,1},{17,25},{25,17},{2,10},{10... | collective-permute-start | bytes 1572872 | tf_op jit(solution)/shard_map/ppermute | solution.py:706
  35.2 13.3 %collective-permute-start.8 = (bf16[4,256,128]{2,1,0:T(8,128)(2,1)S(1)}, bf16[4,256,128]{2,1,0:T(8,128)(2,1)S(1)}, u32[]{:S(2)}, u32[]{:S(2)}) collective-permute-start(bf16[4,256,128]{2,1,0:T(8,128)(2,1)S(1)} %get-tuple-element.132), channel_id=1, source_target_pairs={{0,1},{1,0},{2,3},{3,2},{4,5},{5,4},{6,7},{7,6},{8,9},{9,8},{10,11... | collective-permute-start | bytes 786440 | tf_op jit(solution)/shard_map/ppermute | solution.py:719
  36.0 2.5 %copy-start.6 = (f32[128]{0:T(128)S(1)}, f32[128]{0:T(128)}, u32[]{:S(2)}) copy-start(f32[128]{0:T(128)} %constant.45.clone) | copy-start | bytes 1540
  36.0 4.4 %copy-start.5 = (bf16[2,256,512]{2,1,0:T(8,128)(2,1)S(1)}, bf16[2,256,512]{2,1,0:T(8,128)(2,1)}, u32[]{:S(2)}) copy-start(bf16[2,256,512]{2,1,0:T(8,128)(2,1)} %get-tuple-element.108.act0_ref) | copy-start | bytes 1572868
  36.0 19.6 %collective-permute-start.7 = (bf16[4,512,128]{2,1,0:T(8,128)(2,1)S(1)}, bf16[4,512,128]{2,1,0:T(8,128)(2,1)S(1)}, u32[]{:S(2)}, u32[]{:S(2)}) collective-permute-start(bf16[4,512,128]{2,1,0:T(8,128)(2,1)S(1)} %get-tuple-element.125), channel_id=1, source_target_pairs={{0,1},{1,0},{2,3},{3,2},{4,5},{5,4},{6,7},{7,6},{8,9},{9,8},{10,11... | collective-permute-start | bytes 1572872 | tf_op jit(solution)/shard_map/ppermute | solution.py:719
  54.8 8.1 %collective-permute-start.9 = (bf16[4,256,128]{2,1,0:T(8,128)(2,1)S(1)}, bf16[4,256,128]{2,1,0:T(8,128)(2,1)S(1)}, u32[]{:S(2)}, u32[]{:S(2)}) collective-permute-start(bf16[4,256,128]{2,1,0:T(8,128)(2,1)S(1)} %get-tuple-element.139), channel_id=1, source_target_pairs={{0,1},{1,0},{2,3},{3,2},{4,5},{5,4},{6,7},{7,6},{8,9},{9,8},{10,11... | collective-permute-start | bytes 786440 | tf_op jit(solution)/shard_map/ppermute | solution.py:719
  62.9 16.7 %collective-permute-start.10 = (bf16[2,2,256,512]{3,2,1,0:T(8,128)(2,1)S(1)}, bf16[2,2,256,512]{3,2,1,0:T(8,128)(2,1)S(1)}, u32[]{:S(2)}, u32[]{:S(2)}) collective-permute-start(bf16[2,2,256,512]{3,2,1,0:T(8,128)(2,1)S(1)} %get-tuple-element.140), channel_id=1, source_target_pairs={{0,8},{8,0},{16,24},{24,16},{1,9},{9,1},{17,25},{25,17},{2,10},{10... | collective-permute-start | bytes 3145736 | tf_op jit(solution)/shard_map/ppermute | solution.py:706
  62.9 16.7 %collective-permute-start.11 = (bf16[4,512,128]{2,1,0:T(8,128)(2,1)S(1)}, bf16[4,512,128]{2,1,0:T(8,128)(2,1)S(1)}, u32[]{:S(2)}, u32[]{:S(2)}) collective-permute-start(bf16[4,512,128]{2,1,0:T(8,128)(2,1)S(1)} %get-tuple-element.146), channel_id=1, source_target_pairs={{0,1},{1,0},{2,3},{3,2},{4,5},{5,4},{6,7},{7,6},{8,9},{9,8},{10,11... | collective-permute-start | bytes 1572872 | tf_op jit(solution)/shard_map/ppermute | solution.py:719
  63.8 5.2 %collective-permute-start.12 = (bf16[256,128]{1,0:T(8,128)(2,1)S(1)}, bf16[256,128]{1,0:T(8,128)(2,1)S(1)}, u32[]{:S(2)}, u32[]{:S(2)}) collective-permute-start(bf16[256,128]{1,0:T(8,128)(2,1)S(1)} %get-tuple-element.149), channel_id=1, source_target_pairs={{0,0},{1,1},{16,2},{17,3},{8,4},{9,5},{24,6},{25,7},{2,8},{3,9},{1... | collective-permute-start | bytes 196616 | tf_op jit(solution)/shard_map/ppermute | solution.py:726
  64.5 13.2 %collective-permute-start.13 = (bf16[256,128]{1,0:T(8,128)(2,1)S(1)}, bf16[256,128]{1,0:T(8,128)(2,1)S(1)}, u32[]{:S(2)}, u32[]{:S(2)}) collective-permute-start(bf16[256,128]{1,0:T(8,128)(2,1)S(1)} %get-tuple-element.150), channel_id=1, source_target_pairs={{2,0},{3,1},{18,2},{19,3},{10,4},{11,5},{26,6},{27,7},{0,8},{1,9},... | collective-permute-start | bytes 196616 | tf_op jit(solution)/shard_map/ppermute | solution.py:726
  67.6 10.1 %collective-permute-start.14 = (bf16[256,128]{1,0:T(8,128)(2,1)S(1)}, bf16[256,128]{1,0:T(8,128)(2,1)S(1)}, u32[]{:S(2)}, u32[]{:S(2)}) collective-permute-start(bf16[256,128]{1,0:T(8,128)(2,1)S(1)} %get-tuple-element.151), channel_id=1, source_target_pairs={{4,0},{5,1},{20,2},{21,3},{12,4},{13,5},{28,6},{29,7},{6,8},{7,9},... | collective-permute-start | bytes 196616 | tf_op jit(solution)/shard_map/ppermute | solution.py:726
  69.1 10.6 %collective-permute-start.15 = (bf16[256,128]{1,0:T(8,128)(2,1)S(1)}, bf16[256,128]{1,0:T(8,128)(2,1)S(1)}, u32[]{:S(2)}, u32[]{:S(2)}) collective-permute-start(bf16[256,128]{1,0:T(8,128)(2,1)S(1)} %get-tuple-element.152), channel_id=1, source_target_pairs={{6,0},{7,1},{22,2},{23,3},{14,4},{15,5},{30,6},{31,7},{4,8},{5,9},... | collective-permute-start | bytes 196616 | tf_op jit(solution)/shard_map/ppermute | solution.py:726
  79.6 22.7 %copy-start = (bf16[1,256,512]{2,1,0:T(8,128)(2,1)S(1)}, bf16[1,256,512]{2,1,0:T(8,128)(2,1)}, u32[]{:S(2)}) copy-start(bf16[1,256,512]{2,1,0:T(8,128)(2,1)} %param.16) | copy-start | bytes 786436
  79.6 22.7 %copy-start.1 = (bf16[1,256,512]{2,1,0:T(8,128)(2,1)S(1)}, bf16[1,256,512]{2,1,0:T(8,128)(2,1)}, u32[]{:S(2)}) copy-start(bf16[1,256,512]{2,1,0:T(8,128)(2,1)} %param.18) | copy-start | bytes 786436
  80.8 21.6 %collective-permute-start.16 = (bf16[2,256,512]{2,1,0:T(8,128)(2,1)}, bf16[2,256,512]{2,1,0:T(8,128)(2,1)}, u32[]{:S(2)}, u32[]{:S(2)}) collective-permute-start(bf16[2,256,512]{2,1,0:T(8,128)(2,1)} %get-tuple-element.161), channel_id=1, source_target_pairs={{0,16},{8,24},{16,0},{24,8},{1,17},{9,25},{17,1},{25,9},{2,18},{10... | collective-permute-start | bytes 1572872 | tf_op jit(solution)/shard_map/ppermute | solution.py:706
  81.7 18.8 %all-to-all-start.1 = ((f32[32,8,128]{2,1,0:T(8,128)}), f32[32,8,128]{2,1,0:T(8,128)S(1)}, u32[]{:S(2)}, u32[]{:S(2)}) async-start(f32[32,8,128]{2,1,0:T(8,128)} %share_small.1), calls=%async_computation.1 | async-start | bytes 262144 | tf_op jit(solution)/shard_map/all_to_all | solution.py:867
  85.6 19.7 %copy-start.4 = (s32[5]{0:T(128)S(1)}, s32[5]{0:T(128)}, u32[]{:S(2)}) copy-start(s32[5]{0:T(128)} %copy-done.2) | copy-start | bytes 64
  85.6 19.2 %collective-permute-start.17 = (bf16[512,128]{1,0:T(8,128)(2,1)}, bf16[512,128]{1,0:T(8,128)(2,1)S(1)}, u32[]{:S(2)}, u32[]{:S(2)}) collective-permute-start(bf16[512,128]{1,0:T(8,128)(2,1)} %get-tuple-element.176), channel_id=1, source_target_pairs={{0,0},{1,1},{16,2},{17,3},{8,4},{9,5},{24,6},{25,7},{2,8},{3,9},{1... | collective-permute-start | bytes 393224 | tf_op jit(solution)/shard_map/ppermute | solution.py:726
  87.2 18.1 %collective-permute-start.18 = (bf16[512,128]{1,0:T(8,128)(2,1)}, bf16[512,128]{1,0:T(8,128)(2,1)S(1)}, u32[]{:S(2)}, u32[]{:S(2)}) collective-permute-start(bf16[512,128]{1,0:T(8,128)(2,1)} %get-tuple-element.177), channel_id=1, source_target_pairs={{2,0},{3,1},{18,2},{19,3},{10,4},{11,5},{26,6},{27,7},{0,8},{1,9},... | collective-permute-start | bytes 393224 | tf_op jit(solution)/shard_map/ppermute | solution.py:726
  90.4 14.9 %collective-permute-start.19 = (bf16[512,128]{1,0:T(8,128)(2,1)}, bf16[512,128]{1,0:T(8,128)(2,1)S(1)}, u32[]{:S(2)}, u32[]{:S(2)}) collective-permute-start(bf16[512,128]{1,0:T(8,128)(2,1)} %get-tuple-element.178), channel_id=1, source_target_pairs={{4,0},{5,1},{20,2},{21,3},{12,4},{13,5},{28,6},{29,7},{6,8},{7,9},... | collective-permute-start | bytes 393224 | tf_op jit(solution)/shard_map/ppermute | solution.py:726
  91.8 13.6 %collective-permute-start.20 = (bf16[512,128]{1,0:T(8,128)(2,1)}, bf16[512,128]{1,0:T(8,128)(2,1)S(1)}, u32[]{:S(2)}, u32[]{:S(2)}) collective-permute-start(bf16[512,128]{1,0:T(8,128)(2,1)} %get-tuple-element.179), channel_id=1, source_target_pairs={{6,0},{7,1},{22,2},{23,3},{14,4},{15,5},{30,6},{31,7},{4,8},{5,9},... | collective-permute-start | bytes 393224 | tf_op jit(solution)/shard_map/ppermute | solution.py:726
  100.5 0.7 copy-start.3

commit v6 on v5

--- a/solution.py
+++ b/solution.py
@@ -644,7 +644,7 @@
     out_ref[:, 2, :] = hidden
 
 
-def small_kernel(unused, sums_ref, *outs):
+def small_kernel(sums_ref, *outs):
     total = jnp.sum(sums_ref[...], axis=0)
     part = outs[0].shape[1]
     for i in range(5):
@@ -905,14 +905,13 @@
 
     *pieces, project_shift_grad, up_shift_grad = [
         v[0]
-        for v in call(
+        for v in call_streamed(
             small_kernel,
             "small_sums",
             1 << 24,
-            (where, shares),
+            (shares,),
             (SHAPE((1, part), F32),) * 6
             + (SHAPE((1, project_len), F32), SHAPE((1, up_len), F32)),
-            (),
         )
     ]
     if paired:

time: 109 us -> 109 us (level)
    pallas_call x7 -> x6, Pallas kernels: 26 us -> 24.9 us  [call(): pl.pallas_call(kernel, out_shape=results, in_specs=[SMEM] + places, out_s...]
    pallas_call x5 -> x6, Pallas kernels: 5.66 us -> 6.44 us  [call_streamed(): pl.pallas_call(body, out_shape=results, in_specs=[HBM] * len(operands), o...]
where the time goes in v6:
time: 109 us; the launch traced here: 107 us
  starting transfers between devices  48.9 us (45%)
  Pallas kernels  33.5 us (31%)
  waiting for transfers between devices  21 us (19%)
  other arithmetic  2.09 us (2%)
    pallas_call x6, Pallas kernels, call(): pl.pallas_call(kernel, out_shape=results, in_specs=[SMEM] + places, out_s...  24.9 us
    ppermute x8, starting transfers between devices, bring(): lax.ppermute(b, both, [(home(i, k), i) for i in everyone])  21.6 us
    all_to_all x1, waiting for transfers between devices, on_device(): every = lax.all_to_all(small, both, 0, 0, tiled=True)  9.51 us
    ppermute x4, starting transfers between devices, spread(): lax.ppermute(block, both, [(i, home(i, k)) for i in everyone])  7.73 us
    all_to_all x1, starting transfers between devices, on_device(): every = lax.all_to_all(small, both, 0, 0, tiled=True)  6.93 us
    pallas_call x6, Pallas kernels, call_streamed(): pl.pallas_call(body, out_shape=results, in_specs=[HBM] * len(operands), o...  6.44 us
    ppermute x5, starting transfers between devices, flip(): return lax.ppermute(value, 'row', [(i, i ^ bit) for i in range(rows)])  5.94 us
    all_to_all x1, waiting for transfers between devices, on_device(): shares = lax.all_to_all(small, both, 0, 0, tiled=True)  5.32 us
  transfers between devices with their start and end apart: 23, of which 6 were waited for; matrix products, arithmetic and copies ran while one was open for 2% of the time, Pallas kernels for 27%

profile of v6, /device:TPU:0, one launch (start us, length us, event | category | flops | bytes accessed | tf_op | source)
XLA Modules:
  0.0 106.6 jit_solution(7820922722463255462)
XLA Ops:
  0.7 2.2 %prepare.1 = (bf16[32,8,128]{2,1,0:T(8,128)(2,1)}, bf16[2,256,512]{2,1,0:T(8,128)(2,1)}, bf16[768,128]{1,0:T(8,128)(2,1)}) custom-call(bf16[256,512]{1,0:T(8,128)(2,1)} %bitcast.27, bf16[256,512]{1,0:T(8,128)(2,1)} %bitcast.29, s32[1,256]{1,0:T(1,128)} %refs_2_.1, bf16[192,128]{1,0:T(8,128)(2,1)} %bitcast.31, bf16[64,128]{1,0:T(8,128)(2,1)} %refs_4_.1, ...), custom_call_target="tpu_custom_call" | custom-call | flops 1048576 | bytes 1048576 | tf_op jit(solution)/shard_map/prepare/pallas_call | solution.py:155
  2.9 3.0 %collective-permute-start.5 = (bf16[2,256,512]{2,1,0:T(8,128)(2,1)}, bf16[2,256,512]{2,1,0:T(8,128)(2,1)S(1)}, u32[]{:S(2)}, u32[]{:S(2)}) collective-permute-start(bf16[2,256,512]{2,1,0:T(8,128)(2,1)} %get-tuple-element.108.act0_ref), channel_id=1, source_target_pairs={{0,16},{8,24},{16,0},{24,8},{1,17},{9,25},{17,1},{25,9},{2,18},{10... | collective-permute-start | bytes 1572872 | tf_op jit(solution)/shard_map/ppermute | solution.py:706
  5.9 5.5 %collective-permute-start.4 = (bf16[768,128]{1,0:T(8,128)(2,1)}, bf16[768,128]{1,0:T(8,128)(2,1)S(1)}, u32[]{:S(2)}, u32[]{:S(2)}) collective-permute-start(bf16[768,128]{1,0:T(8,128)(2,1)} %get-tuple-element.109), channel_id=1, source_target_pairs={{0,6},{1,7},{2,22},{3,23},{4,14},{5,15},{6,30},{7,31},{8,4},{9,5},... | collective-permute-start | bytes 589832 | tf_op jit(solution)/shard_map/ppermute | solution.py:722
  12.1 1.6 %collective-permute-start.1 = (bf16[768,128]{1,0:T(8,128)(2,1)}, bf16[768,128]{1,0:T(8,128)(2,1)S(1)}, u32[]{:S(2)}, u32[]{:S(2)}) collective-permute-start(bf16[768,128]{1,0:T(8,128)(2,1)} %get-tuple-element.109), channel_id=1, source_target_pairs={{0,0},{1,1},{2,16},{3,17},{4,8},{5,9},{6,24},{7,25},{8,2},{9,3},{1... | collective-permute-start | bytes 589832 | tf_op jit(solution)/shard_map/ppermute | solution.py:722
  13.6 6.9 %all-to-all-start = ((bf16[32,8,128]{2,1,0:T(8,128)(2,1)}), bf16[32,8,128]{2,1,0:T(8,128)(2,1)S(1)}, u32[]{:S(2)}, u32[]{:S(2)}) async-start(bf16[32,8,128]{2,1,0:T(8,128)(2,1)} %get-tuple-element.110), calls=%async_computation | async-start | bytes 131072 | tf_op jit(solution)/shard_map/all_to_all | solution.py:791
  20.7 1.9 %collective-permute-done.4.slot3_ref.refs_3_.own3_ref = bf16[768,128]{1,0:T(8,128)(2,1)S(1)} collective-permute-done((bf16[768,128]{1,0:T(8,128)(2,1)}, bf16[768,128]{1,0:T(8,128)(2,1)S(1)}, u32[]{:S(2)}, u32[]{:S(2)}) %collective-permute-start.4) | collective-permute-done | bytes 196640 | tf_op jit(solution)/shard_map/ppermute | solution.py:722
  22.6 1.8 %collective-permute-start = (bf16[2,256,512]{2,1,0:T(8,128)(2,1)}, bf16[2,256,512]{2,1,0:T(8,128)(2,1)S(1)}, u32[]{:S(2)}, u32[]{:S(2)}) collective-permute-start(bf16[2,256,512]{2,1,0:T(8,128)(2,1)} %get-tuple-element.108.act0_ref), channel_id=1, source_target_pairs={{0,8},{8,0},{16,24},{24,16},{1,9},{9,1},{17,25},{25,17},{2,10},{10... | collective-permute-start | bytes 1572872 | tf_op jit(solution)/shard_map/ppermute | solution.py:706
  24.4 9.5 %all-to-all-done.every_ref = bf16[32,8,128]{2,1,0:T(8,128)(2,1)S(1)} async-done(((bf16[32,8,128]{2,1,0:T(8,128)(2,1)}), bf16[32,8,128]{2,1,0:T(8,128)(2,1)S(1)}, u32[]{:S(2)}, u32[]{:S(2)}) %all-to-all-start) | async-done | bytes 65568 | tf_op jit(solution)/shard_map/all_to_all | solution.py:791
  34.1 1.1 %cut.1 = (bf16[4,256,128]{2,1,0:T(8,128)(2,1)S(1)}, bf16[4,512,128]{2,1,0:T(8,128)(2,1)S(1)}) custom-call(bf16[768,128]{1,0:T(8,128)(2,1)S(1)} %collective-permute-done.1.slot0_ref.refs_0_.own0_ref, bf16[768,128]{1,0:T(8,128)(2,1)S(1)} %collective-permute-done.2.slot1_ref.refs_1_.own1_ref, ...), custom_call_target="tpu_custom_call" | custom-call | flops 2147483648 | bytes 5368709 | tf_op jit(solution)/shard_map/cut/pallas_call | solution.py:79
  36.0 1.3 %collective-permute-start.7 = (bf16[4,512,128]{2,1,0:T(8,128)(2,1)S(1)}, bf16[4,512,128]{2,1,0:T(8,128)(2,1)S(1)}, u32[]{:S(2)}, u32[]{:S(2)}) collective-permute-start(bf16[4,512,128]{2,1,0:T(8,128)(2,1)S(1)} %get-tuple-element.125), channel_id=1, source_target_pairs={{0,1},{1,0},{2,3},{3,2},{4,5},{5,4},{6,7},{7,6},{8,9},{9,8},{10,11... | collective-permute-start | bytes 1572872 | tf_op jit(solution)/shard_map/ppermute | solution.py:719
  37.3 0.9 layout.1
  38.4 1.9 %multiply_sine_fusion = (f32[1024,128]{1,0:T(8,128)S(1)}, f32[1024,128]{1,0:T(8,128)S(1)}) fusion(f32[128]{0:T(128)S(1)} %copy-done.5, f32[1024]{0:T(1024)S(1)} %convert_reduce_fusion), kind=kLoop, calls=%fused_computation | loop fusion | flops 131072 | bytes 1053184 | tf_op jit(solution)/shard_map/sin | solution.py:48
  40.3 8.1 %attention_first.1 = (bf16[1024,512]{1,0:T(8,128)(2,1)S(1)}, bf16[1024,512]{1,0:T(8,128)(2,1)S(1)}, bf16[1024,512]{1,0:T(8,128)(2,1)S(1)}, bf16[1024,512]{1,0:T(...) custom-call(s32[5]{0:T(128)S(1)} %stack.23.where_ref.unused, ...), custom_call_target="tpu_custom_call" | custom-call | flops 34359738368 | bytes 85899344 | tf_op jit(solution)/shard_map/attention_first/pallas_call | solution.py:94
  48.4 6.4 %attention_second.1 = (bf16[256,512]{1,0:T(8,128)(2,1)S(1)}, bf16[128,512]{1,0:T(8,128)(2,1)S(1)}, bf16[1024,128]{1,0:T(8,128)(2,1)S(1)}, bf16[1024,256]{1,0:T(8...) custom-call(s32[5]{0:T(128)S(1)} %stack.23.where_ref.unused, ...), custom_call_target="tpu_custom_call" | custom-call | flops 34359738368 | bytes 85899344 | tf_op jit(solution)/shard_map/attention_second/pallas_call | solution.py:94
  55.6 6.5 %feed_forward.1 = (bf16[2,2,256,512]{3,2,1,0:T(8,128)(2,1)S(1)}, f32[2,2,256,512]{3,2,1,0:T(8,128)S(1)}, bf16[4,512,128]{2,1,0:T(8,128)(2,1)S(1)}, f32[4,512,128]{2,1,0:T(8,128)S(1)}, f32[8,512]{1,0:T(8,128)S(1)}) custom-call(s32[5]{0:T(128)S(1)} %stack.23.where_ref.unused, bf16[1024,512]{1,0:T(8,128)(2,1)S(1)} %get-tuple-element.122.n2_ref, ...), custom_call_target="tpu_custom_call" | custom-call | flops 34359738368 | bytes 85899344 | tf_op jit(solution)/shard_map/feed_forward/pallas_call | solution.py:94
  64.5 3.1 %collective-permute-start.13 = (bf16[256,128]{1,0:T(8,128)(2,1)S(1)}, bf16[256,128]{1,0:T(8,128)(2,1)S(1)}, u32[]{:S(2)}, u32[]{:S(2)}) collective-permute-start(bf16[256,128]{1,0:T(8,128)(2,1)S(1)} %get-tuple-element.150), channel_id=1, source_target_pairs={{2,0},{3,1},{18,2},{19,3},{10,4},{11,5},{26,6},{27,7},{0,8},{1,9},... | collective-permute-start | bytes 196616 | tf_op jit(solution)/shard_map/ppermute | solution.py:726
  67.6 1.5 %collective-permute-start.14 = (bf16[256,128]{1,0:T(8,128)(2,1)S(1)}, bf16[256,128]{1,0:T(8,128)(2,1)S(1)}, u32[]{:S(2)}, u32[]{:S(2)}) collective-permute-start(bf16[256,128]{1,0:T(8,128)(2,1)S(1)} %get-tuple-element.151), channel_id=1, source_target_pairs={{4,0},{5,1},{20,2},{21,3},{12,4},{13,5},{28,6},{29,7},{6,8},{7,9},... | collective-permute-start | bytes 196616 | tf_op jit(solution)/shard_map/ppermute | solution.py:726
  69.1 6.9 %collective-permute-start.15 = (bf16[256,128]{1,0:T(8,128)(2,1)S(1)}, bf16[256,128]{1,0:T(8,128)(2,1)S(1)}, u32[]{:S(2)}, u32[]{:S(2)}) collective-permute-start(bf16[256,128]{1,0:T(8,128)(2,1)S(1)} %get-tuple-element.152), channel_id=1, source_target_pairs={{6,0},{7,1},{22,2},{23,3},{14,4},{15,5},{30,6},{31,7},{4,8},{5,9},... | collective-permute-start | bytes 196616 | tf_op jit(solution)/shard_map/ppermute | solution.py:726
  75.9 1.7 %share_small.1 = f32[32,8,128]{2,1,0:T(8,128)} custom-call(s32[5]{0:T(128)S(1)} %stack.23.where_ref.unused, f32[8,512]{1,0:T(8,128)S(1)} %get-tuple-element.143.mlp_ref, f32[8,512]{1,0:T(8,128)S(1)} %get-tuple-element.144.own_ref, f32[8,512]{1,0:T(8,128)S(1)} %get-tuple-element.145.oth_ref), custom_call_target="tpu_custom_call" | custom-call | flops 16777216 | bytes 41943 | tf_op jit(solution)/shard_map/share_small/pallas_call | solution.py:94
  77.7 1.9 %collective-permute-done.15.refs_3_ = bf16[256,128]{1,0:T(8,128)(2,1)S(1)} collective-permute-done((bf16[256,128]{1,0:T(8,128)(2,1)S(1)}, bf16[256,128]{1,0:T(8,128)(2,1)S(1)}, u32[]{:S(2)}, u32[]{:S(2)}) %collective-permute-start.15) | collective-permute-done | bytes 65568 | tf_op jit(solution)/shard_map/ppermute | solution.py:726
  79.7 1.1 %add_near.1 = (f32[2,256,512]{2,1,0:T(8,128)S(1)}, bf16[2,256,512]{2,1,0:T(8,128)(2,1)}) custom-call(f32[2,2,256,512]{3,2,1,0:T(8,128)S(1)} %get-tuple-element.137.refs_0_, bf16[2,2,256,512]{3,2,1,0:T(8,128)(2,1)S(1)} %collective-permute-done.10.refs_1_), custom_call_target="tpu_custom_call" | custom-call | flops 16777216 | bytes 41943 | tf_op jit(solution)/shard_map/add_near/pallas_call | solution.py:79
  80.8 0.9 collective-permute-start.16
  81.7 2.9 %all-to-all-start.1 = ((f32[32,8,128]{2,1,0:T(8,128)}), f32[32,8,128]{2,1,0:T(8,128)S(1)}, u32[]{:S(2)}, u32[]{:S(2)}) async-start(f32[32,8,128]{2,1,0:T(8,128)} %share_small.1), calls=%async_computation.1 | async-start | bytes 262144 | tf_op jit(solution)/shard_map/all_to_all | solution.py:867
  84.6 0.9 merge_mlp.1
  85.6 1.6 %collective-permute-start.17 = (bf16[512,128]{1,0:T(8,128)(2,1)}, bf16[512,128]{1,0:T(8,128)(2,1)S(1)}, u32[]{:S(2)}, u32[]{:S(2)}) collective-permute-start(bf16[512,128]{1,0:T(8,128)(2,1)} %get-tuple-element.176), channel_id=1, source_target_pairs={{0,0},{1,1},{16,2},{17,3},{8,4},{9,5},{24,6},{25,7},{2,8},{3,9},{1... | collective-permute-start | bytes 393224 | tf_op jit(solution)/shard_map/ppermute | solution.py:726
  87.2 3.2 %collective-permute-start.18 = (bf16[512,128]{1,0:T(8,128)(2,1)}, bf16[512,128]{1,0:T(8,128)(2,1)S(1)}, u32[]{:S(2)}, u32[]{:S(2)}) collective-permute-start(bf16[512,128]{1,0:T(8,128)(2,1)} %get-tuple-element.177), channel_id=1, source_target_pairs={{2,0},{3,1},{18,2},{19,3},{10,4},{11,5},{26,6},{27,7},{0,8},{1,9},... | collective-permute-start | bytes 393224 | tf_op jit(solution)/shard_map/ppermute | solution.py:726
  90.4 1.4 %collective-permute-start.19 = (bf16[512,128]{1,0:T(8,128)(2,1)}, bf16[512,128]{1,0:T(8,128)(2,1)S(1)}, u32[]{:S(2)}, u32[]{:S(2)}) collective-permute-start(bf16[512,128]{1,0:T(8,128)(2,1)} %get-tuple-element.178), channel_id=1, source_target_pairs={{4,0},{5,1},{20,2},{21,3},{12,4},{13,5},{28,6},{29,7},{6,8},{7,9},... | collective-permute-start | bytes 393224 | tf_op jit(solution)/shard_map/ppermute | solution.py:726
  91.8 3.4 %collective-permute-start.20 = (bf16[512,128]{1,0:T(8,128)(2,1)}, bf16[512,128]{1,0:T(8,128)(2,1)S(1)}, u32[]{:S(2)}, u32[]{:S(2)}) collective-permute-start(bf16[512,128]{1,0:T(8,128)(2,1)} %get-tuple-element.179), channel_id=1, source_target_pairs={{6,0},{7,1},{22,2},{23,3},{14,4},{15,5},{30,6},{31,7},{4,8},{5,9},... | collective-permute-start | bytes 393224 | tf_op jit(solution)/shard_map/ppermute | solution.py:726
  95.2 5.3 %all-to-all-done.1.refs_0_ = f32[32,8,128]{2,1,0:T(8,128)S(1)} async-done(((f32[32,8,128]{2,1,0:T(8,128)}), f32[32,8,128]{2,1,0:T(8,128)S(1)}, u32[]{:S(2)}, u32[]{:S(2)}) %all-to-all-start.1) | async-done | bytes 131104 | tf_op jit(solution)/shard_map/all_to_all | solution.py:867
  101.3 2.4 %finish.1 = (bf16[256,512]{1,0:T(8,128)(2,1)}, f32[256,512]{1,0:T(8,128)}) custom-call(bf16[256,512]{1,0:T(8,128)(2,1)S(1)} %bitcast.28, bf16[256,512]{1,0:T(8,128)(2,1)S(1)} %bitcast.30, f32[2,256,512]{2,1,0:T(8,128)S(1)} %get-tuple-element.141.refs_2_, bf16[2,256,512]{2,1,0:T(8,128)(2,1)} %collective-permute-done.16.refs_3_, ...), custom_call_target="tpu_custom_call" | custom-call | flops 16777216 | bytes 41943 | tf_op jit(solution)/shard_map/finish/pallas_call | solution.py:79
  103.8 1.5 %collective-permute-done.18.refs_5_ = bf16[512,128]{1,0:T(8,128)(2,1)S(1)} collective-permute-done((bf16[512,128]{1,0:T(8,128)(2,1)}, bf16[512,128]{1,0:T(8,128)(2,1)S(1)}, u32[]{:S(2)}, u32[]{:S(2)}) %collective-permute-start.18) | collective-permute-done | bytes 131104 | tf_op jit(solution)/shard_map/ppermute | solution.py:726
  105.3 1.3 %collect.1 = (f32[192,128]{1,0:T(8,128)}, f32[64,128]{1,0:T(8,128)}, f32[128,256]{1,0:T(8,128)}, f32[256,128]{1,0:T(8,128)}) custom-call(s32[5]{0:T(128)S(1)} %copy-done.3, bf16[256,128]{1,0:T(8,128)(2,1)S(1)} %collective-permute-done.12.refs_0_, bf16[256,128]{1,0:T(8,128)(2,1)S(1)} %collective-permute-done.13.refs_1_, ...), custom_call_target="tpu_custom_call" | custom-call | flops 67108864 | bytes 167772 | tf_op jit(solution)/shard_map/collect/pallas_call | solution.py:94
  (42 shorter events, 6.0 us)
Async XLA Ops:
  2.9 31.0 %collective-permute-start.5 = (bf16[2,256,512]{2,1,0:T(8,128)(2,1)}, bf16[2,256,512]{2,1,0:T(8,128)(2,1)S(1)}, u32[]{:S(2)}, u32[]{:S(2)}) collective-permute-start(bf16[2,256,512]{2,1,0:T(8,128)(2,1)} %get-tuple-element.108.act0_ref), channel_id=1, source_target_pairs={{0,16},{8,24},{16,0},{24,8},{1,17},{9,25},{17,1},{25,9},{2,18},{10... | collective-permute-start | bytes 1572872 | tf_op jit(solution)/shard_map/ppermute | solution.py:706
  5.9 16.7 %collective-permute-start.4 = (bf16[768,128]{1,0:T(8,128)(2,1)}, bf16[768,128]{1,0:T(8,128)(2,1)S(1)}, u32[]{:S(2)}, u32[]{:S(2)}) collective-permute-start(bf16[768,128]{1,0:T(8,128)(2,1)} %get-tuple-element.109), channel_id=1, source_target_pairs={{0,6},{1,7},{2,22},{3,23},{4,14},{5,15},{6,30},{7,31},{8,4},{9,5},... | collective-permute-start | bytes 589832 | tf_op jit(solution)/shard_map/ppermute | solution.py:722
  11.4 22.5 %collective-permute-start.3 = (bf16[768,128]{1,0:T(8,128)(2,1)}, bf16[768,128]{1,0:T(8,128)(2,1)S(1)}, u32[]{:S(2)}, u32[]{:S(2)}) collective-permute-start(bf16[768,128]{1,0:T(8,128)(2,1)} %get-tuple-element.109), channel_id=1, source_target_pairs={{0,4},{1,5},{2,20},{3,21},{4,12},{5,13},{6,28},{7,29},{8,6},{9,7},... | collective-permute-start | bytes 589832 | tf_op jit(solution)/shard_map/ppermute | solution.py:722
  11.5 22.4 %collective-permute-start.2 = (bf16[768,128]{1,0:T(8,128)(2,1)}, bf16[768,128]{1,0:T(8,128)(2,1)S(1)}, u32[]{:S(2)}, u32[]{:S(2)}) collective-permute-start(bf16[768,128]{1,0:T(8,128)(2,1)} %get-tuple-element.109), channel_id=1, source_target_pairs={{0,2},{1,3},{2,18},{3,19},{4,10},{5,11},{6,26},{7,27},{8,0},{9,1},... | collective-permute-start | bytes 589832 | tf_op jit(solution)/shard_map/ppermute | solution.py:722
  12.1 21.8 %collective-permute-start.1 = (bf16[768,128]{1,0:T(8,128)(2,1)}, bf16[768,128]{1,0:T(8,128)(2,1)S(1)}, u32[]{:S(2)}, u32[]{:S(2)}) collective-permute-start(bf16[768,128]{1,0:T(8,128)(2,1)} %get-tuple-element.109), channel_id=1, source_target_pairs={{0,0},{1,1},{2,16},{3,17},{4,8},{5,9},{6,24},{7,25},{8,2},{9,3},{1... | collective-permute-start | bytes 589832 | tf_op jit(solution)/shard_map/ppermute | solution.py:722
  13.6 20.2 %all-to-all-start = ((bf16[32,8,128]{2,1,0:T(8,128)(2,1)}), bf16[32,8,128]{2,1,0:T(8,128)(2,1)S(1)}, u32[]{:S(2)}, u32[]{:S(2)}) async-start(bf16[32,8,128]{2,1,0:T(8,128)(2,1)} %get-tuple-element.110), calls=%async_computation | async-start | bytes 131072 | tf_op jit(solution)/shard_map/all_to_all | solution.py:791
  20.7 55.2 %copy-start.2 = (s32[5]{0:T(128)}, s32[5]{0:T(128)S(1)}, u32[]{:S(2)}) copy-start(s32[5]{0:T(128)S(1)} %stack.23.where_ref.unused) | copy-start | bytes 64
  22.6 17.8 %collective-permute-start = (bf16[2,256,512]{2,1,0:T(8,128)(2,1)}, bf16[2,256,512]{2,1,0:T(8,128)(2,1)S(1)}, u32[]{:S(2)}, u32[]{:S(2)}) collective-permute-start(bf16[2,256,512]{2,1,0:T(8,128)(2,1)} %get-tuple-element.108.act0_ref), channel_id=1, source_target_pairs={{0,8},{8,0},{16,24},{24,16},{1,9},{9,1},{17,25},{25,17},{2,10},{10... | collective-permute-start | bytes 1572872 | tf_op jit(solution)/shard_map/ppermute | solution.py:706
  33.9 6.4 %collective-permute-start.6 = (bf16[2,256,512]{2,1,0:T(8,128)(2,1)S(1)}, bf16[2,256,512]{2,1,0:T(8,128)(2,1)S(1)}, u32[]{:S(2)}, u32[]{:S(2)}) collective-permute-start(bf16[2,256,512]{2,1,0:T(8,128)(2,1)S(1)} %collective-permute-done.5.act2_ref), channel_id=1, source_target_pairs={{0,8},{8,0},{16,24},{24,16},{1,9},{9,1},{17,25},{25,17},{2,10},{10... | collective-permute-start | bytes 1572872 | tf_op jit(solution)/shard_map/ppermute | solution.py:706
  35.2 13.2 %collective-permute-start.8 = (bf16[4,256,128]{2,1,0:T(8,128)(2,1)S(1)}, bf16[4,256,128]{2,1,0:T(8,128)(2,1)S(1)}, u32[]{:S(2)}, u32[]{:S(2)}) collective-permute-start(bf16[4,256,128]{2,1,0:T(8,128)(2,1)S(1)} %get-tuple-element.132), channel_id=1, source_target_pairs={{0,1},{1,0},{2,3},{3,2},{4,5},{5,4},{6,7},{7,6},{8,9},{9,8},{10,11... | collective-permute-start | bytes 786440 | tf_op jit(solution)/shard_map/ppermute | solution.py:719
  36.0 2.4 %copy-start.5 = (f32[128]{0:T(128)S(1)}, f32[128]{0:T(128)}, u32[]{:S(2)}) copy-start(f32[128]{0:T(128)} %constant.45.clone) | copy-start | bytes 1540
  36.0 4.4 %copy-start.4 = (bf16[2,256,512]{2,1,0:T(8,128)(2,1)S(1)}, bf16[2,256,512]{2,1,0:T(8,128)(2,1)}, u32[]{:S(2)}) copy-start(bf16[2,256,512]{2,1,0:T(8,128)(2,1)} %get-tuple-element.108.act0_ref) | copy-start | bytes 1572868
  36.0 19.6 %collective-permute-start.7 = (bf16[4,512,128]{2,1,0:T(8,128)(2,1)S(1)}, bf16[4,512,128]{2,1,0:T(8,128)(2,1)S(1)}, u32[]{:S(2)}, u32[]{:S(2)}) collective-permute-start(bf16[4,512,128]{2,1,0:T(8,128)(2,1)S(1)} %get-tuple-element.125), channel_id=1, source_target_pairs={{0,1},{1,0},{2,3},{3,2},{4,5},{5,4},{6,7},{7,6},{8,9},{9,8},{10,11... | collective-permute-start | bytes 1572872 | tf_op jit(solution)/shard_map/ppermute | solution.py:719
  54.8 8.1 %collective-permute-start.9 = (bf16[4,256,128]{2,1,0:T(8,128)(2,1)S(1)}, bf16[4,256,128]{2,1,0:T(8,128)(2,1)S(1)}, u32[]{:S(2)}, u32[]{:S(2)}) collective-permute-start(bf16[4,256,128]{2,1,0:T(8,128)(2,1)S(1)} %get-tuple-element.139), channel_id=1, source_target_pairs={{0,1},{1,0},{2,3},{3,2},{4,5},{5,4},{6,7},{7,6},{8,9},{9,8},{10,11... | collective-permute-start | bytes 786440 | tf_op jit(solution)/shard_map/ppermute | solution.py:719
  62.9 16.7 %collective-permute-start.10 = (bf16[2,2,256,512]{3,2,1,0:T(8,128)(2,1)S(1)}, bf16[2,2,256,512]{3,2,1,0:T(8,128)(2,1)S(1)}, u32[]{:S(2)}, u32[]{:S(2)}) collective-permute-start(bf16[2,2,256,512]{3,2,1,0:T(8,128)(2,1)S(1)} %get-tuple-element.140), channel_id=1, source_target_pairs={{0,8},{8,0},{16,24},{24,16},{1,9},{9,1},{17,25},{25,17},{2,10},{10... | collective-permute-start | bytes 3145736 | tf_op jit(solution)/shard_map/ppermute | solution.py:706
  62.9 16.7 %collective-permute-start.11 = (bf16[4,512,128]{2,1,0:T(8,128)(2,1)S(1)}, bf16[4,512,128]{2,1,0:T(8,128)(2,1)S(1)}, u32[]{:S(2)}, u32[]{:S(2)}) collective-permute-start(bf16[4,512,128]{2,1,0:T(8,128)(2,1)S(1)} %get-tuple-element.146), channel_id=1, source_target_pairs={{0,1},{1,0},{2,3},{3,2},{4,5},{5,4},{6,7},{7,6},{8,9},{9,8},{10,11... | collective-permute-start | bytes 1572872 | tf_op jit(solution)/shard_map/ppermute | solution.py:719
  63.8 5.2 %collective-permute-start.12 = (bf16[256,128]{1,0:T(8,128)(2,1)S(1)}, bf16[256,128]{1,0:T(8,128)(2,1)S(1)}, u32[]{:S(2)}, u32[]{:S(2)}) collective-permute-start(bf16[256,128]{1,0:T(8,128)(2,1)S(1)} %get-tuple-element.149), channel_id=1, source_target_pairs={{0,0},{1,1},{16,2},{17,3},{8,4},{9,5},{24,6},{25,7},{2,8},{3,9},{1... | collective-permute-start | bytes 196616 | tf_op jit(solution)/shard_map/ppermute | solution.py:726
  64.5 13.2 %collective-permute-start.13 = (bf16[256,128]{1,0:T(8,128)(2,1)S(1)}, bf16[256,128]{1,0:T(8,128)(2,1)S(1)}, u32[]{:S(2)}, u32[]{:S(2)}) collective-permute-start(bf16[256,128]{1,0:T(8,128)(2,1)S(1)} %get-tuple-element.150), channel_id=1, source_target_pairs={{2,0},{3,1},{18,2},{19,3},{10,4},{11,5},{26,6},{27,7},{0,8},{1,9},... | collective-permute-start | bytes 196616 | tf_op jit(solution)/shard_map/ppermute | solution.py:726
  67.6 10.1 %collective-permute-start.14 = (bf16[256,128]{1,0:T(8,128)(2,1)S(1)}, bf16[256,128]{1,0:T(8,128)(2,1)S(1)}, u32[]{:S(2)}, u32[]{:S(2)}) collective-permute-start(bf16[256,128]{1,0:T(8,128)(2,1)S(1)} %get-tuple-element.151), channel_id=1, source_target_pairs={{4,0},{5,1},{20,2},{21,3},{12,4},{13,5},{28,6},{29,7},{6,8},{7,9},... | collective-permute-start | bytes 196616 | tf_op jit(solution)/shard_map/ppermute | solution.py:726
  69.1 10.6 %collective-permute-start.15 = (bf16[256,128]{1,0:T(8,128)(2,1)S(1)}, bf16[256,128]{1,0:T(8,128)(2,1)S(1)}, u32[]{:S(2)}, u32[]{:S(2)}) collective-permute-start(bf16[256,128]{1,0:T(8,128)(2,1)S(1)} %get-tuple-element.152), channel_id=1, source_target_pairs={{6,0},{7,1},{22,2},{23,3},{14,4},{15,5},{30,6},{31,7},{4,8},{5,9},... | collective-permute-start | bytes 196616 | tf_op jit(solution)/shard_map/ppermute | solution.py:726
  79.6 21.7 %copy-start = (bf16[1,256,512]{2,1,0:T(8,128)(2,1)S(1)}, bf16[1,256,512]{2,1,0:T(8,128)(2,1)}, u32[]{:S(2)}) copy-start(bf16[1,256,512]{2,1,0:T(8,128)(2,1)} %param.16) | copy-start | bytes 786436
  79.6 21.7 %copy-start.1 = (bf16[1,256,512]{2,1,0:T(8,128)(2,1)S(1)}, bf16[1,256,512]{2,1,0:T(8,128)(2,1)}, u32[]{:S(2)}) copy-start(bf16[1,256,512]{2,1,0:T(8,128)(2,1)} %param.18) | copy-start | bytes 786436
  80.8 20.5 %collective-permute-start.16 = (bf16[2,256,512]{2,1,0:T(8,128)(2,1)}, bf16[2,256,512]{2,1,0:T(8,128)(2,1)}, u32[]{:S(2)}, u32[]{:S(2)}) collective-permute-start(bf16[2,256,512]{2,1,0:T(8,128)(2,1)} %get-tuple-element.161), channel_id=1, source_target_pairs={{0,16},{8,24},{16,0},{24,8},{1,17},{9,25},{17,1},{25,9},{2,18},{10... | collective-permute-start | bytes 1572872 | tf_op jit(solution)/shard_map/ppermute | solution.py:706
  81.7 18.8 %all-to-all-start.1 = ((f32[32,8,128]{2,1,0:T(8,128)}), f32[32,8,128]{2,1,0:T(8,128)S(1)}, u32[]{:S(2)}, u32[]{:S(2)}) async-start(f32[32,8,128]{2,1,0:T(8,128)} %share_small.1), calls=%async_computation.1 | async-start | bytes 262144 | tf_op jit(solution)/shard_map/all_to_all | solution.py:867
  85.6 19.7 %copy-start.3 = (s32[5]{0:T(128)S(1)}, s32[5]{0:T(128)}, u32[]{:S(2)}) copy-start(s32[5]{0:T(128)} %copy-done.2) | copy-start | bytes 64
  85.6 18.1 %collective-permute-start.17 = (bf16[512,128]{1,0:T(8,128)(2,1)}, bf16[512,128]{1,0:T(8,128)(2,1)S(1)}, u32[]{:S(2)}, u32[]{:S(2)}) collective-permute-start(bf16[512,128]{1,0:T(8,128)(2,1)} %get-tuple-element.176), channel_id=1, source_target_pairs={{0,0},{1,1},{16,2},{17,3},{8,4},{9,5},{24,6},{25,7},{2,8},{3,9},{1... | collective-permute-start | bytes 393224 | tf_op jit(solution)/shard_map/ppermute | solution.py:726
  87.2 18.1 %collective-permute-start.18 = (bf16[512,128]{1,0:T(8,128)(2,1)}, bf16[512,128]{1,0:T(8,128)(2,1)S(1)}, u32[]{:S(2)}, u32[]{:S(2)}) collective-permute-start(bf16[512,128]{1,0:T(8,128)(2,1)} %get-tuple-element.177), channel_id=1, source_target_pairs={{2,0},{3,1},{18,2},{19,3},{10,4},{11,5},{26,6},{27,7},{0,8},{1,9},... | collective-permute-start | bytes 393224 | tf_op jit(solution)/shard_map/ppermute | solution.py:726
  90.4 14.9 %collective-permute-start.19 = (bf16[512,128]{1,0:T(8,128)(2,1)}, bf16[512,128]{1,0:T(8,128)(2,1)S(1)}, u32[]{:S(2)}, u32[]{:S(2)}) collective-permute-start(bf16[512,128]{1,0:T(8,128)(2,1)} %get-tuple-element.178), channel_id=1, source_target_pairs={{4,0},{5,1},{20,2},{21,3},{12,4},{13,5},{28,6},{29,7},{6,8},{7,9},... | collective-permute-start | bytes 393224 | tf_op jit(solution)/shard_map/ppermute | solution.py:726
  91.8 13.6 %collective-permute-start.20 = (bf16[512,128]{1,0:T(8,128)(2,1)}, bf16[512,128]{1,0:T(8,128)(2,1)S(1)}, u32[]{:S(2)}, u32[]{:S(2)}) collective-permute-start(bf16[512,128]{1,0:T(8,128)(2,1)} %get-tuple-element.179), channel_id=1, source_target_pairs={{6,0},{7,1},{22,2},{23,3},{14,4},{15,5},{30,6},{31,7},{4,8},{5,9},... | collective-permute-start | bytes 393224 | tf_op jit(solution)/shard_map/ppermute | solution.py:726
